TPU v7x, 32 devices: a whole 2x2x4 slice. The times are simulated.
32 devices in a mesh: dom: 4 (over y, core), fsdp: 8 (over z, x).
Axes of the slice: x: 2, y: 2, z: 4, core: 2. Of those that a mesh axis runs over, the one named last changes fastest.
Arguments:
- features: bfloat16 [128, 1024, 128], P(('dom', 'fsdp')), may hold values from -6 to 6
- history_first: bfloat16 [512, 1024, 128], P('dom', 'fsdp'), may hold values from -6 to 6
- history_second: bfloat16 [512, 1024, 128], P('dom', 'fsdp'), may hold values from -3 to 3
- pull_list: int32 [4, 32, 4], P('dom'), may hold values from 0 to 127
- pull_count: int32 [4, 32], P('dom'), may hold values from 1 to 4, as said below
- tile_src: int32 [128, 6], P(('dom', 'fsdp')), may hold values from 0 to 19
- tile_count: int32 [128], P(('dom', 'fsdp')), may hold values from 1 to 6
- tile_values: bfloat16 [128, 6, 128, 128], P(('dom', 'fsdp')), may hold values from -0.21875 to 0.21875
- w_first: bfloat16 [1024, 1024], P('fsdp'), may hold values from -0.1875 to 0.1875
- w_second: bfloat16 [1024, 1024], P('fsdp'), may hold values from -0.1875 to 0.1875
- bias_first: bfloat16 [1024], P('fsdp'), may hold values from -3 to 3
- out_grad: bfloat16 [128, 1024, 128], P(('dom', 'fsdp')), may hold values from -0.125 to 0.125
Outputs:
- hidden_new: bfloat16 [128, 1024, 128], P(('dom', 'fsdp'))
- grad_w1: float32 [1024, 1024], P('fsdp')
- grad_w2: float32 [1024, 1024], P('fsdp')
- grad_b1: float32 [1024], P('fsdp')
Inputs may be any that keep to these rules, and one draw needn't show every extreme that they name: pull_list[o, q, c] numbers a block within partition o. Slot c of list (o, q) is live when c < pull_count[o, q]; every device q has 4 live slots from at least one partition. tile_src below 4 names one of the device's own batch blocks; 4 + s names its pulled slot s.
All inputs are finite; a program needn't handle non-finite values.
Results may differ from a plain program's by a relative error of at most 0.0075.
Values may be sent and summed in bfloat16 or wider, within the bound.
A program may use at most 192 MiB of HBM per device.

v0:
```python
import jax
import jax.numpy as jnp
from jax import lax
from jax.sharding import PartitionSpec as P


def gelu_tanh(inputs):
    return jax.nn.gelu(inputs, approximate=True)


def pull_rows(table, chosen, is_live):
    taken = jnp.take(table, chosen.reshape(-1), axis=0)
    taken = taken.reshape(chosen.shape + table.shape[1:])
    return jnp.where(is_live[:, :, None, None], taken, jnp.zeros((), table.dtype))


def aggregate(sources, source_ids, tile_live, tile_vals):
    running = jnp.zeros((source_ids.shape[0], sources.shape[1], sources.shape[2]), jnp.float32)
    for tile_slot in range(source_ids.shape[1]):
        blocks = jnp.take(sources, source_ids[:, tile_slot], axis=0)
        product = jnp.einsum(
            "vfj,vji->vfi", blocks, tile_vals[:, tile_slot], preferred_element_type=jnp.float32
        )
        running = running + jnp.where(tile_live[:, tile_slot][:, None, None], product, 0.0)
    return running


def spread_back(back_second, source_ids, tile_live, tile_vals):
    batch_count = back_second.shape[0]
    targets = lax.broadcasted_iota(jnp.int32, (batch_count, batch_count), 1)
    running = jnp.zeros(back_second.shape, jnp.float32)
    for tile_slot in range(source_ids.shape[1]):
        product = jnp.einsum(
            "vai,vji->vaj", back_second, tile_vals[:, tile_slot], preferred_element_type=jnp.float32
        )
        matches = jnp.where(
            (source_ids[:, tile_slot][:, None] == targets) & tile_live[:, tile_slot][:, None],
            1.0,
            0.0,
        ).astype(jnp.float32)
        running = running + jnp.einsum(
            "vu,vaj->uaj", matches, product, precision=lax.Precision.HIGHEST
        )
    return running


def on_device(
    features,
    history_first,
    history_second,
    pull_list,
    pull_count,
    tile_src,
    tile_count,
    tile_values,
    w_first,
    w_second,
    bias_first,
    out_grad,
):
    first_full, second_full, bias_full = (
        lax.all_gather(w_first, "fsdp", axis=0, tiled=True),
        lax.all_gather(w_second, "fsdp", axis=0, tiled=True),
        lax.all_gather(bias_first, "fsdp", axis=0, tiled=True),
    )
    dom_size = lax.axis_size("dom")
    fsdp_size = lax.axis_size("fsdp")
    chosen = pull_list[0]
    requesters = chosen.shape[0]
    slot_cap = chosen.shape[1]
    is_live = lax.broadcasted_iota(jnp.int32, chosen.shape, 1) < pull_count[0][:, None]
    sent_first = pull_rows(history_first, chosen, is_live)
    sent_second = pull_rows(history_second, chosen, is_live)
    block_len = features.shape[2]
    first_cols = history_first.shape[1]
    second_cols = history_second.shape[1]
    arrived_first, arrived_second = (
        lax.all_to_all(
            sent_first.reshape(requesters, slot_cap, 1, first_cols, block_len),
            ("dom", "fsdp"),
            split_axis=0,
            concat_axis=2,
            tiled=True,
        ),
        lax.all_to_all(
            sent_second.reshape(requesters, slot_cap, 1, second_cols, block_len),
            ("dom", "fsdp"),
            split_axis=0,
            concat_axis=2,
            tiled=True,
        ),
    )
    pulled_first = arrived_first.reshape(slot_cap * dom_size, fsdp_size * first_cols, block_len)
    pulled_second = arrived_second.reshape(slot_cap * dom_size, fsdp_size * second_cols, block_len)
    tile_live = lax.broadcasted_iota(jnp.int32, tile_src.shape, 1) < tile_count[:, None]
    agg_first = aggregate(
        jnp.concatenate([features, pulled_first], 0), tile_src, tile_live, tile_values
    ).astype(jnp.bfloat16)
    pre_act = (
        jnp.einsum("fh,vfn->vhn", first_full, agg_first, preferred_element_type=jnp.float32)
        + bias_full.astype(jnp.float32)[None, :, None]
    )
    hidden_new = gelu_tanh(pre_act).astype(jnp.bfloat16)
    agg_second = aggregate(
        jnp.concatenate([hidden_new, pulled_second], 0), tile_src, tile_live, tile_values
    ).astype(jnp.bfloat16)
    back_second = jnp.einsum(
        "ab,vbn->van", second_full, out_grad, preferred_element_type=jnp.float32
    ).astype(jnp.bfloat16)
    back_hidden = spread_back(back_second, tile_src, tile_live, tile_values)
    _, pullback = jax.vjp(gelu_tanh, pre_act)
    back_pre = pullback(back_hidden)[0].astype(jnp.bfloat16)
    first_term = jnp.einsum("vfn,vhn->fh", agg_first, back_pre, preferred_element_type=jnp.float32)
    bias_term = jnp.sum(back_pre.astype(jnp.float32), axis=(0, 2))
    second_term = jnp.einsum(
        "van,vbn->ab", agg_second, out_grad, preferred_element_type=jnp.float32
    )
    first_shard, second_shard, bias_shard = (
        lax.psum_scatter(first_term, "fsdp", scatter_dimension=0, tiled=True),
        lax.psum_scatter(second_term, "fsdp", scatter_dimension=0, tiled=True),
        lax.psum_scatter(bias_term, "fsdp", scatter_dimension=0, tiled=True),
    )
    first_total, second_total, bias_total = lax.psum((first_shard, second_shard, bias_shard), "dom")
    return (hidden_new, first_total, second_total, bias_total)


def solution(mesh):
    return jax.shard_map(
        on_device,
        mesh=mesh,
        in_specs=(
            P(("dom", "fsdp"), None, None),
            P("dom", "fsdp", None),
            P("dom", "fsdp", None),
            P("dom", None, None),
            P("dom", None),
            P(("dom", "fsdp"), None),
            P(("dom", "fsdp")),
            P(("dom", "fsdp"), None, None, None),
            P("fsdp", None),
            P("fsdp", None),
            P("fsdp"),
            P(("dom", "fsdp"), None, None),
        ),
        out_specs=(P(("dom", "fsdp"), None, None), P("fsdp", None), P("fsdp", None), P("fsdp")),
        check_vma=False,
    )
```

profile of v0, /device:TPU:0, one launch (start us, length us, event | category | flops | bytes accessed | tf_op | source)
XLA Modules:
  0.0 578.2 jit_solution(3047371610428938256)
XLA Ops:
  7.2 0.9 copy.84
  8.2 5.3 gather_fusion
  13.4 5.3 gather_fusion.7
  18.8 4.0 broadcast_select_fusion
  22.8 3.7 select_bitcast_fusion
  26.5 7.4 %all-to-all-start = ((bf16[32,4,1,128,128]{4,3,1,2,0:T(8,128)(2,1)}), bf16[32,4,1,128,128]{4,3,1,2,0:T(8,128)(2,1)}, u32[]{:S(2)}, u32[]{:S(2)}) async-start(bf16[32,4,1,128,128]{4,3,1,2,0:T(8,128)(2,1)} %get-tuple-element.34), calls=%async_computation | async-start | bytes 8388608 | tf_op jit(solution)/shard_map/all_to_all | solution.py:78
  35.5 109.2 %all-gather = bf16[8,1,128]{2,1,0:T(2,128)(2,1)S(1)} all-gather(bf16[1,1,128]{2,1,0:T(2,128)(2,1)S(1)} %bitcast.154), channel_id=1, replica_groups=mesh['dom'=4,'fsdp'=8] {'fsdp'}, dimensions={0}, use_global_device_ids=true | all-gather | bytes 2304 | tf_op jit(solution)/shard_map/all_gather | solution.py:64
  145.1 17.6 %all-to-all-done = bf16[32,4,1,128,128]{4,3,1,2,0:T(8,128)(2,1)} async-done(((bf16[32,4,1,128,128]{4,3,1,2,0:T(8,128)(2,1)}), bf16[32,4,1,128,128]{4,3,1,2,0:T(8,128)(2,1)}, u32[]{:S(2)}, u32[]{:S(2)}) %all-to-all-start) | async-done | bytes 4194336 | tf_op jit(solution)/shard_map/all_to_all | solution.py:78
  162.8 10.8 %all-to-all-start.1 = ((bf16[32,4,1,128,128]{4,3,1,2,0:T(8,128)(2,1)}), bf16[32,4,1,128,128]{4,3,1,2,0:T(8,128)(2,1)}, u32[]{:S(2)}, u32[]{:S(2)}) async-start(bf16[32,4,1,128,128]{4,3,1,2,0:T(8,128)(2,1)} %get-tuple-element.33), calls=%async_computation.2 | async-start | bytes 8388608 | tf_op jit(solution)/shard_map/all_to_all | solution.py:85
  173.9 2.9 fusion.26
  176.8 1.4 fusion.103
  178.3 8.3 %fusion.22 = f32[4,1024,128]{2,0,1:T(4,128)} fusion(f32[4,1024,128]{2,1,0:T(8,128)S(1)} %fusion.103, s32[4]{0:T(128)S(1)} %get-tuple-element.25, pred[4]{0:T(512)(128)(4,1)S(1)} %get-tuple-element.40), kind=kOutput, calls=%fused_computation.48 | convolution fusion | flops 25165872 | bytes 4194324 | tf_op jit(solution)/shard_map/vu,vaj->uaj/dot_general | solution.py:41
  186.6 2.9 copy.100
  189.5 1.4 fusion.99
  191.0 8.3 %fusion.20 = f32[4,1024,128]{2,0,1:T(4,128)} fusion(f32[4,1024,128]{2,1,0:T(8,128)S(1)} %fusion.99, s32[4]{0:T(128)S(1)} %get-tuple-element.24, pred[4]{0:T(512)(128)(4,1)S(1)} %get-tuple-element.39), kind=kOutput, calls=%fused_computation.46 | convolution fusion | flops 25165872 | bytes 4194324 | tf_op jit(solution)/shard_map/vu,vaj->uaj/dot_general | solution.py:41
  199.3 2.9 copy.103
  202.2 1.4 fusion.95
  203.6 8.6 %fusion.18 = f32[4,1024,128]{2,0,1:T(4,128)} fusion(f32[4,1024,128]{2,1,0:T(8,128)S(1)} %fusion.95, s32[4]{0:T(128)S(1)} %get-tuple-element.23, pred[4]{0:T(512)(128)(4,1)S(1)} %get-tuple-element.38), kind=kOutput, calls=%fused_computation.44 | convolution fusion | flops 25165872 | bytes 4194324 | tf_op jit(solution)/shard_map/vu,vaj->uaj/dot_general | solution.py:41
  212.2 2.9 copy.106
  215.2 1.4 fusion.91
  216.6 8.4 %fusion.16 = f32[4,1024,128]{2,0,1:T(4,128)} fusion(f32[4,1024,128]{2,1,0:T(8,128)S(1)} %fusion.91, s32[4]{0:T(128)S(1)} %get-tuple-element.27, pred[4]{0:T(512)(128)(4,1)S(1)} %get-tuple-element.37), kind=kOutput, calls=%fused_computation.42 | convolution fusion | flops 25165872 | bytes 4194324 | tf_op jit(solution)/shard_map/vu,vaj->uaj/dot_general | solution.py:41
  225.0 2.9 copy.109
  227.9 1.4 fusion.87
  229.4 8.8 %fusion.14 = f32[4,1024,128]{2,0,1:T(4,128)} fusion(f32[4,1024,128]{2,1,0:T(8,128)S(1)} %fusion.87, s32[4]{0:T(128)S(1)} %get-tuple-element.22, pred[4]{0:T(512)(128)(4,1)S(1)} %get-tuple-element.36), kind=kOutput, calls=%fused_computation.40 | convolution fusion | flops 25165872 | bytes 4194324 | tf_op jit(solution)/shard_map/vu,vaj->uaj/dot_general | solution.py:41
  238.2 2.9 copy.112
  241.1 1.4 fusion.107
  242.5 7.3 %fusion.24 = f32[4,1024,128]{2,0,1:T(4,128)S(1)} fusion(f32[4,1024,128]{2,1,0:T(8,128)S(1)} %fusion.107, s32[4]{0:T(128)S(1)} %get-tuple-element.26, pred[4]{0:T(512)(128)(4,1)S(1)} %get-tuple-element.35), kind=kOutput, calls=%fused_computation.50 | convolution fusion | flops 25165872 | bytes 4194324 | tf_op jit(solution)/shard_map/vu,vaj->uaj/dot_general | solution.py:41
  249.9 2.0 copy.99
  251.9 2.6 copy.86
  254.5 2.8 pad_maximum_fusion
  257.3 4.1 gather_fusion.5
  261.4 4.2 gather_fusion.4
  265.6 4.2 gather_fusion.3
  269.8 4.1 gather_fusion.2
  273.9 3.3 gather_fusion.1
  277.2 4.1 gather_fusion.6
  281.4 1.8 fusion.42
  285.9 0.7 copy-done.5
  286.7 3.1 add_convert_fusion.1
  289.7 9.3 %convert_reduce_fusion = (f32[1024]{0:T(1024)S(1)}, bf16[4,1024,128]{1,2,0:T(8,128)(2,1)}, bf16[4,1024,128]{1,2,0:T(8,128)(2,1)}) fusion(f32[1024]{0:T(1024)S(1)} %bitcast.152, f32[4,1024,128]{1,2,0:T(8,128)} %copy.112, f32[4,1024,128]{1,2,0:T(8,128)} %copy.109, f32[4,1024,128]{1,2,0:T(8,128)} %copy.106, f32[4,1024,128]{1,2,0:T(8,128)} %copy.103, ...), kind=kOutput, calls=%fused_computation.52 | convolution fusion | flops 1089469440 | bytes 17833984 | tf_op jit(solution)/shard_map/fh,vfn->vhn/dot_general | solution.py:100
  299.0 1.8 copy.117
  300.9 2.9 copy.115
  303.8 2.8 pad_maximum_fusion.1
  306.5 4.2 gather_fusion.11
  310.7 4.2 gather_fusion.10
  314.9 4.2 gather_fusion.9
  319.1 4.2 gather_fusion.8
  323.2 4.1 gather_fusion.12
  327.4 4.2 gather_fusion.13
  331.6 1.8 fusion.33
  333.5 1.8 fusion.35
  335.3 1.8 fusion.37
  337.1 1.8 fusion.39
  339.0 1.8 fusion.31
  340.8 7.8 %convolution_bitcast_fusion = f32[1024,1024]{1,0:T(8,128)} fusion(bf16[4,1024,128]{2,1,0:T(8,128)(2,1)S(1)} %copy-done, f32[4,1024,128]{2,1,0:T(8,128)} %fusion.31, f32[4,1024,128]{2,1,0:T(8,128)S(1)} %fusion.33, f32[4,1024,128]{2,1,0:T(8,128)} %fusion.35, f32[4,1024,128]{2,1,0:T(8,128)} %fusion.37, f32[4,1024,128]{2,1,0:T(8,128)} %fusion.39, ...), kind=kOutput, calls=%fused_computation.22 | convolution fusion | flops 1214775296 | bytes 16908316 | tf_op jit(solution)/shard_map/van,vbn->ab/dot_general | solution.py:115
  348.6 1.1 copy-done.4
  350.1 3.2 convolution_bitcast_fusion.1
  353.4 84.4 %reduce-scatter.5.cloned.1.call-done = f32[128,1024]{1,0:T(8,128)} async-done(((f32[1024,1024]{1,0:T(8,128)}), f32[128,1024]{1,0:T(8,128)}) %reduce-scatter.5.cloned.1.call-update) | async-done | bytes 524304 | tf_op jit(solution)/shard_map/reduce_scatter | solution.py:120
  437.8 91.8 %reduce-scatter.3.cloned.1.call-done = f32[128,1024]{1,0:T(8,128)} async-done(((f32[1024,1024]{1,0:T(8,128)}), f32[128,1024]{1,0:T(8,128)}) %reduce-scatter.3.cloned.1.call-update) | async-done | bytes 524304 | tf_op jit(solution)/shard_map/reduce_scatter | solution.py:119
  530.9 20.2 %all-reduce = f32[1024]{0:T(1024)S(1)} all-reduce(f32[1024]{0:T(1024)S(1)} %get-tuple-element.30), channel_id=4, replica_groups=mesh['dom'=4,'fsdp'=8] {'fsdp'}, use_global_device_ids=true, to_apply=%region_5.8.clone | all-reduce | flops 1024 | bytes 8192
  551.1 6.1 %psum.23 = f32[128]{0:T(128)} all-reduce(f32[128]{0:T(128)S(1)} %dynamic-slice.1), channel_id=1, replica_groups=mesh['dom'=4,'fsdp'=8] {'dom'}, use_global_device_ids=true, to_apply=%region_6.9 | all-reduce | flops 128 | bytes 1024 | tf_op jit(solution)/shard_map/psum | solution.py:123
  557.3 10.5 %all-reduce.4.cloned.1.call-done = (f32[128,1024]{1,0:T(8,128)}, f32[128,1024]{1,0:T(8,128)}) async-done(((f32[128,1024]{1,0:T(8,128)}, f32[128,1024]{1,0:T(8,128)}), (f32[128,1024]{1,0:T(8,128)}, f32[128,1024]{1,0:T(8,128)})) %all-reduce.4.cloned.1.call-update) | async-done | bytes 1048592 | tf_op jit(solution)/shard_map/psum | solution.py:123
  567.7 1.9 copy.147
  569.6 1.9 copy.148
  (81 shorter events, 6.2 us)
Async XLA Ops:
  7.2 166.8 %copy-start = (bf16[4,1024,128]{2,1,0:T(8,128)(2,1)S(1)}, bf16[4,1024,128]{2,1,0:T(8,128)(2,1)}, u32[]{:S(2)}) copy-start(bf16[4,1024,128]{2,1,0:T(8,128)(2,1)} %param.27) | copy-start | bytes 3145732
  13.4 5.3 copy-start.17
  26.5 8.9 %copy-start.18 = (bf16[128]{0:T(256)(128)(2,1)S(1)}, bf16[128]{0:T(256)(128)(2,1)}, u32[]{:S(2)}) copy-start(bf16[128]{0:T(256)(128)(2,1)} %param.26) | copy-start | bytes 772
  26.5 118.2 %copy-start.16 = (s32[4,6]{1,0:T(4,128)S(1)}, s32[4,6]{1,0:T(4,128)}, u32[]{:S(2)}) copy-start(s32[4,6]{1,0:T(4,128)} %param.21) | copy-start | bytes 292
  26.5 118.6 %copy-start.19 = (s32[4]{0:T(128)S(1)}, s32[4]{0:T(128)}, u32[]{:S(2)}) copy-start(s32[4]{0:T(128)} %param.22) | copy-start | bytes 52
  26.5 136.3 %all-to-all-start = ((bf16[32,4,1,128,128]{4,3,1,2,0:T(8,128)(2,1)}), bf16[32,4,1,128,128]{4,3,1,2,0:T(8,128)(2,1)}, u32[]{:S(2)}, u32[]{:S(2)}) async-start(bf16[32,4,1,128,128]{4,3,1,2,0:T(8,128)(2,1)} %get-tuple-element.34), calls=%async_computation | async-start | bytes 8388608 | tf_op jit(solution)/shard_map/all_to_all | solution.py:78
  34.0 140.0 %all-gather.6.cloned.1.call-start = ((), (), s32[]{:S(2)}) async-start(), calls=%async_computation.5 | async-start | bytes 2359296 | tf_op jit(solution)/shard_map/all_gather | solution.py:63
  34.7 255.0 %all-gather.4.cloned.1.call-start = ((), (), s32[]{:S(2)}) async-start(), calls=%async_computation.4 | async-start | bytes 2359296 | tf_op jit(solution)/shard_map/all_gather | solution.py:62
  162.8 138.1 %all-to-all-start.1 = ((bf16[32,4,1,128,128]{4,3,1,2,0:T(8,128)(2,1)}), bf16[32,4,1,128,128]{4,3,1,2,0:T(8,128)(2,1)}, u32[]{:S(2)}, u32[]{:S(2)}) async-start(bf16[32,4,1,128,128]{4,3,1,2,0:T(8,128)(2,1)} %get-tuple-element.33), calls=%async_computation.2 | async-start | bytes 8388608 | tf_op jit(solution)/shard_map/all_to_all | solution.py:85
  173.6 264.2 %reduce-scatter.5.cloned.1.call-start = ((), (), s32[]{:S(2)}) async-start(), calls=%async_computation.7 | async-start | bytes 4718592 | tf_op jit(solution)/shard_map/reduce_scatter | solution.py:120
  251.9 2.6 copy-start.14
  273.9 7.5 %copy-start.2 = (bf16[4,6,128,128]{3,2,1,0:T(8,128)(2,1)S(1)}, bf16[4,6,128,128]{3,2,1,0:T(8,128)(2,1)}, u32[]{:S(2)}) copy-start(bf16[4,6,128,128]{3,2,1,0:T(8,128)(2,1)} %param.23) | copy-start | bytes 2359300
  281.4 1.8 copy-start.13
  283.2 1.2 copy-start.12
  283.7 1.3 copy-start.11
  285.5 1.2 copy-start.5
  286.7 3.1 copy-start.1
  300.9 2.9 copy-start.6
  331.6 1.8 copy-start.3
  331.6 1.9 copy-start.10
  333.5 1.8 copy-start.9
  335.3 1.8 copy-start.8
  337.1 1.8 copy-start.7
  348.6 1.2 copy-start.4
  348.6 1.5 copy-start.15
  348.6 181.0 %reduce-scatter.3.cloned.1.call-start = ((), (), s32[]{:S(2)}) async-start(), calls=%async_computation.6 | async-start | bytes 4718592 | tf_op jit(solution)/shard_map/reduce_scatter | solution.py:119
  353.3 176.3 %copy-start.20 = (u32[32]{0:T(128)S(1)}, u32[32]{0:T(128)}, u32[]{:S(2)}) copy-start(u32[32]{0:T(128)} %constant.46) | copy-start | bytes 388
  353.4 214.4 %all-reduce.4.cloned.1.call-start = ((), (), s32[]{:S(2)}) async-start(), calls=%async_computation.8 | async-start | bytes 2097152 | tf_op jit(solution)/shard_map/psum | solution.py:123
Sparse Core Ops, SparseCore 0:
  36.9 98.7 all-gather.5
  137.8 63.8 all-gather.3
  348.7 89.0 reduce-scatter.4
  441.7 87.8 reduce-scatter.2
  531.9 35.7 all-reduce.3
where the time goes:
time: 583 us; the launch traced here: 578 us
  waiting for transfers between devices  206 us (35%)
  blocking collectives  136 us (23%)
  matrix products  97.4 us (17%)
  local copies, waits for them, and re-layouts  92.3 us (16%)
  starting transfers between devices  18.7 us (3%)
  between operations  15.1 us (3%)
  other arithmetic  13.4 us (2%)
    all_gather x1, blocking collectives, on_device(): lax.all_gather(bias_first, 'fsdp', axis=0, tiled=True)  109 us
    reduce_scatter x1, waiting for transfers between devices, on_device(): lax.psum_scatter(first_term, 'fsdp', scatter_dimension=0, tiled=True)  91.8 us
    reduce_scatter x1, waiting for transfers between devices, on_device(): lax.psum_scatter(second_term, 'fsdp', scatter_dimension=0, tiled=True)  84.4 us
    dot_general x6, matrix products, spread_back(): jnp.einsum('vu,vaj->uaj', matches, product, precision=lax.Precision.HIGHEST)  49.7 us
    gather x12, local copies, waits for them, and re-layouts, aggregate(): blocks = jnp.take(sources, source_ids[:, tile_slot], axis=0)  49.2 us
    unnamed x1, blocking collectives  20.2 us
    all_to_all x1, waiting for transfers between devices, on_device(): lax.all_to_all(sent_first.reshape(requesters, slot_cap, 1, first_cols, bl...  17.6 us
    dot_general x6, local copies, waits for them, and re-layouts, spread_back(): jnp.einsum('vu,vaj->uaj', matches, product, precision=lax.Precision.HIGHEST)  16.6 us
  transfers between devices with their start and end apart: 7, of which 4 were waited for; matrix products, arithmetic and copies ran while one was open for 22% of the time, Pallas kernels for 0%

commit v1 on v0

v1 whole, which is shorter than its diff:
```python
import functools

import jax
import jax.numpy as jnp
from jax import lax
from jax.experimental import pallas as pl
from jax.experimental.pallas import tpu as pltpu
from jax.sharding import PartitionSpec as P

F32 = jnp.float32
BF16 = jnp.bfloat16
CHUNK = 256
VMEM_BYTES = 48 * 1024 * 1024
LAST = (((1,), (1,)), ((), ()))


def add_sources(v, src_ref, cnt_ref, own_ref, arr_ref, tiles_ref, acc):
    own_count = own_ref.shape[0]
    parts = arr_ref.shape[0]
    acc[...] = jnp.zeros_like(acc)

    def step(t, carry):
        source = src_ref[v, t]
        tile = tiles_ref[v, t]

        @pl.when(source < own_count)
        def _():
            acc[...] += jnp.dot(own_ref[source], tile, preferred_element_type=F32)

        @pl.when(source >= own_count)
        def _():
            slot = source - own_count
            block = arr_ref[lax.rem(slot, parts), :, lax.div(slot, parts)]
            block = block.reshape(acc.shape)
            acc[...] += jnp.dot(block, tile, preferred_element_type=F32)

        return carry

    lax.fori_loop(0, cnt_ref[v], step, 0)


def outer_kernel_loop(left, right, out_ref):
    @pl.loop(0, left.shape[0] // CHUNK)
    def _(r):
        rows = pl.ds(pl.multiple_of(r * CHUNK, CHUNK), CHUNK)
        out_ref[rows, :] = lax.dot_general(
            left[rows, :], right[...], LAST, preferred_element_type=F32
        )


def back_kernel(src_ref, cnt_ref, w_ref, grad_ref, tiles_ref, out_ref, wide, second):
    count, _, block = grad_ref.shape
    for v in range(count):
        wide[:, v * block : (v + 1) * block] = grad_ref[v]

    @pl.loop(0, w_ref.shape[0] // CHUNK)
    def _(r):
        rows = pl.ds(pl.multiple_of(r * CHUNK, CHUNK), CHUNK)
        product = jnp.dot(w_ref[rows, :], wide[...], preferred_element_type=F32).astype(BF16)
        for v in range(count):
            second[v, rows, :] = product[:, v * block : (v + 1) * block]

    out_ref[...] = jnp.zeros_like(out_ref)
    for v in range(count):

        def step(t, carry, v=v):
            source = src_ref[v, t]

            @pl.when(source < count)
            def _():
                out_ref[source] += lax.dot_general(
                    second[v], tiles_ref[v, t], LAST, preferred_element_type=F32
                )

            return carry

        lax.fori_loop(0, cnt_ref[v], step, 0)


def first_kernel(
    src_ref, cnt_ref, own_ref, arr_ref, tiles_ref, w_ref, bias_ref, back_ref,
    hidden_ref, grad_ref, sum_ref, acc, agg, pre_grad,
):
    count, _, block = own_ref.shape
    for v in range(count):
        add_sources(v, src_ref, cnt_ref, own_ref, arr_ref, tiles_ref, acc)
        agg[:, v * block : (v + 1) * block] = acc[...].astype(BF16)

    @pl.loop(0, w_ref.shape[0] // CHUNK)
    def _(r):
        rows = pl.ds(pl.multiple_of(r * CHUNK, CHUNK), CHUNK)
        x = jnp.dot(w_ref[rows, :], agg[...], preferred_element_type=F32) + bias_ref[rows, :]
        square = x * x
        bent = jnp.tanh(0.7978845608028654 * x * (1.0 + 0.044715 * square))
        half = 0.5 + 0.5 * bent
        hidden = (x * half).astype(BF16)
        slope = half + 0.5 * x * (1.0 - bent * bent) * (
            0.7978845608028654 * (1.0 + 3.0 * 0.044715 * square)
        )
        for v in range(count):
            columns = slice(v * block, (v + 1) * block)
            hidden_ref[v, rows, :] = hidden[:, columns]
            pre_grad[rows, columns] = (back_ref[v, rows, :] * slope[:, columns]).astype(BF16)

    outer_kernel_loop(agg, pre_grad, grad_ref)
    ones = jnp.ones((sum_ref.shape[0], pre_grad.shape[1]), BF16)
    sum_ref[...] = lax.dot_general(ones, pre_grad[...], LAST, preferred_element_type=F32)


def second_kernel(
    src_ref, cnt_ref, own_ref, arr_ref, tiles_ref, cot_ref, grad_ref, acc, agg, wide
):
    count, _, block = own_ref.shape
    for v in range(count):
        add_sources(v, src_ref, cnt_ref, own_ref, arr_ref, tiles_ref, acc)
        agg[:, v * block : (v + 1) * block] = acc[...].astype(BF16)
        wide[:, v * block : (v + 1) * block] = cot_ref[v]
    outer_kernel_loop(agg, wide, grad_ref)


def local_call(kernel, name, scalars, operands, out_shape, scratch, flops):
    in_specs = [pl.BlockSpec(memory_space=pltpu.SMEM)] * len(scalars)
    in_specs += [pl.BlockSpec(memory_space=pltpu.VMEM)] * len(operands)
    moved = sum(a.size * a.dtype.itemsize for a in operands)
    return pl.pallas_call(
        kernel,
        name=name,
        out_shape=out_shape,
        in_specs=in_specs,
        out_specs=jax.tree.map(lambda _: pl.BlockSpec(memory_space=pltpu.VMEM), out_shape),
        scratch_shapes=scratch,
        compiler_params=pltpu.CompilerParams(vmem_limit_bytes=VMEM_BYTES),
        cost_estimate=pl.CostEstimate(flops=flops, bytes_accessed=moved * 2, transcendentals=0),
    )(*scalars, *operands)


def shifted(axis_name, size, stride, length, k):
    pairs = []
    for index in range(size):
        digit = index // stride % length
        pairs.append((index, index + ((digit + k) % length - digit) * stride))
    return functools.partial(lax.ppermute, axis_name=axis_name, perm=pairs)


def scatter_sum(terms, dim, hop, digit, length):
    mine = lax.dynamic_index_in_dim(terms, digit, dim, keepdims=False)
    for k in range(1, length):
        theirs = lax.dynamic_index_in_dim(terms, (digit + k) % length, dim, keepdims=False)
        mine = mine + hop(k)(theirs.astype(BF16)).astype(F32)
    return mine


def gather_all(piece, hop, digit, length):
    whole = jnp.zeros((length,) + piece.shape, piece.dtype)
    whole = lax.dynamic_update_index_in_dim(whole, piece, digit, 0)
    for k in range(1, length):
        whole = lax.dynamic_update_index_in_dim(
            whole, hop(k)(piece), (digit - k + length) % length, 0
        )
    return whole


def sum_all(vector, hop, length):
    total = vector
    for k in range(1, length):
        total = total + hop(k)(vector)
    return total


def on_device(
    features,
    history_first,
    history_second,
    pull_list,
    pull_count,
    tile_src,
    tile_count,
    tile_values,
    w_first,
    w_second,
    bias_first,
    out_grad,
):
    dom_size = lax.axis_size("dom")
    fsdp_size = lax.axis_size("fsdp")
    dom_index = lax.axis_index("dom")
    fsdp_index = lax.axis_index("fsdp")
    cores = 2 if dom_size % 2 == 0 else 1
    y_size = dom_size // cores
    z_size = 4 if fsdp_size % 4 == 0 else 1
    x_size = fsdp_size // z_size
    core, y = dom_index % cores, dom_index // cores
    x, z = fsdp_index % x_size, fsdp_index // x_size

    def core_hop(k):
        return shifted("dom", dom_size, 1, cores, k)

    def y_hop(k):
        return shifted("dom", dom_size, cores, y_size, k)

    def x_hop(k):
        return shifted("fsdp", fsdp_size, 1, x_size, k)

    def z_hop(k):
        return shifted("fsdp", fsdp_size, x_size, z_size, k)

    count, width, block = features.shape
    hidden_width = w_first.shape[1]

    chosen = pull_list[0]
    requesters, cap = chosen.shape
    live = lax.broadcasted_iota(jnp.int32, chosen.shape, 1) < pull_count[0][:, None]

    def pull(table):
        taken = jnp.take(table, chosen.reshape(-1), axis=0)
        taken = taken.reshape(chosen.shape + table.shape[1:])
        sent = jnp.where(live[:, :, None, None], taken, jnp.zeros((), table.dtype))
        got = lax.all_to_all(sent, ("dom", "fsdp"), split_axis=0, concat_axis=0, tiled=True)
        return got.reshape(dom_size, fsdp_size, cap, table.shape[1], block)

    arrived_first = pull(history_first)
    arrived_second = pull(history_second)

    rows = w_first.shape[0]
    share = rows // dom_size
    bias_row = jnp.pad(bias_first[None, :], ((0, 15), (0, hidden_width - bias_first.shape[0])))
    payload = jnp.concatenate(
        [
            lax.dynamic_slice_in_dim(w_first, dom_index * share, share, 0),
            lax.dynamic_slice_in_dim(w_second, dom_index * share, share, 0),
            bias_row,
        ],
        0,
    )
    along = lax.all_gather(payload, "fsdp", axis=0)
    bias_full = along[:, 2 * share, : bias_first.shape[0]].reshape(hidden_width)
    both = lax.all_gather(along[:, : 2 * share], "dom", axis=0)
    both = both.reshape(dom_size, fsdp_size, 2, share, hidden_width)
    both = both.transpose(2, 1, 0, 3, 4).reshape(2, width, hidden_width)
    first_turned = both[0].T
    second_full = both[1]

    scalars = (tile_src, tile_count)
    wide = count * block
    mat = 2 * width * hidden_width * wide
    back_hidden = local_call(
        back_kernel,
        "back_to_hidden",
        scalars,
        (second_full, out_grad, tile_values),
        jax.ShapeDtypeStruct((count, hidden_width, block), F32),
        [
            pltpu.VMEM((hidden_width, wide), BF16),
            pltpu.VMEM((count, hidden_width, block), BF16),
        ],
        2 * mat,
    )
    hidden_new, first_term, bias_rows = local_call(
        first_kernel,
        "first_layer",
        scalars,
        (
            features,
            arrived_first,
            tile_values,
            first_turned,
            bias_full.astype(F32)[:, None],
            back_hidden,
        ),
        (
            jax.ShapeDtypeStruct((count, hidden_width, block), BF16),
            jax.ShapeDtypeStruct((width, hidden_width), F32),
            jax.ShapeDtypeStruct((8, hidden_width), F32),
        ),
        [
            pltpu.VMEM((width, block), F32),
            pltpu.VMEM((width, wide), BF16),
            pltpu.VMEM((hidden_width, wide), BF16),
        ],
        4 * mat,
    )
    second_term = local_call(
        second_kernel,
        "second_layer",
        scalars,
        (hidden_new, arrived_second, tile_values, out_grad),
        jax.ShapeDtypeStruct((hidden_width, hidden_width), F32),
        [
            pltpu.VMEM((hidden_width, block), F32),
            pltpu.VMEM((hidden_width, wide), BF16),
            pltpu.VMEM((hidden_width, wide), BF16),
        ],
        3 * mat,
    )

    def total(term):
        terms = term.reshape(z_size, x_size, y_size, cores, share, hidden_width)
        terms = scatter_sum(terms, 3, core_hop, core, cores)
        terms = scatter_sum(terms, 1, x_hop, x, x_size)
        terms = scatter_sum(terms, 1, y_hop, y, y_size)
        piece = scatter_sum(terms, 0, z_hop, z, z_size)
        pieces = gather_all(piece, y_hop, y, y_size)
        pieces = gather_all(pieces, core_hop, core, cores)
        return pieces.transpose(1, 0, 2, 3).reshape(rows, hidden_width)

    bias_sum = sum_all(bias_rows[0], core_hop, cores)
    bias_sum = sum_all(bias_sum, x_hop, x_size)
    bias_sum = sum_all(bias_sum, y_hop, y_size)
    bias_sum = sum_all(bias_sum, z_hop, z_size)
    bias_len = bias_first.shape[0]
    bias_total = lax.dynamic_slice_in_dim(bias_sum, fsdp_index * bias_len, bias_len, 0)
    return (hidden_new, total(first_term), total(second_term), bias_total)


def solution(mesh):
    return jax.shard_map(
        on_device,
        mesh=mesh,
        in_specs=(
            P(("dom", "fsdp"), None, None),
            P("dom", "fsdp", None),
            P("dom", "fsdp", None),
            P("dom", None, None),
            P("dom", None),
            P(("dom", "fsdp"), None),
            P(("dom", "fsdp")),
            P(("dom", "fsdp"), None, None, None),
            P("fsdp", None),
            P("fsdp", None),
            P("fsdp"),
            P(("dom", "fsdp"), None, None),
        ),
        out_specs=(P(("dom", "fsdp"), None, None), P("fsdp", None), P("fsdp", None), P("fsdp")),
        check_vma=False,
    )
```

time: 583 us -> 334 us (0.57)
  blocking collectives: 136 us -> 0 us
  matrix products: 97.4 us -> 0 us
  local copies, waits for them, and re-layouts: 92.3 us -> 34.6 us
  Pallas kernels: 0 us -> 28.1 us
  starting transfers between devices: 18.7 us -> 28.4 us
  waiting for transfers between devices: 206 us -> 214 us
    reduce_scatter x2 -> x0, waiting for transfers between devices: 176 us -> none  [the longest x1 91.8 us: on_device(): lax.psum_scatter(first_term, 'fsdp', scatter_dimension=0, tiled=True)]
    all_gather x1 -> x0, blocking collectives: 109 us -> none  [on_device(): lax.all_gather(bias_first, 'fsdp', axis=0, tiled=True)]
    dot_general x27 -> x0, matrix products: 97.4 us -> none  [the longest x6 49.7 us: spread_back(): jnp.einsum('vu,vaj->uaj', matches, product, precision=lax.Precision.HIGHEST)]
    all_to_all x2, waiting for transfers between devices: 17.6 us -> 109 us  [pull(): lax.all_to_all(sent, ('dom', 'fsdp'), split_axis=0, concat_axis=0, tiled=...]
    all_gather x2, waiting for transfers between devices: 0.02 us -> 67 us  [the longest x1 67 us: on_device(): both = lax.all_gather(along[:, :2 * share], 'dom', axis=0)]
    gather x14 -> x2, local copies, waits for them, and re-layouts: 59.7 us -> 10.6 us  [pull(): taken = jnp.take(table, chosen.reshape(-1), axis=0)]
    ppermute x0 -> x22, waiting for transfers between devices: none -> 38.2 us  [the longest x12 23.6 us: scatter_sum(): mine = mine + hop(k)(theirs.astype(BF16)).astype(F32)]
    pallas_call x0 -> x3, Pallas kernels: none -> 28.1 us  [local_call(): pl.pallas_call(kernel, name=name, out_shape=out_shape, in_specs=in_specs,...]
  transfers between devices with their start and end apart: 7 -> 26, of which waited for: 4 -> 14; matrix products, arithmetic and copies ran while one was open for 22% -> 7% of each run, Pallas kernels for 0% -> 8%
where the time goes in v1:
time: 334 us; the launch traced here: 333 us
  waiting for transfers between devices  214 us (64%)
  local copies, waits for them, and re-layouts  34.6 us (10%)
  starting transfers between devices  28.4 us (9%)
  Pallas kernels  28.1 us (8%)
  between operations  14.5 us (4%)
  other arithmetic  13.3 us (4%)
    all_to_all x2, waiting for transfers between devices, pull(): lax.all_to_all(sent, ('dom', 'fsdp'), split_axis=0, concat_axis=0, tiled=...  109 us
    all_gather x1, waiting for transfers between devices, on_device(): both = lax.all_gather(along[:, :2 * share], 'dom', axis=0)  67 us
    pallas_call x3, Pallas kernels, local_call(): pl.pallas_call(kernel, name=name, out_shape=out_shape, in_specs=in_specs,...  28.1 us
    ppermute x12, waiting for transfers between devices, scatter_sum(): mine = mine + hop(k)(theirs.astype(BF16)).astype(F32)  23.6 us
    ppermute x12, starting transfers between devices, scatter_sum(): mine = mine + hop(k)(theirs.astype(BF16)).astype(F32)  11.8 us
    all_to_all x2, starting transfers between devices, pull(): lax.all_to_all(sent, ('dom', 'fsdp'), split_axis=0, concat_axis=0, tiled=...  11 us
    gather x2, local copies, waits for them, and re-layouts, pull(): taken = jnp.take(table, chosen.reshape(-1), axis=0)  10.6 us
    ppermute x6, waiting for transfers between devices, sum_all(): total = total + hop(k)(vector)  8.67 us
  transfers between devices with their start and end apart: 26, of which 14 were waited for; matrix products, arithmetic and copies ran while one was open for 7% of the time, Pallas kernels for 8%

profile of v1, /device:TPU:0, one launch (start us, length us, event | category | flops | bytes accessed | tf_op | source)
XLA Modules:
  0.0 333.3 jit_solution(10743254870288860367)
XLA Ops:
  7.2 0.8 copy.39
  7.9 0.1 reshape_squeeze.2
  8.1 5.2 %gather_fusion.1 = bf16[128,128,128]{2,1,0:T(8,128)(2,1)} fusion(bf16[128,128,128]{2,1,0:T(8,128)(2,1)} %param.16, s32[1024]{0:T(1024)S(1)} %pad_clamp_fusion), kind=kCustom, calls=%fused_computation.1.clone | custom fusion | bytes 8389120 | tf_op jit(solution)/shard_map/jit(_take)/gather | solution.py:215
  13.3 5.3 %gather_fusion = bf16[128,128,128]{2,1,0:T(8,128)(2,1)} fusion(bf16[128,128,128]{2,1,0:T(8,128)(2,1)} %param.15, s32[1024]{0:T(1024)S(1)} %pad_clamp_fusion), kind=kCustom, calls=%fused_computation.clone | custom fusion | bytes 8389120 | tf_op jit(solution)/shard_map/jit(_take)/gather | solution.py:215
  18.6 0.1 iota_compare_fusion.1
  18.7 4.0 %broadcast_select_fusion = (bf16[128,128,128]{2,1,0:T(8,128)(2,1)S(1)}, bf16[128,128,128]{2,1,0:T(8,128)(2,1)S(1)}) fusion(bf16[128,128,128]{2,1,0:T(8,128)(2,1)} %gather_fusion.1, pred[128]{0:T(512)(128)(4,1)S(1)} %compare_and_fusion, bf16[128,128,128]{2,1,0:T(8,128)(2,1)} %gather_fusion), kind=kLoop, calls=%fused_computation.2 | loop fusion | flops 4194304 | bytes 16777344 | tf_op jit(solution)/shard_map/jit(_take)/select_n | solution.py:215
  22.7 3.7 %broadcast_select_fusion.2 = (bf16[32,4,128,128]{3,2,1,0:T(8,128)(2,1)}, bf16[32,4,128,128]{3,2,1,0:T(8,128)(2,1)}) fusion(bf16[32,4,128,128]{3,2,1,0:T(8,128)(2,1)S(1)} %bitcast.101, pred[32,4]{1,0:T(8,128)(4,1)S(1)} %iota_compare_fusion.1, bf16[32,4,128,128]{3,2,1,0:T(8,128)(2,1)S(1)} %bitcast.102), kind=kLoop, calls=%fused_computation.4 | loop fusion | flops 4194304 | bytes 16777344 | tf_op jit(solution)/shard_map/jit(_where)/select_n | solution.py:217
  26.4 7.4 %all-to-all-start = ((bf16[32,4,128,128]{3,2,1,0:T(8,128)(2,1)}), bf16[32,4,128,128]{3,2,1,0:T(8,128)(2,1)}, u32[]{:S(2)}, u32[]{:S(2)}) async-start(bf16[32,4,128,128]{3,2,1,0:T(8,128)(2,1)} %get-tuple-element.24), calls=%async_computation | async-start | bytes 8388608 | tf_op jit(solution)/shard_map/all_to_all | solution.py:218
  33.9 0.9 constant_dynamic-slice_fusion
  34.8 0.7 fusion.7
  35.5 109.2 %all-to-all-done = bf16[32,4,128,128]{3,2,1,0:T(8,128)(2,1)} async-done(((bf16[32,4,128,128]{3,2,1,0:T(8,128)(2,1)}), bf16[32,4,128,128]{3,2,1,0:T(8,128)(2,1)}, u32[]{:S(2)}, u32[]{:S(2)}) %all-to-all-start) | async-done | bytes 4194336 | tf_op jit(solution)/shard_map/all_to_all | solution.py:218
  144.7 3.6 %all-to-all-start.1 = ((bf16[32,4,128,128]{3,2,1,0:T(8,128)(2,1)}), bf16[32,4,128,128]{3,2,1,0:T(8,128)(2,1)}, u32[]{:S(2)}, u32[]{:S(2)}) async-start(bf16[32,4,128,128]{3,2,1,0:T(8,128)(2,1)} %get-tuple-element.23), calls=%async_computation.1 | async-start | bytes 8388608 | tf_op jit(solution)/shard_map/all_to_all | solution.py:218
  148.3 2.3 slice.26
  150.6 0.7 fusion.18
  151.4 0.2 copy.43.bias_ref
  151.6 67.0 %all-gather.7.cloned.1.call-done = bf16[32,64,1024]{2,1,0:T(8,128)(2,1)} async-done(((bf16[8,64,1024]{2,1,0:T(8,128)(2,1)}), bf16[32,64,1024]{2,1,0:T(8,128)(2,1)}) %all-gather.7.cloned.1.call-update) | async-done | bytes 4194320 | tf_op jit(solution)/shard_map/all_gather | solution.py:237
  218.6 4.2 %fusion.21 = (bf16[1,8,4,32,1024]{4,3,0,1,2:T(8,128)(2,1)}, bf16[1,8,4,32,1024]{4,3,0,1,2:T(8,128)(2,1)S(1)}) fusion(bf16[2,8,4,32,1024]{4,3,0,1,2:T(8,128)(2,1)} %bitcast.104), kind=kLoop, calls=%fused_computation.62 | loop fusion | bytes 8388608 | tf_op jit(solution)/shard_map/slice | solution.py:241
  222.8 1.6 copy.40
  224.3 2.9 copy.41
  227.3 1.9 copy.42
  229.3 4.0 %back_to_hidden.1.back_ref = f32[4,1024,128]{2,1,0:T(8,128)S(1)} custom-call(s32[4,6]{1,0:T(4,128)S(1)} %copy-done.4, s32[4]{0:T(128)S(1)} %copy-done.5, bf16[1024,1024]{1,0:T(8,128)(2,1)S(1)} %bitcast.100, bf16[4,1024,128]{2,1,0:T(8,128)(2,1)S(1)} %copy-done.1, bf16[4,6,128,128]{3,2,1,0:T(8,128)(2,1)S(1)} %copy-done.3), custom_call_target="tpu_custom_call" | custom-call | flops 2147483648 | bytes 7864320 | tf_op jit(solution)/shard_map/back_to_hidden/pallas_call | solution.py:125
  233.3 1.3 copy-done.7
  234.6 13.8 %first_layer.1 = (bf16[4,1024,128]{2,1,0:T(8,128)(2,1)}, f32[1024,1024]{1,0:T(8,128)}, f32[8,1024]{1,0:T(8,128)S(1)}) custom-call(s32[4,6]{1,0:T(4,128)S(1)} %copy-done.4, s32[4]{0:T(128)S(1)} %copy-done.5, bf16[4,1024,128]{2,1,0:T(8,128)(2,1)S(1)} %copy-done, bf16[4,8,4,128,128]{4,3,2,1,0:T(8,128)(2,1)} %bitcast.2.arr_ref, ...), custom_call_target="tpu_custom_call" | custom-call | flops 4294967296 | bytes 20455424 | tf_op jit(solution)/shard_map/first_layer/pallas_call | solution.py:125
  248.4 1.7 fusion
  250.1 0.3 collective-permute-start
  250.4 1.2 copy-done.2
  251.7 1.2 copy-done.6
  252.9 10.3 %second_layer.1 = f32[1024,1024]{1,0:T(8,128)} custom-call(s32[4,6]{1,0:T(4,128)S(1)} %copy-done.4, s32[4]{0:T(128)S(1)} %copy-done.5, bf16[4,1024,128]{2,1,0:T(8,128)(2,1)S(1)} %copy-done.6, bf16[4,8,4,128,128]{4,3,2,1,0:T(8,128)(2,1)} %bitcast.32.arr_ref, bf16[4,6,128,128]{3,2,1,0:T(8,128)(2,1)S(1)} %copy-done.3, bf16[4,1024,128]{2,1,0:T(8,128)(2,1)S(1)} %copy-done.2), custom_call_target="tpu_custom_call" | custom-call | flops 3221225472 | bytes 14155776 | tf_op jit(solution)/shard_map/second_layer/pallas_call | solution.py:125
  263.2 1.7 fusion.1
  265.0 0.1 collective-permute-start.8
  265.1 0.5 collective-permute-start.16
  265.5 1.8 collective-permute-done.16
  267.4 3.6 %collective-permute-done.17 = f32[1024]{0:T(1024)S(1)} collective-permute-done((f32[1024]{0:T(1024)S(1)}, f32[1024]{0:T(1024)S(1)}, u32[]{:S(2)}, u32[]{:S(2)}) %collective-permute-start.17) | collective-permute-done | bytes 4128 | tf_op jit(solution)/shard_map/ppermute | solution.py:166
  271.0 0.4 collective-permute-start.18
  271.3 3.2 collective-permute-done.18
  274.6 2.3 collective-permute-start.21
  276.9 0.6 collective-permute-start.19
  277.5 1.9 bitcast_add_fusion.1
  279.4 0.1 fusion.2
  279.5 0.1 collective-permute-start.1
  279.6 1.7 bitcast_add_fusion
  281.3 0.1 fusion.3
  281.4 2.1 collective-permute-start.9
  283.5 0.6 dynamic_slice.95
  284.1 10.4 %collective-permute-done.1 = bf16[4,2,32,1024]{3,2,1,0:T(8,128)(2,1)S(1)} collective-permute-done((bf16[4,2,32,1024]{3,2,1,0:T(8,128)(2,1)S(1)}, bf16[4,2,32,1024]{3,2,1,0:T(8,128)(2,1)S(1)}, u32[]{:S(2)}, u32[]{:S(2)}) %collective-permute-start.1) | collective-permute-done | bytes 524320 | tf_op jit(solution)/shard_map/ppermute | solution.py:149
  294.4 0.1 bitcast_add_fusion.3
  294.7 7.2 %collective-permute-done.9 = bf16[4,2,32,1024]{3,2,1,0:T(8,128)(2,1)S(1)} collective-permute-done((bf16[4,2,32,1024]{3,2,1,0:T(8,128)(2,1)S(1)}, bf16[4,2,32,1024]{3,2,1,0:T(8,128)(2,1)S(1)}, u32[]{:S(2)}, u32[]{:S(2)}) %collective-permute-start.9) | collective-permute-done | bytes 524320 | tf_op jit(solution)/shard_map/ppermute | solution.py:149
  301.9 0.2 bitcast_add_fusion.2
  302.1 0.3 collective-permute-start.10
  302.6 3.3 collective-permute-start.5
  305.9 0.8 collective-permute-start.4
  306.8 0.3 collective-permute-start.3
  307.0 1.5 collective-permute-done.10
  308.7 3.3 collective-permute-start.13
  312.0 0.8 collective-permute-start.12
  312.8 0.3 collective-permute-start.11
  313.1 0.7 collective-permute-done.4
  313.9 1.2 collective-permute-start.6
  315.1 2.0 collective-permute-done.12
  317.2 1.7 collective-permute-done.11
  319.0 0.3 collective-permute-start.14
  319.6 4.4 %collective-permute-done.14 = f32[32,1024]{1,0:T(8,128)S(1)} collective-permute-done((f32[32,1024]{1,0:T(8,128)S(1)}, f32[32,1024]{1,0:T(8,128)S(1)}, u32[]{:S(2)}, u32[]{:S(2)}) %collective-permute-start.14) | collective-permute-done | bytes 131104 | tf_op jit(solution)/shard_map/ppermute | solution.py:158
  324.2 1.4 collective-permute-done.15
  325.7 0.8 copy-done.9
  (70 shorter events, 1.1 us)
Async XLA Ops:
  13.3 5.3 %copy-start.12 = (s32[1,32]{1,0:T(1,128)S(1)}, s32[1,32]{1,0:T(1,128)}, u32[]{:S(2)}) copy-start(s32[1,32]{1,0:T(1,128)} %param.18) | copy-start | bytes 388
  26.4 8.4 %copy-start.11 = (bf16[128]{0:T(256)(128)(2,1)S(1)}, bf16[128]{0:T(256)(128)(2,1)}, u32[]{:S(2)}) copy-start(bf16[128]{0:T(256)(128)(2,1)} %param.24) | copy-start | bytes 772
  26.4 118.3 %all-to-all-start = ((bf16[32,4,128,128]{3,2,1,0:T(8,128)(2,1)}), bf16[32,4,128,128]{3,2,1,0:T(8,128)(2,1)}, u32[]{:S(2)}, u32[]{:S(2)}) async-start(bf16[32,4,128,128]{3,2,1,0:T(8,128)(2,1)} %get-tuple-element.24), calls=%async_computation | async-start | bytes 8388608 | tf_op jit(solution)/shard_map/all_to_all | solution.py:218
  33.8 114.5 %all-gather.5.cloned.1.call-start = ((), (), s32[]{:S(2)}) async-start(), calls=%async_computation.2 | async-start | bytes 1474560 | tf_op jit(solution)/shard_map/all_gather | solution.py:235
  144.7 105.8 %all-to-all-start.1 = ((bf16[32,4,128,128]{3,2,1,0:T(8,128)(2,1)}), bf16[32,4,128,128]{3,2,1,0:T(8,128)(2,1)}, u32[]{:S(2)}, u32[]{:S(2)}) async-start(bf16[32,4,128,128]{3,2,1,0:T(8,128)(2,1)} %get-tuple-element.23), calls=%async_computation.1 | async-start | bytes 8388608 | tf_op jit(solution)/shard_map/all_to_all | solution.py:218
  148.3 70.4 %all-gather.7.cloned.1.call-start = ((), (), s32[]{:S(2)}) async-start(), calls=%async_computation.3 | async-start | bytes 5242880 | tf_op jit(solution)/shard_map/all_gather | solution.py:237
  224.3 4.9 %copy-start.3 = (bf16[4,6,128,128]{3,2,1,0:T(8,128)(2,1)S(1)}, bf16[4,6,128,128]{3,2,1,0:T(8,128)(2,1)}, u32[]{:S(2)}) copy-start(bf16[4,6,128,128]{3,2,1,0:T(8,128)(2,1)} %tiles_ref.5) | copy-start | bytes 2359300
  224.3 4.9 %copy-start.4 = (s32[4,6]{1,0:T(4,128)S(1)}, s32[4,6]{1,0:T(4,128)}, u32[]{:S(2)}) copy-start(s32[4,6]{1,0:T(4,128)} %src_ref.5) | copy-start | bytes 292
  224.3 4.9 %copy-start.5 = (s32[4]{0:T(128)S(1)}, s32[4]{0:T(128)}, u32[]{:S(2)}) copy-start(s32[4]{0:T(128)} %cnt_ref.5) | copy-start | bytes 52
  227.3 2.0 copy-start.1
  229.2 5.4 %copy-start = (bf16[4,1024,128]{2,1,0:T(8,128)(2,1)S(1)}, bf16[4,1024,128]{2,1,0:T(8,128)(2,1)}, u32[]{:S(2)}) copy-start(bf16[4,1024,128]{2,1,0:T(8,128)(2,1)} %own_ref.1) | copy-start | bytes 3145732
  233.3 1.3 copy-start.7
  250.1 27.4 %collective-permute-start = (bf16[4,2,2,32,1024]{4,3,2,1,0:T(8,128)(2,1)S(1)}, bf16[4,2,2,32,1024]{4,3,2,1,0:T(8,128)(2,1)S(1)}, u32[]{:S(2)}, u32[]{:S(2)}) collective-permute-start(bf16[4,2,2,32,1024]{4,3,2,1,0:T(8,128)(2,1)S(1)} %fusion), channel_id=1, source_target_pairs={{0,8},{8,0},{16,24},{24,16},{1,9},{9,1},{17,25},{25,17},{2,10},{10... | collective-permute-start | bytes 3145736 | tf_op jit(solution)/shard_map/ppermute | solution.py:149
  250.4 1.2 copy-start.2
  251.7 1.2 copy-start.6
  265.0 14.6 %collective-permute-start.8 = (bf16[4,2,2,32,1024]{4,3,2,1,0:T(8,128)(2,1)S(1)}, bf16[4,2,2,32,1024]{4,3,2,1,0:T(8,128)(2,1)}, u32[]{:S(2)}, u32[]{:S(2)}) collective-permute-start(bf16[4,2,2,32,1024]{4,3,2,1,0:T(8,128)(2,1)S(1)} %fusion.1), channel_id=1, source_target_pairs={{0,8},{8,0},{16,24},{24,16},{1,9},{9,1},{17,25},{25,17},{2,10},{10... | collective-permute-start | bytes 3145736 | tf_op jit(solution)/shard_map/ppermute | solution.py:149
  265.1 2.3 collective-permute-start.16
  267.3 3.6 %collective-permute-start.17 = (f32[1024]{0:T(1024)S(1)}, f32[1024]{0:T(1024)S(1)}, u32[]{:S(2)}, u32[]{:S(2)}) collective-permute-start(f32[1024]{0:T(1024)S(1)} %add.231), channel_id=1, source_target_pairs={{0,1},{1,0},{2,3},{3,2},{4,5},{5,4},{6,7},{7,6},{8,9},{9,8},{10,11... | collective-permute-start | bytes 12296 | tf_op jit(solution)/shard_map/ppermute | solution.py:166
  271.0 3.6 %collective-permute-start.18 = (f32[1024]{0:T(1024)S(1)}, f32[1024]{0:T(1024)S(1)}, u32[]{:S(2)}, u32[]{:S(2)}) collective-permute-start(f32[1024]{0:T(1024)S(1)} %add.232), channel_id=1, source_target_pairs={{0,16},{8,24},{16,0},{24,8},{1,17},{9,25},{17,1},{25,9},{2,18},{10... | collective-permute-start | bytes 12296 | tf_op jit(solution)/shard_map/ppermute | solution.py:166
  271.3 8.3 %copy-start.8 = (f32[1024,1024]{1,0:T(8,128)S(1)}, f32[1024,1024]{1,0:T(8,128)}, u32[]{:S(2)}) copy-start(f32[1024,1024]{1,0:T(8,128)} %second_layer.1) | copy-start | bytes 12582916
  274.6 8.9 %collective-permute-start.21 = (f32[1024]{0:T(1024)S(1)}, f32[1024]{0:T(1024)S(1)}, u32[]{:S(2)}, u32[]{:S(2)}) collective-permute-start(f32[1024]{0:T(1024)S(1)} %add.233), channel_id=1, source_target_pairs={{0,6},{1,7},{2,0},{3,1},{4,2},{5,3},{6,4},{7,5},{8,14},{9,15},{10,... | collective-permute-start | bytes 12296 | tf_op jit(solution)/shard_map/ppermute | solution.py:166
  276.9 6.5 %collective-permute-start.20 = (f32[1024]{0:T(1024)S(1)}, f32[1024]{0:T(1024)S(1)}, u32[]{:S(2)}, u32[]{:S(2)}) collective-permute-start(f32[1024]{0:T(1024)S(1)} %add.233), channel_id=1, source_target_pairs={{0,4},{1,5},{2,6},{3,7},{4,0},{5,1},{6,2},{7,3},{8,12},{9,13},{10,... | collective-permute-start | bytes 12296 | tf_op jit(solution)/shard_map/ppermute | solution.py:166
  276.9 6.5 %collective-permute-start.19 = (f32[1024]{0:T(1024)S(1)}, f32[1024]{0:T(1024)S(1)}, u32[]{:S(2)}, u32[]{:S(2)}) collective-permute-start(f32[1024]{0:T(1024)S(1)} %add.233), channel_id=1, source_target_pairs={{0,2},{1,3},{2,4},{3,5},{4,6},{5,7},{6,0},{7,1},{8,10},{9,11},{10,... | collective-permute-start | bytes 12296 | tf_op jit(solution)/shard_map/ppermute | solution.py:166
  279.5 14.9 %collective-permute-start.1 = (bf16[4,2,32,1024]{3,2,1,0:T(8,128)(2,1)S(1)}, bf16[4,2,32,1024]{3,2,1,0:T(8,128)(2,1)S(1)}, u32[]{:S(2)}, u32[]{:S(2)}) collective-permute-start(bf16[4,2,32,1024]{3,2,1,0:T(8,128)(2,1)S(1)} %fusion.2), channel_id=1, source_target_pairs={{0,1},{1,0},{2,3},{3,2},{4,5},{5,4},{6,7},{7,6},{8,9},{9,8},{10,11... | collective-permute-start | bytes 1572872 | tf_op jit(solution)/shard_map/ppermute | solution.py:149
  281.4 20.5 %collective-permute-start.9 = (bf16[4,2,32,1024]{3,2,1,0:T(8,128)(2,1)S(1)}, bf16[4,2,32,1024]{3,2,1,0:T(8,128)(2,1)S(1)}, u32[]{:S(2)}, u32[]{:S(2)}) collective-permute-start(bf16[4,2,32,1024]{3,2,1,0:T(8,128)(2,1)S(1)} %fusion.3), channel_id=1, source_target_pairs={{0,1},{1,0},{2,3},{3,2},{4,5},{5,4},{6,7},{7,6},{8,9},{9,8},{10,11... | collective-permute-start | bytes 1572872 | tf_op jit(solution)/shard_map/ppermute | solution.py:149
  294.6 7.9 %collective-permute-start.2 = (bf16[4,32,1024]{2,1,0:T(8,128)(2,1)S(1)}, bf16[4,32,1024]{2,1,0:T(8,128)(2,1)S(1)}, u32[]{:S(2)}, u32[]{:S(2)}) collective-permute-start(bf16[4,32,1024]{2,1,0:T(8,128)(2,1)S(1)} %fusion.5), channel_id=1, source_target_pairs={{0,16},{8,24},{16,0},{24,8},{1,17},{9,25},{17,1},{25,9},{2,18},{10... | collective-permute-start | bytes 786440 | tf_op jit(solution)/shard_map/ppermute | solution.py:149
  302.1 6.4 %collective-permute-start.10 = (bf16[4,32,1024]{2,1,0:T(8,128)(2,1)S(1)}, bf16[4,32,1024]{2,1,0:T(8,128)(2,1)S(1)}, u32[]{:S(2)}, u32[]{:S(2)}) collective-permute-start(bf16[4,32,1024]{2,1,0:T(8,128)(2,1)S(1)} %fusion.6), channel_id=1, source_target_pairs={{0,16},{8,24},{16,0},{24,8},{1,17},{9,25},{17,1},{25,9},{2,18},{10... | collective-permute-start | bytes 786440 | tf_op jit(solution)/shard_map/ppermute | solution.py:149
  302.6 10.2 %collective-permute-start.5 = (bf16[32,1024]{1,0:T(8,128)(2,1)S(1)}, bf16[32,1024]{1,0:T(8,128)(2,1)S(1)}, u32[]{:S(2)}, u32[]{:S(2)}) collective-permute-start(bf16[32,1024]{1,0:T(8,128)(2,1)S(1)} %get-tuple-element.21), channel_id=1, source_target_pairs={{0,6},{1,7},{2,0},{3,1},{4,2},{5,3},{6,4},{7,5},{8,14},{9,15},{10,... | collective-permute-start | bytes 196616 | tf_op jit(solution)/shard_map/ppermute | solution.py:149
  305.9 7.9 %collective-permute-start.4 = (bf16[32,1024]{1,0:T(8,128)(2,1)S(1)}, bf16[32,1024]{1,0:T(8,128)(2,1)S(1)}, u32[]{:S(2)}, u32[]{:S(2)}) collective-permute-start(bf16[32,1024]{1,0:T(8,128)(2,1)S(1)} %get-tuple-element.22), channel_id=1, source_target_pairs={{0,4},{1,5},{2,6},{3,7},{4,0},{5,1},{6,2},{7,3},{8,12},{9,13},{10,... | collective-permute-start | bytes 196616 | tf_op jit(solution)/shard_map/ppermute | solution.py:149
  306.8 7.1 %collective-permute-start.3 = (bf16[32,1024]{1,0:T(8,128)(2,1)S(1)}, bf16[32,1024]{1,0:T(8,128)(2,1)S(1)}, u32[]{:S(2)}, u32[]{:S(2)}) collective-permute-start(bf16[32,1024]{1,0:T(8,128)(2,1)S(1)} %get-tuple-element.20), channel_id=1, source_target_pairs={{0,2},{1,3},{2,4},{3,5},{4,6},{5,7},{6,0},{7,1},{8,10},{9,11},{10,... | collective-permute-start | bytes 196616 | tf_op jit(solution)/shard_map/ppermute | solution.py:149
  308.7 6.4 %collective-permute-start.13 = (bf16[32,1024]{1,0:T(8,128)(2,1)S(1)}, bf16[32,1024]{1,0:T(8,128)(2,1)S(1)}, u32[]{:S(2)}, u32[]{:S(2)}) collective-permute-start(bf16[32,1024]{1,0:T(8,128)(2,1)S(1)} %get-tuple-element.18), channel_id=1, source_target_pairs={{0,6},{1,7},{2,0},{3,1},{4,2},{5,3},{6,4},{7,5},{8,14},{9,15},{10,... | collective-permute-start | bytes 196616 | tf_op jit(solution)/shard_map/ppermute | solution.py:149
  312.0 5.2 %collective-permute-start.12 = (bf16[32,1024]{1,0:T(8,128)(2,1)S(1)}, bf16[32,1024]{1,0:T(8,128)(2,1)S(1)}, u32[]{:S(2)}, u32[]{:S(2)}) collective-permute-start(bf16[32,1024]{1,0:T(8,128)(2,1)S(1)} %get-tuple-element.19), channel_id=1, source_target_pairs={{0,4},{1,5},{2,6},{3,7},{4,0},{5,1},{6,2},{7,3},{8,12},{9,13},{10,... | collective-permute-start | bytes 196616 | tf_op jit(solution)/shard_map/ppermute | solution.py:149
  312.8 6.1 %collective-permute-start.11 = (bf16[32,1024]{1,0:T(8,128)(2,1)S(1)}, bf16[32,1024]{1,0:T(8,128)(2,1)S(1)}, u32[]{:S(2)}, u32[]{:S(2)}) collective-permute-start(bf16[32,1024]{1,0:T(8,128)(2,1)S(1)} %get-tuple-element.17), channel_id=1, source_target_pairs={{0,2},{1,3},{2,4},{3,5},{4,6},{5,7},{6,0},{7,1},{8,10},{9,11},{10,... | collective-permute-start | bytes 196616 | tf_op jit(solution)/shard_map/ppermute | solution.py:149
  313.9 5.5 %collective-permute-start.6 = (f32[32,1024]{1,0:T(8,128)S(1)}, f32[32,1024]{1,0:T(8,128)S(1)}, u32[]{:S(2)}, u32[]{:S(2)}) collective-permute-start(f32[32,1024]{1,0:T(8,128)S(1)} %get-tuple-element.14), channel_id=1, source_target_pairs={{0,16},{8,24},{16,0},{24,8},{1,17},{9,25},{17,1},{25,9},{2,18},{10... | collective-permute-start | bytes 393224 | tf_op jit(solution)/shard_map/ppermute | solution.py:158
  319.0 5.0 %collective-permute-start.14 = (f32[32,1024]{1,0:T(8,128)S(1)}, f32[32,1024]{1,0:T(8,128)S(1)}, u32[]{:S(2)}, u32[]{:S(2)}) collective-permute-start(f32[32,1024]{1,0:T(8,128)S(1)} %get-tuple-element.12), channel_id=1, source_target_pairs={{0,16},{8,24},{16,0},{24,8},{1,17},{9,25},{17,1},{25,9},{2,18},{10... | collective-permute-start | bytes 393224 | tf_op jit(solution)/shard_map/ppermute | solution.py:158
  319.4 4.8 %collective-permute-start.7 = (f32[2,32,1024]{2,1,0:T(8,128)S(1)}, f32[2,32,1024]{2,1,0:T(8,128)S(1)}, u32[]{:S(2)}, u32[]{:S(2)}) collective-permute-start(f32[2,32,1024]{2,1,0:T(8,128)S(1)} %bitcast_dynamic-update-slice_fusion.6), channel_id=1, source_target_pairs={{0,8},{8,0},{16,24},{24,16},{1,9},{9,1},{17,25},{25,17},{2,10},{10... | collective-permute-start | bytes 786440 | tf_op jit(solution)/shard_map/ppermute | solution.py:158
  324.0 1.6 collective-permute-start.15
  324.2 1.4 copy-start.10
  325.7 0.8 copy-start.9
Sparse Core Ops, SparseCore 0:
  37.4 74.4 all-gather.4
  151.2 67.3 all-gather.6

commit v2 on v1

--- a/solution.py
+++ b/solution.py
@@ -211,15 +211,14 @@
     requesters, cap = chosen.shape
     live = lax.broadcasted_iota(jnp.int32, chosen.shape, 1) < pull_count[0][:, None]
 
-    def pull(table):
+    def picked(table):
         taken = jnp.take(table, chosen.reshape(-1), axis=0)
         taken = taken.reshape(chosen.shape + table.shape[1:])
-        sent = jnp.where(live[:, :, None, None], taken, jnp.zeros((), table.dtype))
+        return jnp.where(live[:, :, None, None], taken, jnp.zeros((), table.dtype))
+
+    def pull(sent):
         got = lax.all_to_all(sent, ("dom", "fsdp"), split_axis=0, concat_axis=0, tiled=True)
-        return got.reshape(dom_size, fsdp_size, cap, table.shape[1], block)
-
-    arrived_first = pull(history_first)
-    arrived_second = pull(history_second)
+        return got.reshape(dom_size, fsdp_size, cap, sent.shape[2], block)
 
     rows = w_first.shape[0]
     share = rows // dom_size
@@ -233,6 +232,10 @@
         0,
     )
     along = lax.all_gather(payload, "fsdp", axis=0)
+    sent_first, sent_second, along = lax.optimization_barrier(
+        (picked(history_first), picked(history_second), along)
+    )
+    arrived_first = pull(sent_first)
     bias_full = along[:, 2 * share, : bias_first.shape[0]].reshape(hidden_width)
     both = lax.all_gather(along[:, : 2 * share], "dom", axis=0)
     both = both.reshape(dom_size, fsdp_size, 2, share, hidden_width)
@@ -255,6 +258,10 @@
         ],
         2 * mat,
     )
+    sent_second, arrived_first, first_turned, back_hidden = lax.optimization_barrier(
+        (sent_second, arrived_first, first_turned, back_hidden)
+    )
+    arrived_second = pull(sent_second)
     hidden_new, first_term, bias_rows = local_call(
         first_kernel,
         "first_layer",
@@ -279,11 +286,24 @@
         ],
         4 * mat,
     )
+    def near_sum(term):
+        terms = term.reshape(z_size, x_size, y_size, cores, share, hidden_width)
+        terms = scatter_sum(terms, 3, core_hop, core, cores)
+        terms = scatter_sum(terms, 1, x_hop, x, x_size)
+        return scatter_sum(terms, 1, y_hop, y, y_size)
+
+    first_near = near_sum(first_term)
+    bias_sum = sum_all(bias_rows[0], core_hop, cores)
+    bias_sum = sum_all(bias_sum, x_hop, x_size)
+    bias_sum = sum_all(bias_sum, y_hop, y_size)
+    hidden_held, arrived_second, first_near, bias_sum = lax.optimization_barrier(
+        (hidden_new, arrived_second, first_near, bias_sum)
+    )
     second_term = local_call(
         second_kernel,
         "second_layer",
         scalars,
-        (hidden_new, arrived_second, tile_values, out_grad),
+        (hidden_held, arrived_second, tile_values, out_grad),
         jax.ShapeDtypeStruct((hidden_width, hidden_width), F32),
         [
             pltpu.VMEM((hidden_width, block), F32),
@@ -292,24 +312,16 @@
         ],
         3 * mat,
     )
-
-    def total(term):
-        terms = term.reshape(z_size, x_size, y_size, cores, share, hidden_width)
-        terms = scatter_sum(terms, 3, core_hop, core, cores)
-        terms = scatter_sum(terms, 1, x_hop, x, x_size)
-        terms = scatter_sum(terms, 1, y_hop, y, y_size)
-        piece = scatter_sum(terms, 0, z_hop, z, z_size)
-        pieces = gather_all(piece, y_hop, y, y_size)
-        pieces = gather_all(pieces, core_hop, core, cores)
-        return pieces.transpose(1, 0, 2, 3).reshape(rows, hidden_width)
-
-    bias_sum = sum_all(bias_rows[0], core_hop, cores)
-    bias_sum = sum_all(bias_sum, x_hop, x_size)
-    bias_sum = sum_all(bias_sum, y_hop, y_size)
+    near = jnp.stack([first_near, near_sum(second_term)], 1)
+    piece = scatter_sum(near, 0, z_hop, z, z_size)
+    pieces = gather_all(piece, y_hop, y, y_size)
+    pieces = gather_all(pieces, core_hop, core, cores)
+    totals = pieces.transpose(2, 1, 0, 3, 4).reshape(2, rows, hidden_width)
+
     bias_sum = sum_all(bias_sum, z_hop, z_size)
     bias_len = bias_first.shape[0]
     bias_total = lax.dynamic_slice_in_dim(bias_sum, fsdp_index * bias_len, bias_len, 0)
-    return (hidden_new, total(first_term), total(second_term), bias_total)
+    return (hidden_new, totals[0], totals[1], bias_total)
 
 
 def solution(mesh):

time: 334 us -> 328 us (0.982)
  waiting for transfers between devices: 214 us -> 206 us
  other arithmetic: 13.3 us -> 17.1 us
  Pallas kernels: 28.1 us -> 24.6 us
    all_to_all x2, waiting for transfers between devices: 109 us -> 34.6 us  [pull(): lax.all_to_all(sent, ('dom', 'fsdp'), split_axis=0, concat_axis=0, tiled=...]
    ppermute x12 -> x9, waiting for transfers between devices: 23.6 us -> 61.9 us  [scatter_sum(): mine = mine + hop(k)(theirs.astype(BF16)).astype(F32)]
    all_gather x1, waiting for transfers between devices: 0.02 us -> 26.8 us  [on_device(): along = lax.all_gather(payload, 'fsdp', axis=0)]
    ppermute x6, starting transfers between devices: 3.75 us -> 8.58 us  [sum_all(): total = total + hop(k)(vector)]
    all_to_all x2, starting transfers between devices: 11 us -> 7.42 us  [pull(): lax.all_to_all(sent, ('dom', 'fsdp'), split_axis=0, concat_axis=0, tiled=...]
    pallas_call x3, Pallas kernels: 28.1 us -> 24.6 us  [local_call(): pl.pallas_call(kernel, name=name, out_shape=out_shape, in_specs=in_specs,...]
    add x6 -> x5, other arithmetic: 4.03 us -> 7 us  [scatter_sum(): mine = mine + hop(k)(theirs.astype(BF16)).astype(F32)]
    ppermute x12 -> x9, starting transfers between devices: 11.8 us -> 12.1 us  [scatter_sum(): mine = mine + hop(k)(theirs.astype(BF16)).astype(F32)]
  transfers between devices with their start and end apart: 26 -> 21, of which waited for: 14 -> 17; matrix products, arithmetic and copies ran while one was open for 7% -> 12% of each run, Pallas kernels for 8% -> 5%
where the time goes in v2:
time: 328 us; the launch traced here: 327 us
  waiting for transfers between devices  206 us (63%)
  local copies, waits for them, and re-layouts  34.6 us (11%)
  starting transfers between devices  30 us (9%)
  Pallas kernels  24.6 us (8%)
  other arithmetic  17.1 us (5%)
  between operations  14.4 us (4%)
    all_gather x1, waiting for transfers between devices, on_device(): both = lax.all_gather(along[:, :2 * share], 'dom', axis=0)  69.2 us
    ppermute x9, waiting for transfers between devices, scatter_sum(): mine = mine + hop(k)(theirs.astype(BF16)).astype(F32)  61.9 us
    all_to_all x2, waiting for transfers between devices, pull(): lax.all_to_all(sent, ('dom', 'fsdp'), split_axis=0, concat_axis=0, tiled=...  34.6 us
    all_gather x1, waiting for transfers between devices, on_device(): along = lax.all_gather(payload, 'fsdp', axis=0)  26.8 us
    pallas_call x3, Pallas kernels, local_call(): pl.pallas_call(kernel, name=name, out_shape=out_shape, in_specs=in_specs,...  24.6 us
    ppermute x9, starting transfers between devices, scatter_sum(): mine = mine + hop(k)(theirs.astype(BF16)).astype(F32)  12.1 us
    gather x2, local copies, waits for them, and re-layouts, picked(): taken = jnp.take(table, chosen.reshape(-1), axis=0)  10.6 us
    ppermute x6, waiting for transfers between devices, sum_all(): total = total + hop(k)(vector)  9.02 us
  transfers between devices with their start and end apart: 21, of which 17 were waited for; matrix products, arithmetic and copies ran while one was open for 12% of the time, Pallas kernels for 5%

profile of v2, /device:TPU:0, one launch (start us, length us, event | category | flops | bytes accessed | tf_op | source)
XLA Modules:
  0.0 326.9 jit_solution(12676387706584380582)
XLA Ops:
  7.2 0.9 constant_dynamic-slice_fusion.2
  8.1 1.3 fusion.21
  9.5 0.8 copy.51
  10.2 0.1 reshape_squeeze.2
  10.4 5.3 %gather_fusion = bf16[128,128,128]{2,1,0:T(8,128)(2,1)} fusion(bf16[128,128,128]{2,1,0:T(8,128)(2,1)} %param.15, s32[1024]{0:T(1024)S(1)} %pad_clamp_fusion), kind=kCustom, calls=%fused_computation.clone | custom fusion | bytes 8389120 | tf_op jit(solution)/shard_map/jit(_take)/gather | solution.py:215
  15.7 5.3 %gather_fusion.1 = bf16[128,128,128]{2,1,0:T(8,128)(2,1)} fusion(bf16[128,128,128]{2,1,0:T(8,128)(2,1)} %param.16, s32[1024]{0:T(1024)S(1)} %pad_clamp_fusion), kind=kCustom, calls=%fused_computation.1.clone | custom fusion | bytes 8389120 | tf_op jit(solution)/shard_map/jit(_take)/gather | solution.py:215
  20.9 0.1 iota_compare_fusion.1
  21.0 4.1 %broadcast_select_fusion = (bf16[128,128,128]{2,1,0:T(8,128)(2,1)S(1)}, bf16[128,128,128]{2,1,0:T(8,128)(2,1)S(1)}) fusion(bf16[128,128,128]{2,1,0:T(8,128)(2,1)} %gather_fusion.1, pred[128]{0:T(512)(128)(4,1)S(1)} %compare_and_fusion, bf16[128,128,128]{2,1,0:T(8,128)(2,1)} %gather_fusion), kind=kLoop, calls=%fused_computation.2 | loop fusion | flops 4194304 | bytes 16777344 | tf_op jit(solution)/shard_map/jit(_take)/select_n | solution.py:215
  25.1 3.7 %broadcast_select_fusion.2 = (bf16[32,4,128,128]{3,2,1,0:T(8,128)(2,1)}, bf16[32,4,128,128]{3,2,1,0:T(8,128)(2,1)}) fusion(bf16[32,4,128,128]{3,2,1,0:T(8,128)(2,1)S(1)} %bitcast.94, pred[32,4]{1,0:T(8,128)(4,1)S(1)} %iota_compare_fusion.1, bf16[32,4,128,128]{3,2,1,0:T(8,128)(2,1)S(1)} %bitcast.95), kind=kLoop, calls=%fused_computation.4 | loop fusion | flops 4194304 | bytes 16777344 | tf_op jit(solution)/shard_map/jit(_where)/select_n | solution.py:217
  28.8 26.8 %all-gather.5.cloned.1.call-done = bf16[640,1024]{1,0:T(8,128)(2,1)} async-done(((bf16[80,1024]{1,0:T(8,128)(2,1)}), bf16[640,1024]{1,0:T(8,128)(2,1)}) %all-gather.5.cloned.1.call-update) | async-done | bytes 1310736 | tf_op jit(solution)/shard_map/all_gather | solution.py:234
  55.5 3.7 %all-to-all-start = ((bf16[32,4,128,128]{3,2,1,0:T(8,128)(2,1)}), bf16[32,4,128,128]{3,2,1,0:T(8,128)(2,1)}, u32[]{:S(2)}, u32[]{:S(2)}) async-start(bf16[32,4,128,128]{3,2,1,0:T(8,128)(2,1)} %get-tuple-element.20), calls=%async_computation | async-start | bytes 8388608 | tf_op jit(solution)/shard_map/all_to_all | solution.py:220
  59.3 1.1 slice.25
  60.4 69.2 %all-gather.7.cloned.1.call-done = bf16[32,64,1024]{2,1,0:T(8,128)(2,1)} async-done(((bf16[8,64,1024]{2,1,0:T(8,128)(2,1)}), bf16[32,64,1024]{2,1,0:T(8,128)(2,1)}) %all-gather.7.cloned.1.call-update) | async-done | bytes 4194320 | tf_op jit(solution)/shard_map/all_gather | solution.py:240
  129.6 4.2 %fusion.26 = (bf16[1,8,4,32,1024]{4,3,0,1,2:T(8,128)(2,1)}, bf16[1,8,4,32,1024]{4,3,0,1,2:T(8,128)(2,1)S(1)}) fusion(bf16[2,8,4,32,1024]{4,3,0,1,2:T(8,128)(2,1)} %bitcast.99), kind=kLoop, calls=%fused_computation.66 | loop fusion | bytes 8388608 | tf_op jit(solution)/shard_map/slice | solution.py:244
  133.8 1.5 copy.52
  135.3 2.9 copy.53
  138.3 1.8 copy.54
  140.2 3.7 %back_to_hidden.1.back_ref = f32[4,1024,128]{2,1,0:T(8,128)S(1)} custom-call(s32[4,6]{1,0:T(4,128)S(1)} %copy-done.5, s32[4]{0:T(128)S(1)} %copy-done.6, bf16[1024,1024]{1,0:T(8,128)(2,1)S(1)} %bitcast.93, bf16[4,1024,128]{2,1,0:T(8,128)(2,1)S(1)} %copy-done.1, bf16[4,6,128,128]{3,2,1,0:T(8,128)(2,1)S(1)} %copy-done.3), custom_call_target="tpu_custom_call" | custom-call | flops 2147483648 | bytes 7864320 | tf_op jit(solution)/shard_map/back_to_hidden/pallas_call | solution.py:125
  143.9 1.3 copy-done.8
  145.2 9.3 %all-to-all-done = bf16[32,4,128,128]{3,2,1,0:T(8,128)(2,1)} async-done(((bf16[32,4,128,128]{3,2,1,0:T(8,128)(2,1)}), bf16[32,4,128,128]{3,2,1,0:T(8,128)(2,1)}, u32[]{:S(2)}, u32[]{:S(2)}) %all-to-all-start) | async-done | bytes 4194336 | tf_op jit(solution)/shard_map/all_to_all | solution.py:220
  154.5 3.7 %all-to-all-start.1 = ((bf16[32,4,128,128]{3,2,1,0:T(8,128)(2,1)}), bf16[32,4,128,128]{3,2,1,0:T(8,128)(2,1)}, u32[]{:S(2)}, u32[]{:S(2)}) async-start(bf16[32,4,128,128]{3,2,1,0:T(8,128)(2,1)} %get-tuple-element.26), calls=%async_computation.1 | async-start | bytes 8388608 | tf_op jit(solution)/shard_map/all_to_all | solution.py:220
  158.2 0.7 bitcast_convert_fusion
  158.9 0.2 copy.55.bias_ref
  159.2 1.2 copy-done
  160.4 12.2 %first_layer.1 = (bf16[4,1024,128]{2,1,0:T(8,128)(2,1)}, f32[1024,1024]{1,0:T(8,128)}, f32[8,1024]{1,0:T(8,128)S(1)}) custom-call(s32[4,6]{1,0:T(4,128)S(1)} %copy-done.5, s32[4]{0:T(128)S(1)} %copy-done.6, bf16[4,1024,128]{2,1,0:T(8,128)(2,1)S(1)} %copy-done, bf16[4,8,4,128,128]{4,3,2,1,0:T(8,128)(2,1)} %bitcast.5.arr_ref, ...), custom_call_target="tpu_custom_call" | custom-call | flops 4294967296 | bytes 20455424 | tf_op jit(solution)/shard_map/first_layer/pallas_call | solution.py:125
  172.6 2.7 fusion.1
  175.3 0.5 collective-permute-start
  175.8 2.6 collective-permute-done
  178.5 2.2 bitcast_add_fusion.1
  180.7 1.3 copy-done.9
  182.1 3.1 collective-permute-start.1
  185.2 30.1 %collective-permute-done.1 = bf16[4,2,32,1024]{3,2,0,1:T(8,128)(2,1)} collective-permute-done((bf16[4,2,32,1024]{3,2,0,1:T(8,128)(2,1)S(1)}, bf16[4,2,32,1024]{3,2,0,1:T(8,128)(2,1)}, u32[]{:S(2)}, u32[]{:S(2)}) %collective-permute-start.1) | collective-permute-done | bytes 524320 | tf_op jit(solution)/shard_map/ppermute | solution.py:149
  215.3 1.5 bitcast_add_fusion.3
  216.9 1.4 collective-permute-start.2
  218.3 1.2 collective-permute-done.3
  219.5 3.6 %collective-permute-done.4 = f32[1024]{0:T(1024)S(1)} collective-permute-done((f32[1024]{0:T(1024)S(1)}, f32[1024]{0:T(1024)S(1)}, u32[]{:S(2)}, u32[]{:S(2)}) %collective-permute-start.4) | collective-permute-done | bytes 4128 | tf_op jit(solution)/shard_map/ppermute | solution.py:166
  223.1 0.8 collective-permute-start.5
  223.9 2.9 collective-permute-done.5
  226.8 1.2 bitcast_add_fusion.5
  228.0 25.3 %all-to-all-done.1 = bf16[32,4,128,128]{3,2,1,0:T(8,128)(2,1)} async-done(((bf16[32,4,128,128]{3,2,1,0:T(8,128)(2,1)}), bf16[32,4,128,128]{3,2,1,0:T(8,128)(2,1)}, u32[]{:S(2)}, u32[]{:S(2)}) %all-to-all-start.1) | async-done | bytes 4194336 | tf_op jit(solution)/shard_map/all_to_all | solution.py:220
  253.3 8.7 %second_layer.1 = f32[1024,1024]{1,0:T(8,128)} custom-call(s32[4,6]{1,0:T(4,128)S(1)} %copy-done.5, s32[4]{0:T(128)S(1)} %copy-done.6, bf16[4,1024,128]{2,1,0:T(8,128)(2,1)S(1)} %copy-done.7, bf16[4,8,4,128,128]{4,3,2,1,0:T(8,128)(2,1)} %bitcast.13.arr_ref, bf16[4,6,128,128]{3,2,1,0:T(8,128)(2,1)S(1)} %copy-done.4, bf16[4,1024,128]{2,1,0:T(8,128)(2,1)S(1)} %copy-done.2), custom_call_target="tpu_custom_call" | custom-call | flops 3221225472 | bytes 14155776 | tf_op jit(solution)/shard_map/second_layer/pallas_call | solution.py:125
  262.0 1.7 fusion
  263.8 0.2 collective-permute-start.6
  264.0 2.5 collective-permute-done.6
  266.5 1.9 bitcast_add_fusion
  268.5 0.1 fusion.3
  268.5 1.6 collective-permute-start.7
  270.2 12.4 %collective-permute-done.7 = bf16[4,2,32,1024]{3,2,1,0:T(8,128)(2,1)S(1)} collective-permute-done((bf16[4,2,32,1024]{3,2,1,0:T(8,128)(2,1)S(1)}, bf16[4,2,32,1024]{3,2,1,0:T(8,128)(2,1)S(1)}, u32[]{:S(2)}, u32[]{:S(2)}) %collective-permute-start.7) | collective-permute-done | bytes 524320 | tf_op jit(solution)/shard_map/ppermute | solution.py:149
  282.6 0.2 bitcast_add_fusion.2
  282.8 3.1 collective-permute-start.8
  285.8 6.0 %collective-permute-done.8 = bf16[4,32,1024]{2,1,0:T(8,128)(2,1)S(1)} collective-permute-done((bf16[4,32,1024]{2,1,0:T(8,128)(2,1)S(1)}, bf16[4,32,1024]{2,1,0:T(8,128)(2,1)S(1)}, u32[]{:S(2)}, u32[]{:S(2)}) %collective-permute-start.8) | collective-permute-done | bytes 262176 | tf_op jit(solution)/shard_map/ppermute | solution.py:149
  292.1 1.2 collective-permute-start.11
  293.3 0.9 collective-permute-start.9
  294.2 8.2 %collective-permute-done.10 = bf16[2,32,1024]{2,1,0:T(8,128)(2,1)S(1)} collective-permute-done((bf16[2,32,1024]{2,1,0:T(8,128)(2,1)S(1)}, bf16[2,32,1024]{2,1,0:T(8,128)(2,1)S(1)}, u32[]{:S(2)}, u32[]{:S(2)}) %collective-permute-start.10) | collective-permute-done | bytes 131104 | tf_op jit(solution)/shard_map/ppermute | solution.py:149
  302.5 1.7 collective-permute-start.12
  304.2 4.7 %collective-permute-done.12 = f32[2,32,1024]{2,1,0:T(8,128)S(1)} collective-permute-done((f32[2,32,1024]{2,1,0:T(8,128)S(1)}, f32[2,32,1024]{2,1,0:T(8,128)S(1)}, u32[]{:S(2)}, u32[]{:S(2)}) %collective-permute-start.12) | collective-permute-done | bytes 262176 | tf_op jit(solution)/shard_map/ppermute | solution.py:158
  309.0 3.9 %collective-permute-start.14 = (f32[1024]{0:T(1024)S(1)}, f32[1024]{0:T(1024)S(1)}, u32[]{:S(2)}, u32[]{:S(2)}) collective-permute-start(f32[1024]{0:T(1024)S(1)} %add.187), channel_id=1, source_target_pairs={{0,2},{1,3},{2,4},{3,5},{4,6},{5,7},{6,0},{7,1},{8,10},{9,11},{10,... | collective-permute-start | bytes 12296 | tf_op jit(solution)/shard_map/ppermute | solution.py:166
  312.9 1.0 collective-permute-start.15
  314.0 2.8 collective-permute-start.16
  316.8 0.6 collective-permute-done.15
  317.4 0.7 collective-permute-done.16
  318.1 0.6 dynamic_slice.79
  318.7 0.1 broadcast_in_dim.54
  318.9 1.1 fusion.27
  (54 shorter events, 0.9 us)
Async XLA Ops:
  7.2 48.4 %all-gather.5.cloned.1.call-start = ((), (), s32[]{:S(2)}) async-start(), calls=%async_computation.2 | async-start | bytes 1474560 | tf_op jit(solution)/shard_map/all_gather | solution.py:234
  15.7 5.3 %copy-start.12 = (s32[1,32]{1,0:T(1,128)S(1)}, s32[1,32]{1,0:T(1,128)}, u32[]{:S(2)}) copy-start(s32[1,32]{1,0:T(1,128)} %param.18) | copy-start | bytes 388
  55.5 3.8 %copy-start.11 = (bf16[640,1024]{1,0:T(8,128)(2,1)S(1)}, bf16[640,1024]{1,0:T(8,128)(2,1)}, u32[]{:S(2)}) copy-start(bf16[640,1024]{1,0:T(8,128)(2,1)} %all-gather.5.cloned.1.call-done) | copy-start | bytes 3932164
  55.5 98.9 %all-to-all-start = ((bf16[32,4,128,128]{3,2,1,0:T(8,128)(2,1)}), bf16[32,4,128,128]{3,2,1,0:T(8,128)(2,1)}, u32[]{:S(2)}, u32[]{:S(2)}) async-start(bf16[32,4,128,128]{3,2,1,0:T(8,128)(2,1)} %get-tuple-element.20), calls=%async_computation | async-start | bytes 8388608 | tf_op jit(solution)/shard_map/all_to_all | solution.py:220
  59.3 70.4 %all-gather.7.cloned.1.call-start = ((), (), s32[]{:S(2)}) async-start(), calls=%async_computation.3 | async-start | bytes 5242880 | tf_op jit(solution)/shard_map/all_gather | solution.py:240
  135.3 4.8 %copy-start.1 = (bf16[4,1024,128]{2,1,0:T(8,128)(2,1)S(1)}, bf16[4,1024,128]{2,1,0:T(8,128)(2,1)}, u32[]{:S(2)}) copy-start(bf16[4,1024,128]{2,1,0:T(8,128)(2,1)} %cot_ref.1) | copy-start | bytes 3145732
  135.3 4.8 %copy-start.5 = (s32[4,6]{1,0:T(4,128)S(1)}, s32[4,6]{1,0:T(4,128)}, u32[]{:S(2)}) copy-start(s32[4,6]{1,0:T(4,128)} %src_ref.5) | copy-start | bytes 292
  135.3 4.8 %copy-start.6 = (s32[4]{0:T(128)S(1)}, s32[4]{0:T(128)}, u32[]{:S(2)}) copy-start(s32[4]{0:T(128)} %cnt_ref.5) | copy-start | bytes 52
  138.3 1.9 copy-start.3
  143.8 1.3 copy-start.8
  154.5 4.7 %copy-start.4 = (bf16[4,6,128,128]{3,2,1,0:T(8,128)(2,1)S(1)}, bf16[4,6,128,128]{3,2,1,0:T(8,128)(2,1)}, u32[]{:S(2)}) copy-start(bf16[4,6,128,128]{3,2,1,0:T(8,128)(2,1)} %tiles_ref.5) | copy-start | bytes 2359300
  154.5 98.9 %all-to-all-start.1 = ((bf16[32,4,128,128]{3,2,1,0:T(8,128)(2,1)}), bf16[32,4,128,128]{3,2,1,0:T(8,128)(2,1)}, u32[]{:S(2)}, u32[]{:S(2)}) async-start(bf16[32,4,128,128]{3,2,1,0:T(8,128)(2,1)} %get-tuple-element.26), calls=%async_computation.1 | async-start | bytes 8388608 | tf_op jit(solution)/shard_map/all_to_all | solution.py:220
  159.2 1.2 copy-start
  175.3 3.1 collective-permute-start
  175.8 77.5 %copy-start.2 = (bf16[4,1024,128]{2,1,0:T(8,128)(2,1)S(1)}, bf16[4,1024,128]{2,1,0:T(8,128)(2,1)}, u32[]{:S(2)}) copy-start(bf16[4,1024,128]{2,1,0:T(8,128)(2,1)} %cot_ref.1) | copy-start | bytes 3145732
  175.8 77.5 %copy-start.7 = (bf16[4,1024,128]{2,1,0:T(8,128)(2,1)S(1)}, bf16[4,1024,128]{2,1,0:T(8,128)(2,1)}, u32[]{:S(2)}) copy-start(bf16[4,1024,128]{2,1,0:T(8,128)(2,1)} %get-tuple-element.30.own_ref) | copy-start | bytes 3145732
  180.7 1.3 copy-start.9
  182.1 33.2 %collective-permute-start.1 = (bf16[4,2,32,1024]{3,2,0,1:T(8,128)(2,1)S(1)}, bf16[4,2,32,1024]{3,2,0,1:T(8,128)(2,1)}, u32[]{:S(2)}, u32[]{:S(2)}) collective-permute-start(bf16[4,2,32,1024]{3,2,0,1:T(8,128)(2,1)S(1)} %fusion.2), channel_id=1, source_target_pairs={{0,1},{1,0},{2,3},{3,2},{4,5},{5,4},{6,7},{7,6},{8,9},{9,8},{10,11... | collective-permute-start | bytes 1572872 | tf_op jit(solution)/shard_map/ppermute | solution.py:149
  216.8 1.5 copy-start.10
  216.9 10.0 %collective-permute-start.2 = (bf16[4,32,1024]{2,1,0:T(8,128)(2,1)S(1)}, bf16[4,32,1024]{2,1,0:T(8,128)(2,1)}, u32[]{:S(2)}, u32[]{:S(2)}) collective-permute-start(bf16[4,32,1024]{2,1,0:T(8,128)(2,1)S(1)} %fusion.6), channel_id=1, source_target_pairs={{0,16},{8,24},{16,0},{24,8},{1,17},{9,25},{17,1},{25,9},{2,18},{10... | collective-permute-start | bytes 786440 | tf_op jit(solution)/shard_map/ppermute | solution.py:149
  218.3 1.2 collective-permute-start.3
  219.5 3.6 %collective-permute-start.4 = (f32[1024]{0:T(1024)S(1)}, f32[1024]{0:T(1024)S(1)}, u32[]{:S(2)}, u32[]{:S(2)}) collective-permute-start(f32[1024]{0:T(1024)S(1)} %add.185), channel_id=1, source_target_pairs={{0,1},{1,0},{2,3},{3,2},{4,5},{5,4},{6,7},{7,6},{8,9},{9,8},{10,11... | collective-permute-start | bytes 12296 | tf_op jit(solution)/shard_map/ppermute | solution.py:166
  223.1 3.8 %collective-permute-start.5 = (f32[1024]{0:T(1024)S(1)}, f32[1024]{0:T(1024)S(1)}, u32[]{:S(2)}, u32[]{:S(2)}) collective-permute-start(f32[1024]{0:T(1024)S(1)} %add.186), channel_id=1, source_target_pairs={{0,16},{8,24},{16,0},{24,8},{1,17},{9,25},{17,1},{25,9},{2,18},{10... | collective-permute-start | bytes 12296 | tf_op jit(solution)/shard_map/ppermute | solution.py:166
  263.8 2.7 collective-permute-start.6
  268.5 14.0 %collective-permute-start.7 = (bf16[4,2,32,1024]{3,2,1,0:T(8,128)(2,1)S(1)}, bf16[4,2,32,1024]{3,2,1,0:T(8,128)(2,1)S(1)}, u32[]{:S(2)}, u32[]{:S(2)}) collective-permute-start(bf16[4,2,32,1024]{3,2,1,0:T(8,128)(2,1)S(1)} %fusion.3), channel_id=1, source_target_pairs={{0,1},{1,0},{2,3},{3,2},{4,5},{5,4},{6,7},{7,6},{8,9},{9,8},{10,11... | collective-permute-start | bytes 1572872 | tf_op jit(solution)/shard_map/ppermute | solution.py:149
  282.8 9.1 %collective-permute-start.8 = (bf16[4,32,1024]{2,1,0:T(8,128)(2,1)S(1)}, bf16[4,32,1024]{2,1,0:T(8,128)(2,1)S(1)}, u32[]{:S(2)}, u32[]{:S(2)}) collective-permute-start(bf16[4,32,1024]{2,1,0:T(8,128)(2,1)S(1)} %fusion.7), channel_id=1, source_target_pairs={{0,16},{8,24},{16,0},{24,8},{1,17},{9,25},{17,1},{25,9},{2,18},{10... | collective-permute-start | bytes 786440 | tf_op jit(solution)/shard_map/ppermute | solution.py:149
  292.0 10.3 %collective-permute-start.10 = (bf16[2,32,1024]{2,1,0:T(8,128)(2,1)S(1)}, bf16[2,32,1024]{2,1,0:T(8,128)(2,1)S(1)}, u32[]{:S(2)}, u32[]{:S(2)}) collective-permute-start(bf16[2,32,1024]{2,1,0:T(8,128)(2,1)S(1)} %get-tuple-element.40), channel_id=1, source_target_pairs={{0,4},{1,5},{2,6},{3,7},{4,0},{5,1},{6,2},{7,3},{8,12},{9,13},{10,... | collective-permute-start | bytes 393224 | tf_op jit(solution)/shard_map/ppermute | solution.py:149
  292.1 10.3 %collective-permute-start.11 = (bf16[2,32,1024]{2,1,0:T(8,128)(2,1)S(1)}, bf16[2,32,1024]{2,1,0:T(8,128)(2,1)S(1)}, u32[]{:S(2)}, u32[]{:S(2)}) collective-permute-start(bf16[2,32,1024]{2,1,0:T(8,128)(2,1)S(1)} %get-tuple-element.41), channel_id=1, source_target_pairs={{0,6},{1,7},{2,0},{3,1},{4,2},{5,3},{6,4},{7,5},{8,14},{9,15},{10,... | collective-permute-start | bytes 393224 | tf_op jit(solution)/shard_map/ppermute | solution.py:149
  293.3 9.1 %collective-permute-start.9 = (bf16[2,32,1024]{2,1,0:T(8,128)(2,1)S(1)}, bf16[2,32,1024]{2,1,0:T(8,128)(2,1)S(1)}, u32[]{:S(2)}, u32[]{:S(2)}) collective-permute-start(bf16[2,32,1024]{2,1,0:T(8,128)(2,1)S(1)} %get-tuple-element.39), channel_id=1, source_target_pairs={{0,2},{1,3},{2,4},{3,5},{4,6},{5,7},{6,0},{7,1},{8,10},{9,11},{10,... | collective-permute-start | bytes 393224 | tf_op jit(solution)/shard_map/ppermute | solution.py:149
  302.5 6.4 %collective-permute-start.12 = (f32[2,32,1024]{2,1,0:T(8,128)S(1)}, f32[2,32,1024]{2,1,0:T(8,128)S(1)}, u32[]{:S(2)}, u32[]{:S(2)}) collective-permute-start(f32[2,32,1024]{2,1,0:T(8,128)S(1)} %get-tuple-element.34), channel_id=1, source_target_pairs={{0,16},{8,24},{16,0},{24,8},{1,17},{9,25},{17,1},{25,9},{2,18},{10... | collective-permute-start | bytes 786440 | tf_op jit(solution)/shard_map/ppermute | solution.py:158
  309.0 9.9 %collective-permute-start.13 = (f32[2,2,32,1024]{3,2,0,1:T(8,128)S(1)}, f32[2,2,32,1024]{3,2,0,1:T(8,128)S(1)}, u32[]{:S(2)}, u32[]{:S(2)}) collective-permute-start(f32[2,2,32,1024]{3,2,0,1:T(8,128)S(1)} %bitcast_dynamic-update-slice_fusion.2), channel_id=1, source_target_pairs={{0,8},{8,0},{16,24},{24,16},{1,9},{9,1},{17,25},{25,17},{2,10},{10... | collective-permute-start | bytes 1572872 | tf_op jit(solution)/shard_map/ppermute | solution.py:158
  309.0 7.7 %collective-permute-start.14 = (f32[1024]{0:T(1024)S(1)}, f32[1024]{0:T(1024)S(1)}, u32[]{:S(2)}, u32[]{:S(2)}) collective-permute-start(f32[1024]{0:T(1024)S(1)} %add.187), channel_id=1, source_target_pairs={{0,2},{1,3},{2,4},{3,5},{4,6},{5,7},{6,0},{7,1},{8,10},{9,11},{10,... | collective-permute-start | bytes 12296 | tf_op jit(solution)/shard_map/ppermute | solution.py:166
  312.9 4.5 %collective-permute-start.15 = (f32[1024]{0:T(1024)S(1)}, f32[1024]{0:T(1024)S(1)}, u32[]{:S(2)}, u32[]{:S(2)}) collective-permute-start(f32[1024]{0:T(1024)S(1)} %add.187), channel_id=1, source_target_pairs={{0,4},{1,5},{2,6},{3,7},{4,0},{5,1},{6,2},{7,3},{8,12},{9,13},{10,... | collective-permute-start | bytes 12296 | tf_op jit(solution)/shard_map/ppermute | solution.py:166
  314.0 4.2 %collective-permute-start.16 = (f32[1024]{0:T(1024)S(1)}, f32[1024]{0:T(1024)S(1)}, u32[]{:S(2)}, u32[]{:S(2)}) collective-permute-start(f32[1024]{0:T(1024)S(1)} %add.187), channel_id=1, source_target_pairs={{0,6},{1,7},{2,0},{3,1},{4,2},{5,3},{6,4},{7,5},{8,14},{9,15},{10,... | collective-permute-start | bytes 12296 | tf_op jit(solution)/shard_map/ppermute | solution.py:166
Sparse Core Ops, SparseCore 0:
  10.8 44.7 all-gather.4
  62.2 67.3 all-gather.6

commit v3 on v2

--- a/solution.py
+++ b/solution.py
@@ -211,7 +211,7 @@
     requesters, cap = chosen.shape
     live = lax.broadcasted_iota(jnp.int32, chosen.shape, 1) < pull_count[0][:, None]
 
-    def picked(table):
+    def picked(table, chosen):
         taken = jnp.take(table, chosen.reshape(-1), axis=0)
         taken = taken.reshape(chosen.shape + table.shape[1:])
         return jnp.where(live[:, :, None, None], taken, jnp.zeros((), table.dtype))
@@ -232,10 +232,11 @@
         0,
     )
     along = lax.all_gather(payload, "fsdp", axis=0)
-    sent_first, sent_second, along = lax.optimization_barrier(
-        (picked(history_first), picked(history_second), along)
-    )
+    payload, chosen = lax.optimization_barrier((payload, chosen))
+    sent_first = picked(history_first, chosen)
+    sent_first, chosen = lax.optimization_barrier((sent_first, chosen))
     arrived_first = pull(sent_first)
+    sent_second = picked(history_second, chosen)
     bias_full = along[:, 2 * share, : bias_first.shape[0]].reshape(hidden_width)
     both = lax.all_gather(along[:, : 2 * share], "dom", axis=0)
     both = both.reshape(dom_size, fsdp_size, 2, share, hidden_width)
@@ -289,13 +290,18 @@
     def near_sum(term):
         terms = term.reshape(z_size, x_size, y_size, cores, share, hidden_width)
         terms = scatter_sum(terms, 3, core_hop, core, cores)
-        terms = scatter_sum(terms, 1, x_hop, x, x_size)
-        return scatter_sum(terms, 1, y_hop, y, y_size)
+        cut = hidden_width // 2
+        left = scatter_sum(terms[..., :cut], 1, x_hop, x, x_size)
+        right = scatter_sum(terms[..., cut:], 2, y_hop, y, y_size)
+        left = scatter_sum(left, 1, y_hop, y, y_size)
+        right = scatter_sum(right, 1, x_hop, x, x_size)
+        return jnp.concatenate([left, right], -1)
 
     first_near = near_sum(first_term)
     bias_sum = sum_all(bias_rows[0], core_hop, cores)
     bias_sum = sum_all(bias_sum, x_hop, x_size)
     bias_sum = sum_all(bias_sum, y_hop, y_size)
+    bias_sum = sum_all(bias_sum, z_hop, z_size)
     hidden_held, arrived_second, first_near, bias_sum = lax.optimization_barrier(
         (hidden_new, arrived_second, first_near, bias_sum)
     )
@@ -313,12 +319,11 @@
         3 * mat,
     )
     near = jnp.stack([first_near, near_sum(second_term)], 1)
-    piece = scatter_sum(near, 0, z_hop, z, z_size)
+    piece = scatter_sum(near, 0, z_hop, z, z_size).astype(BF16)
     pieces = gather_all(piece, y_hop, y, y_size)
     pieces = gather_all(pieces, core_hop, core, cores)
-    totals = pieces.transpose(2, 1, 0, 3, 4).reshape(2, rows, hidden_width)
-
-    bias_sum = sum_all(bias_sum, z_hop, z_size)
+    totals = pieces.transpose(2, 1, 0, 3, 4).reshape(2, rows, hidden_width).astype(F32)
+
     bias_len = bias_first.shape[0]
     bias_total = lax.dynamic_slice_in_dim(bias_sum, fsdp_index * bias_len, bias_len, 0)
     return (hidden_new, totals[0], totals[1], bias_total)

time: 328 us -> 326 us (level)
  waiting for transfers between devices: 206 us -> 190 us
  starting transfers between devices: 30 us -> 43.1 us
    ppermute x6, waiting for transfers between devices: 9.02 us -> 69.4 us  [sum_all(): total = total + hop(k)(vector)]
    all_gather x1, waiting for transfers between devices: 69.2 us -> 32.1 us  [on_device(): both = lax.all_gather(along[:, :2 * share], 'dom', axis=0)]
    all_to_all x2, waiting for transfers between devices: 34.6 us -> 0.01 us  [pull(): lax.all_to_all(sent, ('dom', 'fsdp'), split_axis=0, concat_axis=0, tiled=...]
    ppermute x9 -> x13, waiting for transfers between devices: 61.9 us -> 29.3 us  [scatter_sum(): mine = mine + hop(k)(theirs.astype(BF16)).astype(F32)]
    all_gather x1, waiting for transfers between devices: 26.8 us -> 53.7 us  [on_device(): along = lax.all_gather(payload, 'fsdp', axis=0)]
    all_to_all x2, starting transfers between devices: 7.42 us -> 21.3 us  [pull(): lax.all_to_all(sent, ('dom', 'fsdp'), split_axis=0, concat_axis=0, tiled=...]
    ppermute x9 -> x13, starting transfers between devices: 12.1 us -> 16.2 us  [scatter_sum(): mine = mine + hop(k)(theirs.astype(BF16)).astype(F32)]
    ppermute x6, starting transfers between devices: 8.58 us -> 5.16 us  [sum_all(): total = total + hop(k)(vector)]
  transfers between devices with their start and end apart: 21 -> 25, of which waited for: 17 -> 18; matrix products, arithmetic and copies ran while one was open for 12% -> 13% of each run, Pallas kernels for 5% -> 5%
where the time goes in v3:
time: 326 us; the launch traced here: 325 us
  waiting for transfers between devices  190 us (58%)
  starting transfers between devices  43.1 us (13%)
  local copies, waits for them, and re-layouts  33.9 us (10%)
  Pallas kernels  26.2 us (8%)
  other arithmetic  17.5 us (5%)
  between operations  14.6 us (4%)
    ppermute x6, waiting for transfers between devices, sum_all(): total = total + hop(k)(vector)  69.4 us
    all_gather x1, waiting for transfers between devices, on_device(): along = lax.all_gather(payload, 'fsdp', axis=0)  53.7 us
    all_gather x1, waiting for transfers between devices, on_device(): both = lax.all_gather(along[:, :2 * share], 'dom', axis=0)  32.1 us
    ppermute x13, waiting for transfers between devices, scatter_sum(): mine = mine + hop(k)(theirs.astype(BF16)).astype(F32)  29.3 us
    pallas_call x3, Pallas kernels, local_call(): pl.pallas_call(kernel, name=name, out_shape=out_shape, in_specs=in_specs,...  26.2 us
    all_to_all x2, starting transfers between devices, pull(): lax.all_to_all(sent, ('dom', 'fsdp'), split_axis=0, concat_axis=0, tiled=...  21.3 us
    ppermute x13, starting transfers between devices, scatter_sum(): mine = mine + hop(k)(theirs.astype(BF16)).astype(F32)  16.2 us
    gather x2, local copies, waits for them, and re-layouts, picked(): taken = jnp.take(table, chosen.reshape(-1), axis=0)  10.5 us
  transfers between devices with their start and end apart: 25, of which 18 were waited for; matrix products, arithmetic and copies ran while one was open for 13% of the time, Pallas kernels for 5%

profile of v3, /device:TPU:0, one launch (start us, length us, event | category | flops | bytes accessed | tf_op | source)
XLA Modules:
  0.0 325.3 jit_solution(6470201837142465932)
XLA Ops:
  7.2 0.9 constant_dynamic-slice_fusion.4
  8.1 1.3 fusion.22
  9.5 0.8 copy.57
  10.4 0.7 iota_compare_fusion.1
  11.1 5.2 %gather_fusion = bf16[128,128,128]{2,1,0:T(8,128)(2,1)} fusion(bf16[128,128,128]{2,1,0:T(8,128)(2,1)} %param.15, s32[1024]{0:T(1024)S(1)} %pad_clamp_fusion.1), kind=kCustom, calls=%fused_computation.clone | custom fusion | bytes 8389120 | tf_op jit(solution)/shard_map/jit(_take)/gather | solution.py:215
  16.3 2.6 broadcast_select_fusion.1
  19.0 2.4 broadcast_select_fusion.3
  21.4 7.4 %all-to-all-start = ((bf16[32,4,128,128]{3,2,1,0:T(8,128)(2,1)}), bf16[32,4,128,128]{3,2,1,0:T(8,128)(2,1)}, u32[]{:S(2)}, u32[]{:S(2)}) async-start(bf16[32,4,128,128]{3,2,1,0:T(8,128)(2,1)} %broadcast_select_fusion.3), calls=%async_computation | async-start | bytes 8388608 | tf_op jit(solution)/shard_map/all_to_all | solution.py:220
  28.9 53.7 %all-gather.5.cloned.1.call-done = bf16[640,1024]{1,0:T(8,128)(2,1)} async-done(((bf16[80,1024]{1,0:T(8,128)(2,1)}), bf16[640,1024]{1,0:T(8,128)(2,1)}) %all-gather.5.cloned.1.call-update) | async-done | bytes 1310736 | tf_op jit(solution)/shard_map/all_gather | solution.py:234
  82.6 2.3 slice.52
  85.1 5.3 %gather_fusion.1 = bf16[128,128,128]{2,1,0:T(8,128)(2,1)} fusion(bf16[128,128,128]{2,1,0:T(8,128)(2,1)} %param.16, s32[1024]{0:T(1024)S(1)} %pad_clamp_fusion), kind=kCustom, calls=%fused_computation.1.clone | custom fusion | bytes 8389120 | tf_op jit(solution)/shard_map/jit(_take)/gather | solution.py:215
  90.4 2.6 broadcast_select_fusion
  93.0 2.4 broadcast_select_fusion.2
  95.4 32.1 %all-gather.7.cloned.1.call-done = bf16[32,64,1024]{2,1,0:T(8,128)(2,1)} async-done(((bf16[8,64,1024]{2,1,0:T(8,128)(2,1)}), bf16[32,64,1024]{2,1,0:T(8,128)(2,1)}) %all-gather.7.cloned.1.call-update) | async-done | bytes 4194320 | tf_op jit(solution)/shard_map/all_gather | solution.py:241
  127.5 4.2 %fusion.32 = (bf16[1,8,4,32,1024]{4,3,0,1,2:T(8,128)(2,1)}, bf16[1,8,4,32,1024]{4,3,0,1,2:T(8,128)(2,1)S(1)}) fusion(bf16[2,8,4,32,1024]{4,3,0,1,2:T(8,128)(2,1)} %bitcast.121), kind=kLoop, calls=%fused_computation.88 | loop fusion | bytes 8388608 | tf_op jit(solution)/shard_map/slice | solution.py:245
  131.6 1.6 copy.59
  133.2 2.9 copy.60
  136.2 1.8 copy.61
  138.0 3.7 %back_to_hidden.1.back_ref = f32[4,1024,128]{2,1,0:T(8,128)S(1)} custom-call(s32[4,6]{1,0:T(4,128)S(1)} %copy-done.5, s32[4]{0:T(128)S(1)} %copy-done.6, bf16[1024,1024]{1,0:T(8,128)(2,1)S(1)} %bitcast.115, bf16[4,1024,128]{2,1,0:T(8,128)(2,1)S(1)} %copy-done.1, bf16[4,6,128,128]{3,2,1,0:T(8,128)(2,1)S(1)} %copy-done.3), custom_call_target="tpu_custom_call" | custom-call | flops 2147483648 | bytes 7864320 | tf_op jit(solution)/shard_map/back_to_hidden/pallas_call | solution.py:125
  141.8 1.3 copy-done.8
  143.1 13.9 %all-to-all-start.1 = ((bf16[32,4,128,128]{3,2,1,0:T(8,128)(2,1)}), bf16[32,4,128,128]{3,2,1,0:T(8,128)(2,1)}, u32[]{:S(2)}, u32[]{:S(2)}) async-start(bf16[32,4,128,128]{3,2,1,0:T(8,128)(2,1)} %broadcast_select_fusion.2), calls=%async_computation.1 | async-start | bytes 8388608 | tf_op jit(solution)/shard_map/all_to_all | solution.py:220
  157.0 0.7 fusion.30
  157.8 0.2 copy.62.bias_ref
  158.0 1.2 copy-done
  159.2 12.9 %first_layer.1 = (bf16[4,1024,128]{2,1,0:T(8,128)(2,1)}, f32[1024,1024]{1,0:T(8,128)}, f32[8,1024]{1,0:T(8,128)S(1)}) custom-call(s32[4,6]{1,0:T(4,128)S(1)} %copy-done.5, s32[4]{0:T(128)S(1)} %copy-done.6, bf16[4,1024,128]{2,1,0:T(8,128)(2,1)S(1)} %copy-done, bf16[4,8,4,128,128]{4,3,2,1,0:T(8,128)(2,1)} %bitcast.5.arr_ref, ...), custom_call_target="tpu_custom_call" | custom-call | flops 4294967296 | bytes 20455424 | tf_op jit(solution)/shard_map/first_layer/pallas_call | solution.py:125
  172.1 1.7 fusion.1
  173.8 0.4 collective-permute-start
  174.3 0.1 collective-permute-start.5
  174.4 2.2 collective-permute-done.5
  176.6 3.0 collective-permute-start.6
  179.6 24.4 %collective-permute-done.6 = f32[1024]{0:T(1024)S(1)} collective-permute-done((f32[1024]{0:T(1024)S(1)}, f32[1024]{0:T(1024)S(1)}, u32[]{:S(2)}, u32[]{:S(2)}) %collective-permute-start.6) | collective-permute-done | bytes 4128 | tf_op jit(solution)/shard_map/ppermute | solution.py:166
  204.0 4.0 %collective-permute-done.7 = f32[1024]{0:T(1024)S(1)} collective-permute-done((f32[1024]{0:T(1024)S(1)}, f32[1024]{0:T(1024)S(1)}, u32[]{:S(2)}, u32[]{:S(2)}) %collective-permute-start.7) | collective-permute-done | bytes 4128 | tf_op jit(solution)/shard_map/ppermute | solution.py:166
  208.1 2.0 collective-permute-start.8
  210.1 1.9 bitcast_add_fusion.1
  212.0 0.2 fusion.34
  212.3 17.7 %collective-permute-done.10 = f32[1024]{0:T(1024)S(1)} collective-permute-done((f32[1024]{0:T(1024)S(1)}, f32[1024]{0:T(1024)S(1)}, u32[]{:S(2)}, u32[]{:S(2)}) %collective-permute-start.10) | collective-permute-done | bytes 4128 | tf_op jit(solution)/shard_map/ppermute | solution.py:166
  230.0 1.9 collective-permute-done.8
  231.9 19.2 %collective-permute-done.9 = f32[1024]{0:T(1024)S(1)} collective-permute-done((f32[1024]{0:T(1024)S(1)}, f32[1024]{0:T(1024)S(1)}, u32[]{:S(2)}, u32[]{:S(2)}) %collective-permute-start.9) | collective-permute-done | bytes 4128 | tf_op jit(solution)/shard_map/ppermute | solution.py:166
  251.1 1.7 collective-permute-start.3
  253.0 0.4 collective-permute-start.2
  253.4 7.0 %collective-permute-done.3 = bf16[4,2,32,512]{3,2,0,1:T(8,128)(2,1)S(1)} collective-permute-done((bf16[4,2,32,512]{3,2,0,1:T(8,128)(2,1)S(1)}, bf16[4,2,32,512]{3,2,0,1:T(8,128)(2,1)S(1)}, u32[]{:S(2)}, u32[]{:S(2)}) %collective-permute-start.3) | collective-permute-done | bytes 262176 | tf_op jit(solution)/shard_map/ppermute | solution.py:149
  260.5 1.5 collective-permute-start.4
  262.0 3.5 %collective-permute-done.4 = bf16[4,32,512]{2,1,0:T(8,128)(2,1)S(1)} collective-permute-done((bf16[4,32,512]{2,1,0:T(8,128)(2,1)S(1)}, bf16[4,32,512]{2,1,0:T(8,128)(2,1)S(1)}, u32[]{:S(2)}, u32[]{:S(2)}) %collective-permute-start.4) | collective-permute-done | bytes 131104 | tf_op jit(solution)/shard_map/ppermute | solution.py:149
  265.6 9.6 %second_layer.1 = f32[1024,1024]{1,0:T(8,128)} custom-call(s32[4,6]{1,0:T(4,128)S(1)} %copy-done.5, s32[4]{0:T(128)S(1)} %copy-done.6, bf16[4,1024,128]{2,1,0:T(8,128)(2,1)S(1)} %copy-done.7, bf16[4,8,4,128,128]{4,3,2,1,0:T(8,128)(2,1)} %bitcast.14.arr_ref, bf16[4,6,128,128]{3,2,1,0:T(8,128)(2,1)S(1)} %copy-done.4, bf16[4,1024,128]{2,1,0:T(8,128)(2,1)S(1)} %copy-done.2), custom_call_target="tpu_custom_call" | custom-call | flops 3221225472 | bytes 14155776 | tf_op jit(solution)/shard_map/second_layer/pallas_call | solution.py:125
  275.2 1.7 fusion
  277.1 2.6 collective-permute-done.11
  279.7 1.9 bitcast_add_fusion
  281.7 0.2 fusion.33
  281.9 0.8 collective-permute-start.12
  282.7 3.1 collective-permute-start.14
  285.9 4.4 %collective-permute-done.12 = bf16[4,2,32,512]{3,2,0,1:T(8,128)(2,1)S(1)} collective-permute-done((bf16[4,2,32,512]{3,2,0,1:T(8,128)(2,1)S(1)}, bf16[4,2,32,512]{3,2,0,1:T(8,128)(2,1)S(1)}, u32[]{:S(2)}, u32[]{:S(2)}) %collective-permute-start.12) | collective-permute-done | bytes 262176 | tf_op jit(solution)/shard_map/ppermute | solution.py:149
  290.4 3.8 %collective-permute-start.13 = (bf16[4,32,512]{2,1,0:T(8,128)(2,1)S(1)}, bf16[4,32,512]{2,1,0:T(8,128)(2,1)S(1)}, u32[]{:S(2)}, u32[]{:S(2)}) collective-permute-start(bf16[4,32,512]{2,1,0:T(8,128)(2,1)S(1)} %fusion.25), channel_id=1, source_target_pairs={{0,16},{8,24},{16,0},{24,8},{1,17},{9,25},{17,1},{25,9},{2,18},{10... | collective-permute-start | bytes 393224 | tf_op jit(solution)/shard_map/ppermute | solution.py:149
  294.3 0.4 collective-permute-start.15
  294.7 2.5 collective-permute-done.13
  297.2 2.2 collective-permute-done.15
  299.6 3.7 %collective-permute-start.18 = (bf16[2,32,1024]{2,1,0:T(8,128)(2,1)S(1)}, bf16[2,32,1024]{2,1,0:T(8,128)(2,1)S(1)}, u32[]{:S(2)}, u32[]{:S(2)}) collective-permute-start(bf16[2,32,1024]{2,1,0:T(8,128)(2,1)S(1)} %get-tuple-element.45), channel_id=1, source_target_pairs={{0,6},{1,7},{2,0},{3,1},{4,2},{5,3},{6,4},{7,5},{8,14},{9,15},{10,... | collective-permute-start | bytes 393224 | tf_op jit(solution)/shard_map/ppermute | solution.py:149
  303.4 4.2 %collective-permute-done.16 = bf16[2,32,1024]{2,1,0:T(8,128)(2,1)S(1)} collective-permute-done((bf16[2,32,1024]{2,1,0:T(8,128)(2,1)S(1)}, bf16[2,32,1024]{2,1,0:T(8,128)(2,1)S(1)}, u32[]{:S(2)}, u32[]{:S(2)}) %collective-permute-start.16) | collective-permute-done | bytes 131104 | tf_op jit(solution)/shard_map/ppermute | solution.py:149
  307.6 2.9 collective-permute-done.17
  310.6 0.3 collective-permute-start.19
  310.9 4.7 %collective-permute-done.19 = bf16[2,32,1024]{2,1,0:T(8,128)(2,1)S(1)} collective-permute-done((bf16[2,32,1024]{2,1,0:T(8,128)(2,1)S(1)}, bf16[2,32,1024]{2,1,0:T(8,128)(2,1)S(1)}, u32[]{:S(2)}, u32[]{:S(2)}) %collective-permute-start.19) | collective-permute-done | bytes 131104 | tf_op jit(solution)/shard_map/ppermute | solution.py:158
  315.7 0.6 dynamic_slice.112
  316.4 0.8 collective-permute-done.20
  317.2 0.1 convert_bitcast_fusion
  317.4 1.1 fusion.35
  (76 shorter events, 1.9 us)
Async XLA Ops:
  7.2 75.4 %all-gather.5.cloned.1.call-start = ((), (), s32[]{:S(2)}) async-start(), calls=%async_computation.2 | async-start | bytes 1474560 | tf_op jit(solution)/shard_map/all_gather | solution.py:234
  21.4 63.5 %copy-start.9 = (s32[1,32,4]{1,2,0:T(4,128)S(1)}, s32[1,32,4]{1,2,0:T(4,128)}, u32[]{:S(2)}) copy-start(s32[1,32,4]{1,2,0:T(4,128)} %param.17) | copy-start | bytes 1540
  21.4 121.7 %all-to-all-start = ((bf16[32,4,128,128]{3,2,1,0:T(8,128)(2,1)}), bf16[32,4,128,128]{3,2,1,0:T(8,128)(2,1)}, u32[]{:S(2)}, u32[]{:S(2)}) async-start(bf16[32,4,128,128]{3,2,1,0:T(8,128)(2,1)} %broadcast_select_fusion.3), calls=%async_computation | async-start | bytes 8388608 | tf_op jit(solution)/shard_map/all_to_all | solution.py:220
  28.8 98.6 %all-gather.7.cloned.1.call-start = ((), (), s32[]{:S(2)}) async-start(), calls=%async_computation.3 | async-start | bytes 5242880 | tf_op jit(solution)/shard_map/all_gather | solution.py:241
  133.2 4.8 %copy-start.1 = (bf16[4,1024,128]{2,1,0:T(8,128)(2,1)S(1)}, bf16[4,1024,128]{2,1,0:T(8,128)(2,1)}, u32[]{:S(2)}) copy-start(bf16[4,1024,128]{2,1,0:T(8,128)(2,1)} %cot_ref.1) | copy-start | bytes 3145732
  133.2 4.8 %copy-start.5 = (s32[4,6]{1,0:T(4,128)S(1)}, s32[4,6]{1,0:T(4,128)}, u32[]{:S(2)}) copy-start(s32[4,6]{1,0:T(4,128)} %src_ref.5) | copy-start | bytes 292
  133.2 4.8 %copy-start.6 = (s32[4]{0:T(128)S(1)}, s32[4]{0:T(128)}, u32[]{:S(2)}) copy-start(s32[4]{0:T(128)} %cnt_ref.5) | copy-start | bytes 52
  136.2 1.9 copy-start.3
  141.8 1.3 copy-start.8
  143.1 14.9 %copy-start.4 = (bf16[4,6,128,128]{3,2,1,0:T(8,128)(2,1)S(1)}, bf16[4,6,128,128]{3,2,1,0:T(8,128)(2,1)}, u32[]{:S(2)}) copy-start(bf16[4,6,128,128]{3,2,1,0:T(8,128)(2,1)} %tiles_ref.5) | copy-start | bytes 2359300
  143.1 122.5 %all-to-all-start.1 = ((bf16[32,4,128,128]{3,2,1,0:T(8,128)(2,1)}), bf16[32,4,128,128]{3,2,1,0:T(8,128)(2,1)}, u32[]{:S(2)}, u32[]{:S(2)}) async-start(bf16[32,4,128,128]{3,2,1,0:T(8,128)(2,1)} %broadcast_select_fusion.2), calls=%async_computation.1 | async-start | bytes 8388608 | tf_op jit(solution)/shard_map/all_to_all | solution.py:220
  158.0 1.2 copy-start
  173.8 36.2 %collective-permute-start = (bf16[4,2,2,32,1024]{4,3,0,1,2:T(8,128)(2,1)S(1)}, bf16[4,2,2,32,1024]{4,3,0,1,2:T(8,128)(2,1)S(1)}, u32[]{:S(2)}, u32[]{:S(2)}) collective-permute-start(bf16[4,2,2,32,1024]{4,3,0,1,2:T(8,128)(2,1)S(1)} %fusion.1), channel_id=1, source_target_pairs={{0,8},{8,0},{16,24},{24,16},{1,9},{9,1},{17,25},{25,17},{2,10},{10... | collective-permute-start | bytes 3145736 | tf_op jit(solution)/shard_map/ppermute | solution.py:149
  174.3 2.3 collective-permute-start.5
  176.6 27.4 %collective-permute-start.6 = (f32[1024]{0:T(1024)S(1)}, f32[1024]{0:T(1024)S(1)}, u32[]{:S(2)}, u32[]{:S(2)}) collective-permute-start(f32[1024]{0:T(1024)S(1)} %add.216), channel_id=1, source_target_pairs={{0,1},{1,0},{2,3},{3,2},{4,5},{5,4},{6,7},{7,6},{8,9},{9,8},{10,11... | collective-permute-start | bytes 12296 | tf_op jit(solution)/shard_map/ppermute | solution.py:166
  204.0 4.0 %collective-permute-start.7 = (f32[1024]{0:T(1024)S(1)}, f32[1024]{0:T(1024)S(1)}, u32[]{:S(2)}, u32[]{:S(2)}) collective-permute-start(f32[1024]{0:T(1024)S(1)} %add.217), channel_id=1, source_target_pairs={{0,16},{8,24},{16,0},{24,8},{1,17},{9,25},{17,1},{25,9},{2,18},{10... | collective-permute-start | bytes 12296 | tf_op jit(solution)/shard_map/ppermute | solution.py:166
  208.0 21.9 %collective-permute-start.10 = (f32[1024]{0:T(1024)S(1)}, f32[1024]{0:T(1024)S(1)}, u32[]{:S(2)}, u32[]{:S(2)}) collective-permute-start(f32[1024]{0:T(1024)S(1)} %add.218), channel_id=1, source_target_pairs={{0,6},{1,7},{2,0},{3,1},{4,2},{5,3},{6,4},{7,5},{8,14},{9,15},{10,... | collective-permute-start | bytes 12296 | tf_op jit(solution)/shard_map/ppermute | solution.py:166
  208.1 23.9 %collective-permute-start.8 = (f32[1024]{0:T(1024)S(1)}, f32[1024]{0:T(1024)S(1)}, u32[]{:S(2)}, u32[]{:S(2)}) collective-permute-start(f32[1024]{0:T(1024)S(1)} %add.218), channel_id=1, source_target_pairs={{0,2},{1,3},{2,4},{3,5},{4,6},{5,7},{6,0},{7,1},{8,10},{9,11},{10,... | collective-permute-start | bytes 12296 | tf_op jit(solution)/shard_map/ppermute | solution.py:166
  210.1 41.0 %collective-permute-start.9 = (f32[1024]{0:T(1024)S(1)}, f32[1024]{0:T(1024)S(1)}, u32[]{:S(2)}, u32[]{:S(2)}) collective-permute-start(f32[1024]{0:T(1024)S(1)} %add.218), channel_id=1, source_target_pairs={{0,4},{1,5},{2,6},{3,7},{4,0},{5,1},{6,2},{7,3},{8,12},{9,13},{10,... | collective-permute-start | bytes 12296 | tf_op jit(solution)/shard_map/ppermute | solution.py:166
  212.2 53.5 %copy-start.2 = (bf16[4,1024,128]{2,1,0:T(8,128)(2,1)S(1)}, bf16[4,1024,128]{2,1,0:T(8,128)(2,1)}, u32[]{:S(2)}) copy-start(bf16[4,1024,128]{2,1,0:T(8,128)(2,1)} %cot_ref.1) | copy-start | bytes 3145732
  212.2 53.5 %copy-start.7 = (bf16[4,1024,128]{2,1,0:T(8,128)(2,1)S(1)}, bf16[4,1024,128]{2,1,0:T(8,128)(2,1)}, u32[]{:S(2)}) copy-start(bf16[4,1024,128]{2,1,0:T(8,128)(2,1)} %get-tuple-element.30.own_ref) | copy-start | bytes 3145732
  212.2 40.6 %collective-permute-start.1 = (bf16[4,2,32,512]{3,2,0,1:T(8,128)(2,1)S(1)}, bf16[4,2,32,512]{3,2,0,1:T(8,128)(2,1)S(1)}, u32[]{:S(2)}, u32[]{:S(2)}) collective-permute-start(bf16[4,2,32,512]{3,2,0,1:T(8,128)(2,1)S(1)} %fusion.4), channel_id=1, source_target_pairs={{0,1},{1,0},{2,3},{3,2},{4,5},{5,4},{6,7},{7,6},{8,9},{9,8},{10,11... | collective-permute-start | bytes 786440 | tf_op jit(solution)/shard_map/ppermute | solution.py:149
  251.1 9.3 %collective-permute-start.3 = (bf16[4,2,32,512]{3,2,0,1:T(8,128)(2,1)S(1)}, bf16[4,2,32,512]{3,2,0,1:T(8,128)(2,1)S(1)}, u32[]{:S(2)}, u32[]{:S(2)}) collective-permute-start(bf16[4,2,32,512]{3,2,0,1:T(8,128)(2,1)S(1)} %fusion.5), channel_id=1, source_target_pairs={{0,16},{8,24},{16,0},{24,8},{1,17},{9,25},{17,1},{25,9},{2,18},{10... | collective-permute-start | bytes 786440 | tf_op jit(solution)/shard_map/ppermute | solution.py:149
  253.0 9.0 %collective-permute-start.2 = (bf16[4,32,512]{2,1,0:T(8,128)(2,1)S(1)}, bf16[4,32,512]{2,1,0:T(8,128)(2,1)S(1)}, u32[]{:S(2)}, u32[]{:S(2)}) collective-permute-start(bf16[4,32,512]{2,1,0:T(8,128)(2,1)S(1)} %fusion.23), channel_id=1, source_target_pairs={{0,16},{8,24},{16,0},{24,8},{1,17},{9,25},{17,1},{25,9},{2,18},{10... | collective-permute-start | bytes 393224 | tf_op jit(solution)/shard_map/ppermute | solution.py:149
  260.5 5.0 %collective-permute-start.4 = (bf16[4,32,512]{2,1,0:T(8,128)(2,1)S(1)}, bf16[4,32,512]{2,1,0:T(8,128)(2,1)S(1)}, u32[]{:S(2)}, u32[]{:S(2)}) collective-permute-start(bf16[4,32,512]{2,1,0:T(8,128)(2,1)S(1)} %fusion.24), channel_id=1, source_target_pairs={{0,1},{1,0},{2,3},{3,2},{4,5},{5,4},{6,7},{7,6},{8,9},{9,8},{10,11... | collective-permute-start | bytes 393224 | tf_op jit(solution)/shard_map/ppermute | solution.py:149
  277.0 2.7 collective-permute-start.11
  281.9 8.4 %collective-permute-start.12 = (bf16[4,2,32,512]{3,2,0,1:T(8,128)(2,1)S(1)}, bf16[4,2,32,512]{3,2,0,1:T(8,128)(2,1)S(1)}, u32[]{:S(2)}, u32[]{:S(2)}) collective-permute-start(bf16[4,2,32,512]{3,2,0,1:T(8,128)(2,1)S(1)} %fusion.7), channel_id=1, source_target_pairs={{0,1},{1,0},{2,3},{3,2},{4,5},{5,4},{6,7},{7,6},{8,9},{9,8},{10,11... | collective-permute-start | bytes 786440 | tf_op jit(solution)/shard_map/ppermute | solution.py:149
  282.7 11.5 %collective-permute-start.14 = (bf16[4,2,32,512]{3,2,1,0:T(8,128)(2,1)S(1)}, bf16[4,2,32,512]{3,2,1,0:T(8,128)(2,1)S(1)}, u32[]{:S(2)}, u32[]{:S(2)}) collective-permute-start(bf16[4,2,32,512]{3,2,1,0:T(8,128)(2,1)S(1)} %fusion.6), channel_id=1, source_target_pairs={{0,16},{8,24},{16,0},{24,8},{1,17},{9,25},{17,1},{25,9},{2,18},{10... | collective-permute-start | bytes 786440 | tf_op jit(solution)/shard_map/ppermute | solution.py:149
  290.4 6.7 %collective-permute-start.13 = (bf16[4,32,512]{2,1,0:T(8,128)(2,1)S(1)}, bf16[4,32,512]{2,1,0:T(8,128)(2,1)S(1)}, u32[]{:S(2)}, u32[]{:S(2)}) collective-permute-start(bf16[4,32,512]{2,1,0:T(8,128)(2,1)S(1)} %fusion.25), channel_id=1, source_target_pairs={{0,16},{8,24},{16,0},{24,8},{1,17},{9,25},{17,1},{25,9},{2,18},{10... | collective-permute-start | bytes 393224 | tf_op jit(solution)/shard_map/ppermute | solution.py:149
  294.3 5.0 %collective-permute-start.15 = (bf16[4,32,512]{2,1,0:T(8,128)(2,1)S(1)}, bf16[4,32,512]{2,1,0:T(8,128)(2,1)S(1)}, u32[]{:S(2)}, u32[]{:S(2)}) collective-permute-start(bf16[4,32,512]{2,1,0:T(8,128)(2,1)S(1)} %fusion.26), channel_id=1, source_target_pairs={{0,1},{1,0},{2,3},{3,2},{4,5},{5,4},{6,7},{7,6},{8,9},{9,8},{10,11... | collective-permute-start | bytes 393224 | tf_op jit(solution)/shard_map/ppermute | solution.py:149
  299.5 8.1 %collective-permute-start.16 = (bf16[2,32,1024]{2,1,0:T(8,128)(2,1)S(1)}, bf16[2,32,1024]{2,1,0:T(8,128)(2,1)S(1)}, u32[]{:S(2)}, u32[]{:S(2)}) collective-permute-start(bf16[2,32,1024]{2,1,0:T(8,128)(2,1)S(1)} %get-tuple-element.43), channel_id=1, source_target_pairs={{0,2},{1,3},{2,4},{3,5},{4,6},{5,7},{6,0},{7,1},{8,10},{9,11},{10,... | collective-permute-start | bytes 393224 | tf_op jit(solution)/shard_map/ppermute | solution.py:149
  299.6 10.9 %collective-permute-start.17 = (bf16[2,32,1024]{2,1,0:T(8,128)(2,1)S(1)}, bf16[2,32,1024]{2,1,0:T(8,128)(2,1)S(1)}, u32[]{:S(2)}, u32[]{:S(2)}) collective-permute-start(bf16[2,32,1024]{2,1,0:T(8,128)(2,1)S(1)} %get-tuple-element.44), channel_id=1, source_target_pairs={{0,4},{1,5},{2,6},{3,7},{4,0},{5,1},{6,2},{7,3},{8,12},{9,13},{10,... | collective-permute-start | bytes 393224 | tf_op jit(solution)/shard_map/ppermute | solution.py:149
  299.6 10.8 %collective-permute-start.18 = (bf16[2,32,1024]{2,1,0:T(8,128)(2,1)S(1)}, bf16[2,32,1024]{2,1,0:T(8,128)(2,1)S(1)}, u32[]{:S(2)}, u32[]{:S(2)}) collective-permute-start(bf16[2,32,1024]{2,1,0:T(8,128)(2,1)S(1)} %get-tuple-element.45), channel_id=1, source_target_pairs={{0,6},{1,7},{2,0},{3,1},{4,2},{5,3},{6,4},{7,5},{8,14},{9,15},{10,... | collective-permute-start | bytes 393224 | tf_op jit(solution)/shard_map/ppermute | solution.py:149
  310.6 5.0 %collective-permute-start.19 = (bf16[2,32,1024]{2,1,0:T(8,128)(2,1)S(1)}, bf16[2,32,1024]{2,1,0:T(8,128)(2,1)S(1)}, u32[]{:S(2)}, u32[]{:S(2)}) collective-permute-start(bf16[2,32,1024]{2,1,0:T(8,128)(2,1)S(1)} %get-tuple-element.34), channel_id=1, source_target_pairs={{0,16},{8,24},{16,0},{24,8},{1,17},{9,25},{17,1},{25,9},{2,18},{10... | collective-permute-start | bytes 393224 | tf_op jit(solution)/shard_map/ppermute | solution.py:158
  315.6 1.6 collective-permute-start.20
Sparse Core Ops, SparseCore 0:
  10.8 71.7 all-gather.4
  85.0 42.4 all-gather.6

commit v4 on v3

--- a/solution.py
+++ b/solution.py
@@ -259,9 +259,7 @@
         ],
         2 * mat,
     )
-    sent_second, arrived_first, first_turned, back_hidden = lax.optimization_barrier(
-        (sent_second, arrived_first, first_turned, back_hidden)
-    )
+    sent_second, arrived_first = lax.optimization_barrier((sent_second, arrived_first))
     arrived_second = pull(sent_second)
     hidden_new, first_term, bias_rows = local_call(
         first_kernel,
@@ -287,9 +285,12 @@
         ],
         4 * mat,
     )
-    def near_sum(term):
+    def near_sum(term, split):
         terms = term.reshape(z_size, x_size, y_size, cores, share, hidden_width)
         terms = scatter_sum(terms, 3, core_hop, core, cores)
+        if not split:
+            terms = scatter_sum(terms, 1, x_hop, x, x_size)
+            return scatter_sum(terms, 1, y_hop, y, y_size)
         cut = hidden_width // 2
         left = scatter_sum(terms[..., :cut], 1, x_hop, x, x_size)
         right = scatter_sum(terms[..., cut:], 2, y_hop, y, y_size)
@@ -297,11 +298,10 @@
         right = scatter_sum(right, 1, x_hop, x, x_size)
         return jnp.concatenate([left, right], -1)
 
-    first_near = near_sum(first_term)
+    first_near = near_sum(first_term, False)
     bias_sum = sum_all(bias_rows[0], core_hop, cores)
     bias_sum = sum_all(bias_sum, x_hop, x_size)
     bias_sum = sum_all(bias_sum, y_hop, y_size)
-    bias_sum = sum_all(bias_sum, z_hop, z_size)
     hidden_held, arrived_second, first_near, bias_sum = lax.optimization_barrier(
         (hidden_new, arrived_second, first_near, bias_sum)
     )
@@ -318,14 +318,18 @@
         ],
         3 * mat,
     )
-    near = jnp.stack([first_near, near_sum(second_term)], 1)
-    piece = scatter_sum(near, 0, z_hop, z, z_size).astype(BF16)
+    bias_rows = jnp.pad(bias_sum.reshape(z_size, 1, -1), ((0, 0), (0, 7), (0, 0)))
+    bias_rows = jnp.pad(
+        bias_rows, ((0, 0), (0, 0), (0, hidden_width - hidden_width // z_size))
+    )
+    near = jnp.concatenate([first_near, near_sum(second_term, True), bias_rows], 1)
+    piece = scatter_sum(near, 0, z_hop, z, z_size)
+    bias_len = bias_first.shape[0]
+    bias_total = lax.dynamic_slice_in_dim(piece[2 * share], x * bias_len, bias_len, 0)
+    piece = piece[: 2 * share].astype(BF16).reshape(2, share, hidden_width)
     pieces = gather_all(piece, y_hop, y, y_size)
     pieces = gather_all(pieces, core_hop, core, cores)
     totals = pieces.transpose(2, 1, 0, 3, 4).reshape(2, rows, hidden_width).astype(F32)
-
-    bias_len = bias_first.shape[0]
-    bias_total = lax.dynamic_slice_in_dim(bias_sum, fsdp_index * bias_len, bias_len, 0)
     return (hidden_new, totals[0], totals[1], bias_total)
 
 

time: 326 us -> 311 us (0.954)
  waiting for transfers between devices: 190 us -> 158 us
  starting transfers between devices: 43.1 us -> 56.4 us
    ppermute x6 -> x3, waiting for transfers between devices: 69.4 us -> 5.5 us  [sum_all(): total = total + hop(k)(vector)]
    all_gather x1, waiting for transfers between devices: 32.1 us -> 2.05 us  [on_device(): both = lax.all_gather(along[:, :2 * share], 'dom', axis=0)]
    ppermute x13 -> x11, starting transfers between devices: 16.2 us -> 41 us  [scatter_sum(): mine = mine + hop(k)(theirs.astype(BF16)).astype(F32)]
    all_gather x1, waiting for transfers between devices: 53.7 us -> 77.3 us  [on_device(): along = lax.all_gather(payload, 'fsdp', axis=0)]
    all_to_all x2, waiting for transfers between devices: 0.01 us -> 19.5 us  [pull(): lax.all_to_all(sent, ('dom', 'fsdp'), split_axis=0, concat_axis=0, tiled=...]
    ppermute x13 -> x11, waiting for transfers between devices: 29.3 us -> 47.5 us  [scatter_sum(): mine = mine + hop(k)(theirs.astype(BF16)).astype(F32)]
    all_to_all x2, starting transfers between devices: 21.3 us -> 11 us  [pull(): lax.all_to_all(sent, ('dom', 'fsdp'), split_axis=0, concat_axis=0, tiled=...]
    add x10 -> x9, other arithmetic: 4.24 us -> 6.83 us  [scatter_sum(): mine = mine + hop(k)(theirs.astype(BF16)).astype(F32)]
  transfers between devices with their start and end apart: 25 -> 20, of which waited for: 18 -> 17; matrix products, arithmetic and copies ran while one was open for 13% -> 10% of each run, Pallas kernels for 5% -> 5%
where the time goes in v4:
time: 311 us; the launch traced here: 310 us
  waiting for transfers between devices  158 us (51%)
  starting transfers between devices  56.4 us (18%)
  local copies, waits for them, and re-layouts  34.1 us (11%)
  Pallas kernels  26.7 us (9%)
  other arithmetic  20.3 us (7%)
  between operations  14.6 us (5%)
    all_gather x1, waiting for transfers between devices, on_device(): along = lax.all_gather(payload, 'fsdp', axis=0)  77.3 us
    ppermute x11, waiting for transfers between devices, scatter_sum(): mine = mine + hop(k)(theirs.astype(BF16)).astype(F32)  47.5 us
    ppermute x11, starting transfers between devices, scatter_sum(): mine = mine + hop(k)(theirs.astype(BF16)).astype(F32)  41 us
    pallas_call x3, Pallas kernels, local_call(): pl.pallas_call(kernel, name=name, out_shape=out_shape, in_specs=in_specs,...  26.7 us
    all_to_all x2, waiting for transfers between devices, pull(): lax.all_to_all(sent, ('dom', 'fsdp'), split_axis=0, concat_axis=0, tiled=...  19.5 us
    all_to_all x2, starting transfers between devices, pull(): lax.all_to_all(sent, ('dom', 'fsdp'), split_axis=0, concat_axis=0, tiled=...  11 us
    gather x2, local copies, waits for them, and re-layouts, picked(): taken = jnp.take(table, chosen.reshape(-1), axis=0)  10.6 us
    add x9, other arithmetic, scatter_sum(): mine = mine + hop(k)(theirs.astype(BF16)).astype(F32)  6.83 us
  transfers between devices with their start and end apart: 20, of which 17 were waited for; matrix products, arithmetic and copies ran while one was open for 10% of the time, Pallas kernels for 5%

profile of v4, /device:TPU:0, one launch (start us, length us, event | category | flops | bytes accessed | tf_op | source)
XLA Modules:
  0.0 309.7 jit_solution(14258629708016684762)
XLA Ops:
  7.2 0.9 constant_dynamic-slice_fusion.5
  8.1 1.3 fusion.9
  9.4 0.8 copy.51
  10.2 0.1 reshape.104
  10.3 0.7 iota_compare_fusion.2
  11.0 5.3 %gather_fusion = bf16[128,128,128]{2,1,0:T(8,128)(2,1)} fusion(bf16[128,128,128]{2,1,0:T(8,128)(2,1)} %param.15, s32[1024]{0:T(1024)S(1)} %pad_clamp_fusion.1), kind=kCustom, calls=%fused_computation.clone | custom fusion | bytes 8389120 | tf_op jit(solution)/shard_map/jit(_take)/gather | solution.py:215
  16.3 2.6 broadcast_select_fusion.1
  18.9 2.3 broadcast_select_fusion.3
  21.3 7.4 %all-to-all-start = ((bf16[32,4,128,128]{3,2,1,0:T(8,128)(2,1)}), bf16[32,4,128,128]{3,2,1,0:T(8,128)(2,1)}, u32[]{:S(2)}, u32[]{:S(2)}) async-start(bf16[32,4,128,128]{3,2,1,0:T(8,128)(2,1)} %broadcast_select_fusion.3), calls=%async_computation | async-start | bytes 8388608 | tf_op jit(solution)/shard_map/all_to_all | solution.py:220
  28.8 0.7 all-gather.5.cloned.1.call-update
  29.5 77.3 %all-gather.5.cloned.1.call-done = bf16[640,1024]{1,0:T(8,128)(2,1)} async-done(((bf16[80,1024]{1,0:T(8,128)(2,1)}), bf16[640,1024]{1,0:T(8,128)(2,1)}) %all-gather.5.cloned.1.call-update) | async-done | bytes 1310736 | tf_op jit(solution)/shard_map/all_gather | solution.py:234
  106.8 2.3 slice.53
  109.1 0.1 copy.52
  109.2 0.1 reshape.106
  109.4 5.3 %gather_fusion.1 = bf16[128,128,128]{2,1,0:T(8,128)(2,1)} fusion(bf16[128,128,128]{2,1,0:T(8,128)(2,1)} %param.16, s32[1024]{0:T(1024)S(1)} %pad_clamp_fusion), kind=kCustom, calls=%fused_computation.1.clone | custom fusion | bytes 8389120 | tf_op jit(solution)/shard_map/jit(_take)/gather | solution.py:215
  114.7 2.9 broadcast_select_fusion
  117.6 2.5 broadcast_select_fusion.2
  120.1 19.5 %all-to-all-done = bf16[32,4,128,128]{3,2,1,0:T(8,128)(2,1)} async-done(((bf16[32,4,128,128]{3,2,1,0:T(8,128)(2,1)}), bf16[32,4,128,128]{3,2,1,0:T(8,128)(2,1)}, u32[]{:S(2)}, u32[]{:S(2)}) %all-to-all-start) | async-done | bytes 4194336 | tf_op jit(solution)/shard_map/all_to_all | solution.py:220
  139.5 3.6 %all-to-all-start.1 = ((bf16[32,4,128,128]{3,2,1,0:T(8,128)(2,1)}), bf16[32,4,128,128]{3,2,1,0:T(8,128)(2,1)}, u32[]{:S(2)}, u32[]{:S(2)}) async-start(bf16[32,4,128,128]{3,2,1,0:T(8,128)(2,1)} %broadcast_select_fusion.2), calls=%async_computation.1 | async-start | bytes 8388608 | tf_op jit(solution)/shard_map/all_to_all | solution.py:220
  143.1 0.7 fusion.15
  143.9 0.2 copy.56.bias_ref
  144.1 2.1 all-gather.7.cloned.1.call-done
  146.2 4.2 %fusion.17 = (bf16[1,8,4,32,1024]{4,3,0,1,2:T(8,128)(2,1)}, bf16[1,8,4,32,1024]{4,3,0,1,2:T(8,128)(2,1)S(1)}) fusion(bf16[2,8,4,32,1024]{4,3,0,1,2:T(8,128)(2,1)} %bitcast.90), kind=kLoop, calls=%fused_computation.67 | loop fusion | bytes 8388608 | tf_op jit(solution)/shard_map/slice | solution.py:245
  150.3 1.6 copy.53
  151.9 2.9 copy.54
  154.8 2.0 copy.55
  156.9 3.7 %back_to_hidden.1.back_ref = f32[4,1024,128]{2,1,0:T(8,128)S(1)} custom-call(s32[4,6]{1,0:T(4,128)S(1)} %copy-done.4, s32[4]{0:T(128)S(1)} %copy-done.5, bf16[1024,1024]{1,0:T(8,128)(2,1)S(1)} %bitcast.86, bf16[4,1024,128]{2,1,0:T(8,128)(2,1)S(1)} %copy-done.1, bf16[4,6,128,128]{3,2,1,0:T(8,128)(2,1)S(1)} %copy-done.3), custom_call_target="tpu_custom_call" | custom-call | flops 2147483648 | bytes 7864320 | tf_op jit(solution)/shard_map/back_to_hidden/pallas_call | solution.py:125
  160.6 1.4 copy-done.7
  161.9 13.1 %first_layer.1 = (bf16[4,1024,128]{2,1,0:T(8,128)(2,1)}, f32[1024,1024]{1,0:T(8,128)}, f32[8,1024]{1,0:T(8,128)S(1)}) custom-call(s32[4,6]{1,0:T(4,128)S(1)} %copy-done.4, s32[4]{0:T(128)S(1)} %copy-done.5, bf16[4,1024,128]{2,1,0:T(8,128)(2,1)S(1)} %copy-done, bf16[4,8,4,128,128]{4,3,2,1,0:T(8,128)(2,1)} %bitcast.5.arr_ref, ...), custom_call_target="tpu_custom_call" | custom-call | flops 4294967296 | bytes 20455424 | tf_op jit(solution)/shard_map/first_layer/pallas_call | solution.py:125
  175.0 1.7 fusion
  176.9 2.6 collective-permute-done
  179.5 1.9 bitcast_add_fusion.1
  181.5 1.3 copy-done.8
  182.9 32.5 %collective-permute-start.1 = (bf16[4,2,32,1024]{3,2,0,1:T(8,128)(2,1)S(1)}, bf16[4,2,32,1024]{3,2,0,1:T(8,128)(2,1)}, u32[]{:S(2)}, u32[]{:S(2)}) collective-permute-start(bf16[4,2,32,1024]{3,2,0,1:T(8,128)(2,1)S(1)} %fusion.2), channel_id=1, source_target_pairs={{0,1},{1,0},{2,3},{3,2},{4,5},{5,4},{6,7},{7,6},{8,9},{9,8},{10,11... | collective-permute-start | bytes 1572872 | tf_op jit(solution)/shard_map/ppermute | solution.py:149
  215.4 21.5 %collective-permute-done.1 = bf16[4,2,32,1024]{3,2,0,1:T(8,128)(2,1)} collective-permute-done((bf16[4,2,32,1024]{3,2,0,1:T(8,128)(2,1)S(1)}, bf16[4,2,32,1024]{3,2,0,1:T(8,128)(2,1)}, u32[]{:S(2)}, u32[]{:S(2)}) %collective-permute-start.1) | collective-permute-done | bytes 524320 | tf_op jit(solution)/shard_map/ppermute | solution.py:149
  236.8 1.5 bitcast_add_fusion.2
  238.4 1.4 collective-permute-start.2
  239.9 1.2 collective-permute-done.3
  241.0 2.6 collective-permute-start.4
  243.6 1.6 collective-permute-done.4
  245.2 0.8 collective-permute-start.5
  246.0 2.8 collective-permute-done.5
  248.8 1.2 bitcast_add_fusion.5
  250.0 9.9 %second_layer.1 = f32[1024,1024]{1,0:T(8,128)} custom-call(s32[4,6]{1,0:T(4,128)S(1)} %copy-done.4, s32[4]{0:T(128)S(1)} %copy-done.5, bf16[4,1024,128]{2,1,0:T(8,128)(2,1)S(1)} %copy-done.6, bf16[4,8,4,128,128]{4,3,2,1,0:T(8,128)(2,1)} %bitcast.14.arr_ref, bf16[4,6,128,128]{3,2,1,0:T(8,128)(2,1)S(1)} %copy-done.3, bf16[4,1024,128]{2,1,0:T(8,128)(2,1)S(1)} %copy-done.2), custom_call_target="tpu_custom_call" | custom-call | flops 3221225472 | bytes 14155776 | tf_op jit(solution)/shard_map/second_layer/pallas_call | solution.py:125
  259.9 1.7 fusion.1
  261.7 2.6 collective-permute-done.6
  264.4 1.9 bitcast_add_fusion
  266.3 0.2 fusion.18
  266.5 2.5 collective-permute-start.7
  269.2 6.5 %collective-permute-done.7 = bf16[4,2,32,512]{3,2,0,1:T(8,128)(2,1)S(1)} collective-permute-done((bf16[4,2,32,512]{3,2,0,1:T(8,128)(2,1)S(1)}, bf16[4,2,32,512]{3,2,0,1:T(8,128)(2,1)S(1)}, u32[]{:S(2)}, u32[]{:S(2)}) %collective-permute-start.7) | collective-permute-done | bytes 262176 | tf_op jit(solution)/shard_map/ppermute | solution.py:149
  275.9 1.4 collective-permute-done.9
  277.3 0.5 collective-permute-start.10
  277.8 3.1 collective-permute-done.8
  280.9 1.5 collective-permute-done.10
  282.4 0.1 select_maximum_fusion
  282.8 3.7 %collective-permute-start.13 = (bf16[72,1024]{1,0:T(8,128)(2,1)S(1)}, bf16[72,1024]{1,0:T(8,128)(2,1)S(1)}, u32[]{:S(2)}, u32[]{:S(2)}) collective-permute-start(bf16[72,1024]{1,0:T(8,128)(2,1)S(1)} %get-tuple-element.34), channel_id=1, source_target_pairs={{0,6},{1,7},{2,0},{3,1},{4,2},{5,3},{6,4},{7,5},{8,14},{9,15},{10,... | collective-permute-start | bytes 442376 | tf_op jit(solution)/shard_map/ppermute | solution.py:149
  286.5 4.8 %collective-permute-done.11 = bf16[72,1024]{1,0:T(8,128)(2,1)S(1)} collective-permute-done((bf16[72,1024]{1,0:T(8,128)(2,1)S(1)}, bf16[72,1024]{1,0:T(8,128)(2,1)S(1)}, u32[]{:S(2)}, u32[]{:S(2)}) %collective-permute-start.11) | collective-permute-done | bytes 147488 | tf_op jit(solution)/shard_map/ppermute | solution.py:149
  291.3 3.6 %collective-permute-done.12 = bf16[72,1024]{1,0:T(8,128)(2,1)S(1)} collective-permute-done((bf16[72,1024]{1,0:T(8,128)(2,1)S(1)}, bf16[72,1024]{1,0:T(8,128)(2,1)S(1)}, u32[]{:S(2)}, u32[]{:S(2)}) %collective-permute-start.12) | collective-permute-done | bytes 147488 | tf_op jit(solution)/shard_map/ppermute | solution.py:149
  295.0 0.8 collective-permute-start.14
  295.9 4.1 %collective-permute-done.14 = bf16[2,32,1024]{2,1,0:T(8,128)(2,1)S(1)} collective-permute-done((bf16[2,32,1024]{2,1,0:T(8,128)(2,1)S(1)}, bf16[2,32,1024]{2,1,0:T(8,128)(2,1)S(1)}, u32[]{:S(2)}, u32[]{:S(2)}) %collective-permute-start.14) | collective-permute-done | bytes 131104 | tf_op jit(solution)/shard_map/ppermute | solution.py:158
  300.1 0.5 fusion.16
  300.7 0.9 collective-permute-done.15
  301.6 0.1 convert_bitcast_fusion
  301.8 1.1 fusion.19
  (64 shorter events, 1.5 us)
Async XLA Ops:
  21.3 118.3 %all-to-all-start = ((bf16[32,4,128,128]{3,2,1,0:T(8,128)(2,1)}), bf16[32,4,128,128]{3,2,1,0:T(8,128)(2,1)}, u32[]{:S(2)}, u32[]{:S(2)}) async-start(bf16[32,4,128,128]{3,2,1,0:T(8,128)(2,1)} %broadcast_select_fusion.3), calls=%async_computation | async-start | bytes 8388608 | tf_op jit(solution)/shard_map/all_to_all | solution.py:220
  28.7 80.4 %copy-start.10 = (s32[1,32,4]{1,2,0:T(4,128)S(1)}, s32[1,32,4]{1,2,0:T(4,128)}, u32[]{:S(2)}) copy-start(s32[1,32,4]{1,2,0:T(4,128)} %param.17) | copy-start | bytes 1540
  28.7 78.1 %all-gather.5.cloned.1.call-start = ((), (), s32[]{:S(2)}) async-start(), calls=%async_computation.2 | async-start | bytes 1474560 | tf_op jit(solution)/shard_map/all_gather | solution.py:234
  29.5 116.7 %all-gather.7.cloned.1.call-start = ((), (), s32[]{:S(2)}) async-start(), calls=%async_computation.3 | async-start | bytes 5242880 | tf_op jit(solution)/shard_map/all_gather | solution.py:241
  139.5 110.4 %all-to-all-start.1 = ((bf16[32,4,128,128]{3,2,1,0:T(8,128)(2,1)}), bf16[32,4,128,128]{3,2,1,0:T(8,128)(2,1)}, u32[]{:S(2)}, u32[]{:S(2)}) async-start(bf16[32,4,128,128]{3,2,1,0:T(8,128)(2,1)} %broadcast_select_fusion.2), calls=%async_computation.1 | async-start | bytes 8388608 | tf_op jit(solution)/shard_map/all_to_all | solution.py:220
  154.8 2.0 copy-start.1
  154.8 2.1 copy-start.3
  154.8 2.1 copy-start.4
  154.8 2.1 copy-start.5
  156.8 5.1 %copy-start = (bf16[4,1024,128]{2,1,0:T(8,128)(2,1)S(1)}, bf16[4,1024,128]{2,1,0:T(8,128)(2,1)}, u32[]{:S(2)}) copy-start(bf16[4,1024,128]{2,1,0:T(8,128)(2,1)} %own_ref.1) | copy-start | bytes 3145732
  160.6 1.4 copy-start.7
  176.8 2.7 collective-permute-start
  181.4 1.4 copy-start.8
  182.9 54.0 %collective-permute-start.1 = (bf16[4,2,32,1024]{3,2,0,1:T(8,128)(2,1)S(1)}, bf16[4,2,32,1024]{3,2,0,1:T(8,128)(2,1)}, u32[]{:S(2)}, u32[]{:S(2)}) collective-permute-start(bf16[4,2,32,1024]{3,2,0,1:T(8,128)(2,1)S(1)} %fusion.2), channel_id=1, source_target_pairs={{0,1},{1,0},{2,3},{3,2},{4,5},{5,4},{6,7},{7,6},{8,9},{9,8},{10,11... | collective-permute-start | bytes 1572872 | tf_op jit(solution)/shard_map/ppermute | solution.py:149
  215.4 34.6 %copy-start.2 = (bf16[4,1024,128]{2,1,0:T(8,128)(2,1)S(1)}, bf16[4,1024,128]{2,1,0:T(8,128)(2,1)}, u32[]{:S(2)}) copy-start(bf16[4,1024,128]{2,1,0:T(8,128)(2,1)} %cot_ref.1) | copy-start | bytes 3145732
  215.4 34.6 %copy-start.6 = (bf16[4,1024,128]{2,1,0:T(8,128)(2,1)S(1)}, bf16[4,1024,128]{2,1,0:T(8,128)(2,1)}, u32[]{:S(2)}) copy-start(bf16[4,1024,128]{2,1,0:T(8,128)(2,1)} %get-tuple-element.26.own_ref) | copy-start | bytes 3145732
  238.4 1.5 copy-start.9
  238.4 10.4 %collective-permute-start.2 = (bf16[4,32,1024]{2,1,0:T(8,128)(2,1)S(1)}, bf16[4,32,1024]{2,1,0:T(8,128)(2,1)}, u32[]{:S(2)}, u32[]{:S(2)}) collective-permute-start(bf16[4,32,1024]{2,1,0:T(8,128)(2,1)S(1)} %fusion.6), channel_id=1, source_target_pairs={{0,16},{8,24},{16,0},{24,8},{1,17},{9,25},{17,1},{25,9},{2,18},{10... | collective-permute-start | bytes 786440 | tf_op jit(solution)/shard_map/ppermute | solution.py:149
  239.9 1.2 collective-permute-start.3
  241.0 4.1 %collective-permute-start.4 = (f32[1024]{0:T(1024)S(1)}, f32[1024]{0:T(1024)S(1)}, u32[]{:S(2)}, u32[]{:S(2)}) collective-permute-start(f32[1024]{0:T(1024)S(1)} %add.197), channel_id=1, source_target_pairs={{0,1},{1,0},{2,3},{3,2},{4,5},{5,4},{6,7},{7,6},{8,9},{9,8},{10,11... | collective-permute-start | bytes 12296 | tf_op jit(solution)/shard_map/ppermute | solution.py:166
  245.2 3.6 %collective-permute-start.5 = (f32[1024]{0:T(1024)S(1)}, f32[1024]{0:T(1024)S(1)}, u32[]{:S(2)}, u32[]{:S(2)}) collective-permute-start(f32[1024]{0:T(1024)S(1)} %add.198), channel_id=1, source_target_pairs={{0,16},{8,24},{16,0},{24,8},{1,17},{9,25},{17,1},{25,9},{2,18},{10... | collective-permute-start | bytes 12296 | tf_op jit(solution)/shard_map/ppermute | solution.py:166
  261.6 2.7 collective-permute-start.6
  266.5 9.1 %collective-permute-start.7 = (bf16[4,2,32,512]{3,2,0,1:T(8,128)(2,1)S(1)}, bf16[4,2,32,512]{3,2,0,1:T(8,128)(2,1)S(1)}, u32[]{:S(2)}, u32[]{:S(2)}) collective-permute-start(bf16[4,2,32,512]{3,2,0,1:T(8,128)(2,1)S(1)} %fusion.7), channel_id=1, source_target_pairs={{0,1},{1,0},{2,3},{3,2},{4,5},{5,4},{6,7},{7,6},{8,9},{9,8},{10,11... | collective-permute-start | bytes 786440 | tf_op jit(solution)/shard_map/ppermute | solution.py:149
  269.1 8.1 %collective-permute-start.9 = (bf16[4,2,32,512]{3,2,0,1:T(8,128)(2,1)S(1)}, bf16[4,2,32,512]{3,2,0,1:T(8,128)(2,1)S(1)}, u32[]{:S(2)}, u32[]{:S(2)}) collective-permute-start(bf16[4,2,32,512]{3,2,0,1:T(8,128)(2,1)S(1)} %fusion.8), channel_id=1, source_target_pairs={{0,16},{8,24},{16,0},{24,8},{1,17},{9,25},{17,1},{25,9},{2,18},{10... | collective-permute-start | bytes 786440 | tf_op jit(solution)/shard_map/ppermute | solution.py:149
  275.8 5.1 %collective-permute-start.8 = (bf16[4,32,512]{2,1,0:T(8,128)(2,1)S(1)}, bf16[4,32,512]{2,1,0:T(8,128)(2,1)S(1)}, u32[]{:S(2)}, u32[]{:S(2)}) collective-permute-start(bf16[4,32,512]{2,1,0:T(8,128)(2,1)S(1)} %fusion.13), channel_id=1, source_target_pairs={{0,16},{8,24},{16,0},{24,8},{1,17},{9,25},{17,1},{25,9},{2,18},{10... | collective-permute-start | bytes 393224 | tf_op jit(solution)/shard_map/ppermute | solution.py:149
  277.3 5.0 %collective-permute-start.10 = (bf16[4,32,512]{2,1,0:T(8,128)(2,1)S(1)}, bf16[4,32,512]{2,1,0:T(8,128)(2,1)S(1)}, u32[]{:S(2)}, u32[]{:S(2)}) collective-permute-start(bf16[4,32,512]{2,1,0:T(8,128)(2,1)S(1)} %fusion.14), channel_id=1, source_target_pairs={{0,1},{1,0},{2,3},{3,2},{4,5},{5,4},{6,7},{7,6},{8,9},{9,8},{10,11... | collective-permute-start | bytes 393224 | tf_op jit(solution)/shard_map/ppermute | solution.py:149
  282.6 8.7 %collective-permute-start.11 = (bf16[72,1024]{1,0:T(8,128)(2,1)S(1)}, bf16[72,1024]{1,0:T(8,128)(2,1)S(1)}, u32[]{:S(2)}, u32[]{:S(2)}) collective-permute-start(bf16[72,1024]{1,0:T(8,128)(2,1)S(1)} %get-tuple-element.33), channel_id=1, source_target_pairs={{0,2},{1,3},{2,4},{3,5},{4,6},{5,7},{6,0},{7,1},{8,10},{9,11},{10,... | collective-permute-start | bytes 442376 | tf_op jit(solution)/shard_map/ppermute | solution.py:149
  282.7 12.2 %collective-permute-start.12 = (bf16[72,1024]{1,0:T(8,128)(2,1)S(1)}, bf16[72,1024]{1,0:T(8,128)(2,1)S(1)}, u32[]{:S(2)}, u32[]{:S(2)}) collective-permute-start(bf16[72,1024]{1,0:T(8,128)(2,1)S(1)} %get-tuple-element.35), channel_id=1, source_target_pairs={{0,4},{1,5},{2,6},{3,7},{4,0},{5,1},{6,2},{7,3},{8,12},{9,13},{10,... | collective-permute-start | bytes 442376 | tf_op jit(solution)/shard_map/ppermute | solution.py:149
  282.8 12.1 %collective-permute-start.13 = (bf16[72,1024]{1,0:T(8,128)(2,1)S(1)}, bf16[72,1024]{1,0:T(8,128)(2,1)S(1)}, u32[]{:S(2)}, u32[]{:S(2)}) collective-permute-start(bf16[72,1024]{1,0:T(8,128)(2,1)S(1)} %get-tuple-element.34), channel_id=1, source_target_pairs={{0,6},{1,7},{2,0},{3,1},{4,2},{5,3},{6,4},{7,5},{8,14},{9,15},{10,... | collective-permute-start | bytes 442376 | tf_op jit(solution)/shard_map/ppermute | solution.py:149
  295.0 5.0 %collective-permute-start.14 = (bf16[2,32,1024]{2,1,0:T(8,128)(2,1)S(1)}, bf16[2,32,1024]{2,1,0:T(8,128)(2,1)S(1)}, u32[]{:S(2)}, u32[]{:S(2)}) collective-permute-start(bf16[2,32,1024]{2,1,0:T(8,128)(2,1)S(1)} %bitcast.97), channel_id=1, source_target_pairs={{0,16},{8,24},{16,0},{24,8},{1,17},{9,25},{17,1},{25,9},{2,18},{10... | collective-permute-start | bytes 393224 | tf_op jit(solution)/shard_map/ppermute | solution.py:158
  300.0 1.6 collective-permute-start.15
Sparse Core Ops, SparseCore 0:
  32.3 74.4 all-gather.4
  109.2 36.8 all-gather.6

commit v5 on v4

--- a/solution.py
+++ b/solution.py
@@ -302,8 +302,8 @@
     bias_sum = sum_all(bias_rows[0], core_hop, cores)
     bias_sum = sum_all(bias_sum, x_hop, x_size)
     bias_sum = sum_all(bias_sum, y_hop, y_size)
-    hidden_held, arrived_second, first_near, bias_sum = lax.optimization_barrier(
-        (hidden_new, arrived_second, first_near, bias_sum)
+    hidden_held, arrived_second, first_near = lax.optimization_barrier(
+        (hidden_new, arrived_second, first_near)
     )
     second_term = local_call(
         second_kernel,

time: 311 us -> 317 us (1.019)
  starting transfers between devices: 56.4 us -> 60.1 us
    ppermute x11, starting transfers between devices: 41 us -> 48.2 us  [scatter_sum(): mine = mine + hop(k)(theirs.astype(BF16)).astype(F32)]
    ppermute x3, waiting for transfers between devices: 5.5 us -> 10.2 us  [sum_all(): total = total + hop(k)(vector)]
    ppermute x3, starting transfers between devices: 3.41 us -> 0.09 us  [sum_all(): total = total + hop(k)(vector)]
  transfers between devices with their start and end apart: 20 -> 20, of which waited for: 17 -> 16; matrix products, arithmetic and copies ran while one was open for 10% -> 10% of each run, Pallas kernels for 5% -> 5%
where the time goes in v5:
time: 317 us; the launch traced here: 316 us
  waiting for transfers between devices  161 us (51%)
  starting transfers between devices  60.1 us (19%)
  local copies, waits for them, and re-layouts  35 us (11%)
  Pallas kernels  25.1 us (8%)
  other arithmetic  20.2 us (6%)
  between operations  14.5 us (5%)
    all_gather x1, waiting for transfers between devices, on_device(): along = lax.all_gather(payload, 'fsdp', axis=0)  77.3 us
    ppermute x11, starting transfers between devices, scatter_sum(): mine = mine + hop(k)(theirs.astype(BF16)).astype(F32)  48.2 us
    ppermute x11, waiting for transfers between devices, scatter_sum(): mine = mine + hop(k)(theirs.astype(BF16)).astype(F32)  46 us
    pallas_call x3, Pallas kernels, local_call(): pl.pallas_call(kernel, name=name, out_shape=out_shape, in_specs=in_specs,...  25.1 us
    all_to_all x2, waiting for transfers between devices, pull(): lax.all_to_all(sent, ('dom', 'fsdp'), split_axis=0, concat_axis=0, tiled=...  19.5 us
    all_to_all x2, starting transfers between devices, pull(): lax.all_to_all(sent, ('dom', 'fsdp'), split_axis=0, concat_axis=0, tiled=...  11 us
    gather x2, local copies, waits for them, and re-layouts, picked(): taken = jnp.take(table, chosen.reshape(-1), axis=0)  10.6 us
    ppermute x3, waiting for transfers between devices, sum_all(): total = total + hop(k)(vector)  10.2 us
  transfers between devices with their start and end apart: 20, of which 16 were waited for; matrix products, arithmetic and copies ran while one was open for 10% of the time, Pallas kernels for 5%

profile of v5, /device:TPU:0, one launch (start us, length us, event | category | flops | bytes accessed | tf_op | source)
XLA Modules:
  0.0 316.0 jit_solution(13384248469699862244)
XLA Ops:
  7.2 0.9 constant_dynamic-slice_fusion.5
  8.1 1.3 fusion.9
  9.4 0.8 copy.51
  10.2 0.1 reshape.104
  10.3 0.7 iota_compare_fusion.2
  11.0 5.3 %gather_fusion = bf16[128,128,128]{2,1,0:T(8,128)(2,1)} fusion(bf16[128,128,128]{2,1,0:T(8,128)(2,1)} %param.15, s32[1024]{0:T(1024)S(1)} %pad_clamp_fusion.1), kind=kCustom, calls=%fused_computation.clone | custom fusion | bytes 8389120 | tf_op jit(solution)/shard_map/jit(_take)/gather | solution.py:215
  16.3 2.6 broadcast_select_fusion.1
  18.9 2.3 broadcast_select_fusion.3
  21.3 7.4 %all-to-all-start = ((bf16[32,4,128,128]{3,2,1,0:T(8,128)(2,1)}), bf16[32,4,128,128]{3,2,1,0:T(8,128)(2,1)}, u32[]{:S(2)}, u32[]{:S(2)}) async-start(bf16[32,4,128,128]{3,2,1,0:T(8,128)(2,1)} %broadcast_select_fusion.3), calls=%async_computation | async-start | bytes 8388608 | tf_op jit(solution)/shard_map/all_to_all | solution.py:220
  28.8 0.7 all-gather.5.cloned.1.call-update
  29.5 77.3 %all-gather.5.cloned.1.call-done = bf16[640,1024]{1,0:T(8,128)(2,1)} async-done(((bf16[80,1024]{1,0:T(8,128)(2,1)}), bf16[640,1024]{1,0:T(8,128)(2,1)}) %all-gather.5.cloned.1.call-update) | async-done | bytes 1310736 | tf_op jit(solution)/shard_map/all_gather | solution.py:234
  106.8 2.3 slice.53
  109.1 0.1 copy.52
  109.2 0.1 reshape.106
  109.4 5.3 %gather_fusion.1 = bf16[128,128,128]{2,1,0:T(8,128)(2,1)} fusion(bf16[128,128,128]{2,1,0:T(8,128)(2,1)} %param.16, s32[1024]{0:T(1024)S(1)} %pad_clamp_fusion), kind=kCustom, calls=%fused_computation.1.clone | custom fusion | bytes 8389120 | tf_op jit(solution)/shard_map/jit(_take)/gather | solution.py:215
  114.7 2.9 broadcast_select_fusion
  117.6 2.5 broadcast_select_fusion.2
  120.1 19.5 %all-to-all-done = bf16[32,4,128,128]{3,2,1,0:T(8,128)(2,1)} async-done(((bf16[32,4,128,128]{3,2,1,0:T(8,128)(2,1)}), bf16[32,4,128,128]{3,2,1,0:T(8,128)(2,1)}, u32[]{:S(2)}, u32[]{:S(2)}) %all-to-all-start) | async-done | bytes 4194336 | tf_op jit(solution)/shard_map/all_to_all | solution.py:220
  139.5 3.6 %all-to-all-start.1 = ((bf16[32,4,128,128]{3,2,1,0:T(8,128)(2,1)}), bf16[32,4,128,128]{3,2,1,0:T(8,128)(2,1)}, u32[]{:S(2)}, u32[]{:S(2)}) async-start(bf16[32,4,128,128]{3,2,1,0:T(8,128)(2,1)} %broadcast_select_fusion.2), calls=%async_computation.1 | async-start | bytes 8388608 | tf_op jit(solution)/shard_map/all_to_all | solution.py:220
  143.1 0.7 fusion.15
  143.9 0.2 copy.56.bias_ref
  144.1 2.1 all-gather.7.cloned.1.call-done
  146.2 4.2 %fusion.17 = (bf16[1,8,4,32,1024]{4,3,0,1,2:T(8,128)(2,1)}, bf16[1,8,4,32,1024]{4,3,0,1,2:T(8,128)(2,1)S(1)}) fusion(bf16[2,8,4,32,1024]{4,3,0,1,2:T(8,128)(2,1)} %bitcast.90), kind=kLoop, calls=%fused_computation.67 | loop fusion | bytes 8388608 | tf_op jit(solution)/shard_map/slice | solution.py:245
  150.3 1.6 copy.53
  151.9 2.9 copy.54
  154.8 2.0 copy.55
  156.9 3.0 back_to_hidden.1.back_ref
  159.9 1.4 copy-done.7
  161.2 12.6 %first_layer.1 = (bf16[4,1024,128]{2,1,0:T(8,128)(2,1)}, f32[1024,1024]{1,0:T(8,128)}, f32[8,1024]{1,0:T(8,128)S(1)}) custom-call(s32[4,6]{1,0:T(4,128)S(1)} %copy-done.4, s32[4]{0:T(128)S(1)} %copy-done.5, bf16[4,1024,128]{2,1,0:T(8,128)(2,1)S(1)} %copy-done, bf16[4,8,4,128,128]{4,3,2,1,0:T(8,128)(2,1)} %bitcast.5.arr_ref, ...), custom_call_target="tpu_custom_call" | custom-call | flops 4294967296 | bytes 20455424 | tf_op jit(solution)/shard_map/first_layer/pallas_call | solution.py:125
  173.9 1.7 fusion
  175.6 0.3 collective-permute-start
  176.0 2.4 collective-permute-done
  178.3 1.9 bitcast_add_fusion.1
  180.3 1.3 copy-done.8
  181.7 34.8 %collective-permute-start.1 = (bf16[4,2,32,1024]{3,2,0,1:T(8,128)(2,1)S(1)}, bf16[4,2,32,1024]{3,2,0,1:T(8,128)(2,1)}, u32[]{:S(2)}, u32[]{:S(2)}) collective-permute-start(bf16[4,2,32,1024]{3,2,0,1:T(8,128)(2,1)S(1)} %fusion.2), channel_id=1, source_target_pairs={{0,1},{1,0},{2,3},{3,2},{4,5},{5,4},{6,7},{7,6},{8,9},{9,8},{10,11... | collective-permute-start | bytes 1572872 | tf_op jit(solution)/shard_map/ppermute | solution.py:149
  216.6 20.3 %collective-permute-done.1 = bf16[4,2,32,1024]{3,2,0,1:T(8,128)(2,1)} collective-permute-done((bf16[4,2,32,1024]{3,2,0,1:T(8,128)(2,1)S(1)}, bf16[4,2,32,1024]{3,2,0,1:T(8,128)(2,1)}, u32[]{:S(2)}, u32[]{:S(2)}) %collective-permute-start.1) | collective-permute-done | bytes 524320 | tf_op jit(solution)/shard_map/ppermute | solution.py:149
  236.8 1.5 bitcast_add_fusion.2
  238.4 1.0 copy-done.9
  239.4 1.3 collective-permute-start.2
  240.7 5.2 %collective-permute-done.2 = bf16[4,32,1024]{2,1,0:T(8,128)(2,1)} collective-permute-done((bf16[4,32,1024]{2,1,0:T(8,128)(2,1)S(1)}, bf16[4,32,1024]{2,1,0:T(8,128)(2,1)}, u32[]{:S(2)}, u32[]{:S(2)}) %collective-permute-start.2) | collective-permute-done | bytes 262176 | tf_op jit(solution)/shard_map/ppermute | solution.py:149
  245.9 1.2 bitcast_add_fusion.5
  247.1 9.4 %second_layer.1 = f32[1024,1024]{1,0:T(8,128)} custom-call(s32[4,6]{1,0:T(4,128)S(1)} %copy-done.4, s32[4]{0:T(128)S(1)} %copy-done.5, bf16[4,1024,128]{2,1,0:T(8,128)(2,1)S(1)} %copy-done.6, bf16[4,8,4,128,128]{4,3,2,1,0:T(8,128)(2,1)} %bitcast.14.arr_ref, bf16[4,6,128,128]{3,2,1,0:T(8,128)(2,1)S(1)} %copy-done.3, bf16[4,1024,128]{2,1,0:T(8,128)(2,1)S(1)} %copy-done.2), custom_call_target="tpu_custom_call" | custom-call | flops 3221225472 | bytes 14155776 | tf_op jit(solution)/shard_map/second_layer/pallas_call | solution.py:125
  256.6 1.7 fusion.1
  258.4 2.6 collective-permute-done.3
  261.0 1.9 bitcast_add_fusion
  262.9 0.2 fusion.18
  263.2 4.2 %collective-permute-start.4 = (bf16[4,2,32,512]{3,2,0,1:T(8,128)(2,1)S(1)}, bf16[4,2,32,512]{3,2,0,1:T(8,128)(2,1)S(1)}, u32[]{:S(2)}, u32[]{:S(2)}) collective-permute-start(bf16[4,2,32,512]{3,2,0,1:T(8,128)(2,1)S(1)} %fusion.7), channel_id=1, source_target_pairs={{0,1},{1,0},{2,3},{3,2},{4,5},{5,4},{6,7},{7,6},{8,9},{9,8},{10,11... | collective-permute-start | bytes 786440 | tf_op jit(solution)/shard_map/ppermute | solution.py:149
  267.3 1.2 collective-permute-done.8
  268.6 5.4 %collective-permute-done.9 = f32[1024]{0:T(1024)S(1)} collective-permute-done((f32[1024]{0:T(1024)S(1)}, f32[1024]{0:T(1024)S(1)}, u32[]{:S(2)}, u32[]{:S(2)}) %collective-permute-start.9) | collective-permute-done | bytes 4128 | tf_op jit(solution)/shard_map/ppermute | solution.py:166
  274.0 3.6 %collective-permute-done.10 = f32[1024]{0:T(1024)S(1)} collective-permute-done((f32[1024]{0:T(1024)S(1)}, f32[1024]{0:T(1024)S(1)}, u32[]{:S(2)}, u32[]{:S(2)}) %collective-permute-start.10) | collective-permute-done | bytes 4128 | tf_op jit(solution)/shard_map/ppermute | solution.py:166
  277.9 2.1 collective-permute-start.5
  279.9 5.9 %collective-permute-done.6 = bf16[4,2,32,512]{3,2,0,1:T(8,128)(2,1)S(1)} collective-permute-done((bf16[4,2,32,512]{3,2,0,1:T(8,128)(2,1)S(1)}, bf16[4,2,32,512]{3,2,0,1:T(8,128)(2,1)S(1)}, u32[]{:S(2)}, u32[]{:S(2)}) %collective-permute-start.6) | collective-permute-done | bytes 262176 | tf_op jit(solution)/shard_map/ppermute | solution.py:149
  285.9 1.5 collective-permute-start.7
  287.5 3.5 %collective-permute-done.7 = bf16[4,32,512]{2,1,0:T(8,128)(2,1)S(1)} collective-permute-done((bf16[4,32,512]{2,1,0:T(8,128)(2,1)S(1)}, bf16[4,32,512]{2,1,0:T(8,128)(2,1)S(1)}, u32[]{:S(2)}, u32[]{:S(2)}) %collective-permute-start.7) | collective-permute-done | bytes 131104 | tf_op jit(solution)/shard_map/ppermute | solution.py:149
  291.0 0.1 select_maximum_fusion
  291.4 3.7 %collective-permute-start.13 = (bf16[72,1024]{1,0:T(8,128)(2,1)S(1)}, bf16[72,1024]{1,0:T(8,128)(2,1)S(1)}, u32[]{:S(2)}, u32[]{:S(2)}) collective-permute-start(bf16[72,1024]{1,0:T(8,128)(2,1)S(1)} %get-tuple-element.32), channel_id=1, source_target_pairs={{0,6},{1,7},{2,0},{3,1},{4,2},{5,3},{6,4},{7,5},{8,14},{9,15},{10,... | collective-permute-start | bytes 442376 | tf_op jit(solution)/shard_map/ppermute | solution.py:149
  295.1 3.3 %collective-permute-done.11 = bf16[72,1024]{1,0:T(8,128)(2,1)S(1)} collective-permute-done((bf16[72,1024]{1,0:T(8,128)(2,1)S(1)}, bf16[72,1024]{1,0:T(8,128)(2,1)S(1)}, u32[]{:S(2)}, u32[]{:S(2)}) %collective-permute-start.11) | collective-permute-done | bytes 147488 | tf_op jit(solution)/shard_map/ppermute | solution.py:149
  298.4 2.8 collective-permute-done.12
  301.3 0.6 collective-permute-start.14
  302.0 4.3 %collective-permute-done.14 = bf16[2,32,1024]{2,1,0:T(8,128)(2,1)S(1)} collective-permute-done((bf16[2,32,1024]{2,1,0:T(8,128)(2,1)S(1)}, bf16[2,32,1024]{2,1,0:T(8,128)(2,1)S(1)}, u32[]{:S(2)}, u32[]{:S(2)}) %collective-permute-start.14) | collective-permute-done | bytes 131104 | tf_op jit(solution)/shard_map/ppermute | solution.py:158
  306.4 0.5 fusion.16
  307.0 0.9 collective-permute-done.15
  308.0 0.1 convert_bitcast_fusion
  308.1 1.1 fusion.19
  (64 shorter events, 1.4 us)
Async XLA Ops:
  21.3 118.3 %all-to-all-start = ((bf16[32,4,128,128]{3,2,1,0:T(8,128)(2,1)}), bf16[32,4,128,128]{3,2,1,0:T(8,128)(2,1)}, u32[]{:S(2)}, u32[]{:S(2)}) async-start(bf16[32,4,128,128]{3,2,1,0:T(8,128)(2,1)} %broadcast_select_fusion.3), calls=%async_computation | async-start | bytes 8388608 | tf_op jit(solution)/shard_map/all_to_all | solution.py:220
  28.7 80.4 %copy-start.10 = (s32[1,32,4]{1,2,0:T(4,128)S(1)}, s32[1,32,4]{1,2,0:T(4,128)}, u32[]{:S(2)}) copy-start(s32[1,32,4]{1,2,0:T(4,128)} %param.17) | copy-start | bytes 1540
  28.7 78.1 %all-gather.5.cloned.1.call-start = ((), (), s32[]{:S(2)}) async-start(), calls=%async_computation.2 | async-start | bytes 1474560 | tf_op jit(solution)/shard_map/all_gather | solution.py:234
  29.5 116.7 %all-gather.7.cloned.1.call-start = ((), (), s32[]{:S(2)}) async-start(), calls=%async_computation.3 | async-start | bytes 5242880 | tf_op jit(solution)/shard_map/all_gather | solution.py:241
  139.5 107.6 %all-to-all-start.1 = ((bf16[32,4,128,128]{3,2,1,0:T(8,128)(2,1)}), bf16[32,4,128,128]{3,2,1,0:T(8,128)(2,1)}, u32[]{:S(2)}, u32[]{:S(2)}) async-start(bf16[32,4,128,128]{3,2,1,0:T(8,128)(2,1)} %broadcast_select_fusion.2), calls=%async_computation.1 | async-start | bytes 8388608 | tf_op jit(solution)/shard_map/all_to_all | solution.py:220
  154.8 2.0 copy-start.1
  154.8 2.1 copy-start.3
  154.8 2.1 copy-start.4
  154.8 2.1 copy-start.5
  156.8 4.4 %copy-start = (bf16[4,1024,128]{2,1,0:T(8,128)(2,1)S(1)}, bf16[4,1024,128]{2,1,0:T(8,128)(2,1)}, u32[]{:S(2)}) copy-start(bf16[4,1024,128]{2,1,0:T(8,128)(2,1)} %own_ref.1) | copy-start | bytes 3145732
  159.9 1.4 copy-start.7
  175.6 2.7 collective-permute-start
  180.3 1.4 copy-start.8
  181.7 55.1 %collective-permute-start.1 = (bf16[4,2,32,1024]{3,2,0,1:T(8,128)(2,1)S(1)}, bf16[4,2,32,1024]{3,2,0,1:T(8,128)(2,1)}, u32[]{:S(2)}, u32[]{:S(2)}) collective-permute-start(bf16[4,2,32,1024]{3,2,0,1:T(8,128)(2,1)S(1)} %fusion.2), channel_id=1, source_target_pairs={{0,1},{1,0},{2,3},{3,2},{4,5},{5,4},{6,7},{7,6},{8,9},{9,8},{10,11... | collective-permute-start | bytes 1572872 | tf_op jit(solution)/shard_map/ppermute | solution.py:149
  216.6 30.6 %copy-start.2 = (bf16[4,1024,128]{2,1,0:T(8,128)(2,1)S(1)}, bf16[4,1024,128]{2,1,0:T(8,128)(2,1)}, u32[]{:S(2)}) copy-start(bf16[4,1024,128]{2,1,0:T(8,128)(2,1)} %cot_ref.1) | copy-start | bytes 3145732
  216.6 30.6 %copy-start.6 = (bf16[4,1024,128]{2,1,0:T(8,128)(2,1)S(1)}, bf16[4,1024,128]{2,1,0:T(8,128)(2,1)}, u32[]{:S(2)}) copy-start(bf16[4,1024,128]{2,1,0:T(8,128)(2,1)} %get-tuple-element.24.own_ref) | copy-start | bytes 3145732
  238.4 1.0 copy-start.9
  239.4 6.5 %collective-permute-start.2 = (bf16[4,32,1024]{2,1,0:T(8,128)(2,1)S(1)}, bf16[4,32,1024]{2,1,0:T(8,128)(2,1)}, u32[]{:S(2)}, u32[]{:S(2)}) collective-permute-start(bf16[4,32,1024]{2,1,0:T(8,128)(2,1)S(1)} %fusion.6), channel_id=1, source_target_pairs={{0,16},{8,24},{16,0},{24,8},{1,17},{9,25},{17,1},{25,9},{2,18},{10... | collective-permute-start | bytes 786440 | tf_op jit(solution)/shard_map/ppermute | solution.py:149
  258.3 2.7 collective-permute-start.3
  263.2 14.6 %collective-permute-start.4 = (bf16[4,2,32,512]{3,2,0,1:T(8,128)(2,1)S(1)}, bf16[4,2,32,512]{3,2,0,1:T(8,128)(2,1)S(1)}, u32[]{:S(2)}, u32[]{:S(2)}) collective-permute-start(bf16[4,2,32,512]{3,2,0,1:T(8,128)(2,1)S(1)} %fusion.7), channel_id=1, source_target_pairs={{0,1},{1,0},{2,3},{3,2},{4,5},{5,4},{6,7},{7,6},{8,9},{9,8},{10,11... | collective-permute-start | bytes 786440 | tf_op jit(solution)/shard_map/ppermute | solution.py:149
  267.3 1.2 collective-permute-start.8
  268.5 5.5 %collective-permute-start.9 = (f32[1024]{0:T(1024)S(1)}, f32[1024]{0:T(1024)S(1)}, u32[]{:S(2)}, u32[]{:S(2)}) collective-permute-start(f32[1024]{0:T(1024)S(1)} %add.202), channel_id=1, source_target_pairs={{0,1},{1,0},{2,3},{3,2},{4,5},{5,4},{6,7},{7,6},{8,9},{9,8},{10,11... | collective-permute-start | bytes 12296 | tf_op jit(solution)/shard_map/ppermute | solution.py:166
  274.0 3.6 %collective-permute-start.10 = (f32[1024]{0:T(1024)S(1)}, f32[1024]{0:T(1024)S(1)}, u32[]{:S(2)}, u32[]{:S(2)}) collective-permute-start(f32[1024]{0:T(1024)S(1)} %add.203), channel_id=1, source_target_pairs={{0,16},{8,24},{16,0},{24,8},{1,17},{9,25},{17,1},{25,9},{2,18},{10... | collective-permute-start | bytes 12296 | tf_op jit(solution)/shard_map/ppermute | solution.py:166
  277.7 8.2 %collective-permute-start.6 = (bf16[4,2,32,512]{3,2,0,1:T(8,128)(2,1)S(1)}, bf16[4,2,32,512]{3,2,0,1:T(8,128)(2,1)S(1)}, u32[]{:S(2)}, u32[]{:S(2)}) collective-permute-start(bf16[4,2,32,512]{3,2,0,1:T(8,128)(2,1)S(1)} %fusion.8), channel_id=1, source_target_pairs={{0,16},{8,24},{16,0},{24,8},{1,17},{9,25},{17,1},{25,9},{2,18},{10... | collective-permute-start | bytes 786440 | tf_op jit(solution)/shard_map/ppermute | solution.py:149
  277.9 9.6 %collective-permute-start.5 = (bf16[4,32,512]{2,1,0:T(8,128)(2,1)S(1)}, bf16[4,32,512]{2,1,0:T(8,128)(2,1)S(1)}, u32[]{:S(2)}, u32[]{:S(2)}) collective-permute-start(bf16[4,32,512]{2,1,0:T(8,128)(2,1)S(1)} %fusion.13), channel_id=1, source_target_pairs={{0,16},{8,24},{16,0},{24,8},{1,17},{9,25},{17,1},{25,9},{2,18},{10... | collective-permute-start | bytes 393224 | tf_op jit(solution)/shard_map/ppermute | solution.py:149
  285.9 5.0 %collective-permute-start.7 = (bf16[4,32,512]{2,1,0:T(8,128)(2,1)S(1)}, bf16[4,32,512]{2,1,0:T(8,128)(2,1)S(1)}, u32[]{:S(2)}, u32[]{:S(2)}) collective-permute-start(bf16[4,32,512]{2,1,0:T(8,128)(2,1)S(1)} %fusion.14), channel_id=1, source_target_pairs={{0,1},{1,0},{2,3},{3,2},{4,5},{5,4},{6,7},{7,6},{8,9},{9,8},{10,11... | collective-permute-start | bytes 393224 | tf_op jit(solution)/shard_map/ppermute | solution.py:149
  291.2 7.2 %collective-permute-start.11 = (bf16[72,1024]{1,0:T(8,128)(2,1)S(1)}, bf16[72,1024]{1,0:T(8,128)(2,1)S(1)}, u32[]{:S(2)}, u32[]{:S(2)}) collective-permute-start(bf16[72,1024]{1,0:T(8,128)(2,1)S(1)} %get-tuple-element.31), channel_id=1, source_target_pairs={{0,2},{1,3},{2,4},{3,5},{4,6},{5,7},{6,0},{7,1},{8,10},{9,11},{10,... | collective-permute-start | bytes 442376 | tf_op jit(solution)/shard_map/ppermute | solution.py:149
  291.3 9.9 %collective-permute-start.12 = (bf16[72,1024]{1,0:T(8,128)(2,1)S(1)}, bf16[72,1024]{1,0:T(8,128)(2,1)S(1)}, u32[]{:S(2)}, u32[]{:S(2)}) collective-permute-start(bf16[72,1024]{1,0:T(8,128)(2,1)S(1)} %get-tuple-element.33), channel_id=1, source_target_pairs={{0,4},{1,5},{2,6},{3,7},{4,0},{5,1},{6,2},{7,3},{8,12},{9,13},{10,... | collective-permute-start | bytes 442376 | tf_op jit(solution)/shard_map/ppermute | solution.py:149
  291.4 9.8 %collective-permute-start.13 = (bf16[72,1024]{1,0:T(8,128)(2,1)S(1)}, bf16[72,1024]{1,0:T(8,128)(2,1)S(1)}, u32[]{:S(2)}, u32[]{:S(2)}) collective-permute-start(bf16[72,1024]{1,0:T(8,128)(2,1)S(1)} %get-tuple-element.32), channel_id=1, source_target_pairs={{0,6},{1,7},{2,0},{3,1},{4,2},{5,3},{6,4},{7,5},{8,14},{9,15},{10,... | collective-permute-start | bytes 442376 | tf_op jit(solution)/shard_map/ppermute | solution.py:149
  301.3 5.0 %collective-permute-start.14 = (bf16[2,32,1024]{2,1,0:T(8,128)(2,1)S(1)}, bf16[2,32,1024]{2,1,0:T(8,128)(2,1)S(1)}, u32[]{:S(2)}, u32[]{:S(2)}) collective-permute-start(bf16[2,32,1024]{2,1,0:T(8,128)(2,1)S(1)} %bitcast.97), channel_id=1, source_target_pairs={{0,16},{8,24},{16,0},{24,8},{1,17},{9,25},{17,1},{25,9},{2,18},{10... | collective-permute-start | bytes 393224 | tf_op jit(solution)/shard_map/ppermute | solution.py:158
  306.3 1.6 collective-permute-start.15
Sparse Core Ops, SparseCore 0:
  32.3 74.4 all-gather.4
  109.2 36.8 all-gather.6

commit v6 on v5

--- a/solution.py
+++ b/solution.py
@@ -232,7 +232,6 @@
         0,
     )
     along = lax.all_gather(payload, "fsdp", axis=0)
-    payload, chosen = lax.optimization_barrier((payload, chosen))
     sent_first = picked(history_first, chosen)
     sent_first, chosen = lax.optimization_barrier((sent_first, chosen))
     arrived_first = pull(sent_first)
@@ -285,9 +284,11 @@
         ],
         4 * mat,
     )
-    def near_sum(term, split):
+    def near_sum(term, split, extra=None):
         terms = term.reshape(z_size, x_size, y_size, cores, share, hidden_width)
         terms = scatter_sum(terms, 3, core_hop, core, cores)
+        if extra is not None:
+            terms = jnp.concatenate([terms, extra], 3)
         if not split:
             terms = scatter_sum(terms, 1, x_hop, x, x_size)
             return scatter_sum(terms, 1, y_hop, y, y_size)
@@ -298,10 +299,14 @@
         right = scatter_sum(right, 1, x_hop, x, x_size)
         return jnp.concatenate([left, right], -1)
 
-    first_near = near_sum(first_term, False)
-    bias_sum = sum_all(bias_rows[0], core_hop, cores)
-    bias_sum = sum_all(bias_sum, x_hop, x_size)
-    bias_sum = sum_all(bias_sum, y_hop, y_size)
+    bias_len = bias_first.shape[0]
+    bias_share = bias_len // dom_size
+    bias_terms = bias_rows[0].reshape(z_size, x_size, y_size, cores, 1, bias_share)
+    bias_terms = scatter_sum(bias_terms, 3, core_hop, core, cores)
+    bias_terms = jnp.pad(
+        bias_terms, ((0, 0), (0, 0), (0, 0), (0, 7), (0, hidden_width - bias_share))
+    )
+    first_near = near_sum(first_term, False, bias_terms)
     hidden_held, arrived_second, first_near = lax.optimization_barrier(
         (hidden_new, arrived_second, first_near)
     )
@@ -318,19 +323,15 @@
         ],
         3 * mat,
     )
-    bias_rows = jnp.pad(bias_sum.reshape(z_size, 1, -1), ((0, 0), (0, 7), (0, 0)))
-    bias_rows = jnp.pad(
-        bias_rows, ((0, 0), (0, 0), (0, hidden_width - hidden_width // z_size))
-    )
-    near = jnp.concatenate([first_near, near_sum(second_term, True), bias_rows], 1)
-    piece = scatter_sum(near, 0, z_hop, z, z_size)
-    bias_len = bias_first.shape[0]
-    bias_total = lax.dynamic_slice_in_dim(piece[2 * share], x * bias_len, bias_len, 0)
-    piece = piece[: 2 * share].astype(BF16).reshape(2, share, hidden_width)
+    near = jnp.concatenate([first_near, near_sum(second_term, True)], 1)
+    piece = scatter_sum(near, 0, z_hop, z, z_size).astype(BF16)
     pieces = gather_all(piece, y_hop, y, y_size)
     pieces = gather_all(pieces, core_hop, core, cores)
-    totals = pieces.transpose(2, 1, 0, 3, 4).reshape(2, rows, hidden_width).astype(F32)
-    return (hidden_new, totals[0], totals[1], bias_total)
+    pieces = pieces.transpose(1, 0, 2, 3).astype(F32)
+    first_total = pieces[:, :, :share].reshape(rows, hidden_width)
+    second_total = pieces[:, :, share + 8 :].reshape(rows, hidden_width)
+    bias_total = pieces[:, :, share, :bias_share].reshape(bias_len)
+    return (hidden_new, first_total, second_total, bias_total)
 
 
 def solution(mesh):

time: 317 us -> 322 us (1.016)
  local copies, waits for them, and re-layouts: 35 us -> 45.6 us
  starting transfers between devices: 60.1 us -> 54 us
  waiting for transfers between devices: 161 us -> 157 us
  Pallas kernels: 25.1 us -> 28.8 us
    ppermute x3 -> x0, waiting for transfers between devices: 10.2 us -> none  [sum_all(): total = total + hop(k)(vector)]
    ppermute x11 -> x12, waiting for transfers between devices: 46 us -> 55.1 us  [scatter_sum(): mine = mine + hop(k)(theirs.astype(BF16)).astype(F32)]
    ppermute x11 -> x12, starting transfers between devices: 48.2 us -> 41.5 us  [scatter_sum(): mine = mine + hop(k)(theirs.astype(BF16)).astype(F32)]
    dynamic_update_slice x2, local copies, waits for them, and re-layouts: 0.03 us -> 3.91 us  [gather_all(): lax.dynamic_update_index_in_dim(whole, hop(k)(piece), (digit - k + length...]
    dynamic_update_slice x2 -> x1, local copies, waits for them, and re-layouts: 0.04 us -> 3.9 us  [gather_all(): whole = lax.dynamic_update_index_in_dim(whole, piece, digit, 0)]
    pallas_call x3, Pallas kernels: 25.1 us -> 28.8 us  [local_call(): pl.pallas_call(kernel, name=name, out_shape=out_shape, in_specs=in_specs,...]
  transfers between devices with their start and end apart: 20 -> 18, of which waited for: 16 -> 13; matrix products, arithmetic and copies ran while one was open for 10% -> 12% of each run, Pallas kernels for 5% -> 6%
where the time goes in v6:
time: 322 us; the launch traced here: 321 us
  waiting for transfers between devices  157 us (49%)
  starting transfers between devices  54 us (17%)
  local copies, waits for them, and re-layouts  45.6 us (14%)
  Pallas kernels  28.8 us (9%)
  other arithmetic  20.8 us (6%)
  between operations  14.6 us (5%)
    all_gather x1, waiting for transfers between devices, on_device(): along = lax.all_gather(payload, 'fsdp', axis=0)  76.4 us
    ppermute x12, waiting for transfers between devices, scatter_sum(): mine = mine + hop(k)(theirs.astype(BF16)).astype(F32)  55.1 us
    ppermute x12, starting transfers between devices, scatter_sum(): mine = mine + hop(k)(theirs.astype(BF16)).astype(F32)  41.5 us
    pallas_call x3, Pallas kernels, local_call(): pl.pallas_call(kernel, name=name, out_shape=out_shape, in_specs=in_specs,...  28.8 us
    all_to_all x2, waiting for transfers between devices, pull(): lax.all_to_all(sent, ('dom', 'fsdp'), split_axis=0, concat_axis=0, tiled=...  19.5 us
    all_to_all x2, starting transfers between devices, pull(): lax.all_to_all(sent, ('dom', 'fsdp'), split_axis=0, concat_axis=0, tiled=...  11 us
    gather x2, local copies, waits for them, and re-layouts, picked(): taken = jnp.take(table, chosen.reshape(-1), axis=0)  10.6 us
    add x9, other arithmetic, scatter_sum(): mine = mine + hop(k)(theirs.astype(BF16)).astype(F32)  7.03 us
  transfers between devices with their start and end apart: 18, of which 13 were waited for; matrix products, arithmetic and copies ran while one was open for 12% of the time, Pallas kernels for 6%

profile of v6, /device:TPU:0, one launch (start us, length us, event | category | flops | bytes accessed | tf_op | source)
XLA Modules:
  0.0 320.7 jit_solution(9505875475313748312)
XLA Ops:
  7.2 0.8 copy.63
  8.1 0.7 iota_compare_fusion.2
  8.8 5.2 %gather_fusion = bf16[128,128,128]{2,1,0:T(8,128)(2,1)} fusion(bf16[128,128,128]{2,1,0:T(8,128)(2,1)} %param.15, s32[1024]{0:T(1024)S(1)} %pad_clamp_fusion.1), kind=kCustom, calls=%fused_computation.clone | custom fusion | bytes 8389120 | tf_op jit(solution)/shard_map/jit(_take)/gather | solution.py:215
  14.0 2.6 broadcast_select_fusion.1
  16.7 2.3 broadcast_select_fusion.3
  19.0 7.4 %all-to-all-start = ((bf16[32,4,128,128]{3,2,1,0:T(8,128)(2,1)}), bf16[32,4,128,128]{3,2,1,0:T(8,128)(2,1)}, u32[]{:S(2)}, u32[]{:S(2)}) async-start(bf16[32,4,128,128]{3,2,1,0:T(8,128)(2,1)} %broadcast_select_fusion.3), calls=%async_computation | async-start | bytes 8388608 | tf_op jit(solution)/shard_map/all_to_all | solution.py:220
  26.5 0.9 constant_dynamic-slice_fusion.6
  27.4 0.7 fusion.10
  28.2 76.4 %all-gather.5.cloned.1.call-done = bf16[640,1024]{1,0:T(8,128)(2,1)} async-done(((bf16[80,1024]{1,0:T(8,128)(2,1)}), bf16[640,1024]{1,0:T(8,128)(2,1)}) %all-gather.5.cloned.1.call-update) | async-done | bytes 1310736 | tf_op jit(solution)/shard_map/all_gather | solution.py:234
  104.6 2.3 slice.46
  107.1 5.3 %gather_fusion.1 = bf16[128,128,128]{2,1,0:T(8,128)(2,1)} fusion(bf16[128,128,128]{2,1,0:T(8,128)(2,1)} %param.16, s32[1024]{0:T(1024)S(1)} %pad_clamp_fusion), kind=kCustom, calls=%fused_computation.1.clone | custom fusion | bytes 8389120 | tf_op jit(solution)/shard_map/jit(_take)/gather | solution.py:215
  112.4 2.9 broadcast_select_fusion
  115.3 2.5 broadcast_select_fusion.2
  117.8 19.5 %all-to-all-done = bf16[32,4,128,128]{3,2,1,0:T(8,128)(2,1)} async-done(((bf16[32,4,128,128]{3,2,1,0:T(8,128)(2,1)}), bf16[32,4,128,128]{3,2,1,0:T(8,128)(2,1)}, u32[]{:S(2)}, u32[]{:S(2)}) %all-to-all-start) | async-done | bytes 4194336 | tf_op jit(solution)/shard_map/all_to_all | solution.py:220
  137.3 3.6 %all-to-all-start.1 = ((bf16[32,4,128,128]{3,2,1,0:T(8,128)(2,1)}), bf16[32,4,128,128]{3,2,1,0:T(8,128)(2,1)}, u32[]{:S(2)}, u32[]{:S(2)}) async-start(bf16[32,4,128,128]{3,2,1,0:T(8,128)(2,1)} %broadcast_select_fusion.2), calls=%async_computation.1 | async-start | bytes 8388608 | tf_op jit(solution)/shard_map/all_to_all | solution.py:220
  140.9 0.7 fusion.16
  141.6 0.2 copy.68.bias_ref
  141.8 2.0 all-gather.7.cloned.1.call-done
  143.9 4.2 %fusion.18 = (bf16[1,8,4,32,1024]{4,3,0,1,2:T(8,128)(2,1)}, bf16[1,8,4,32,1024]{4,3,0,1,2:T(8,128)(2,1)S(1)}) fusion(bf16[2,8,4,32,1024]{4,3,0,1,2:T(8,128)(2,1)} %bitcast.89), kind=kLoop, calls=%fused_computation.69 | loop fusion | bytes 8388608 | tf_op jit(solution)/shard_map/slice | solution.py:244
  148.1 1.6 copy.65
  149.6 2.9 copy.66
  152.5 2.0 copy.67
  154.6 4.0 %back_to_hidden.1.back_ref = f32[4,1024,128]{2,1,0:T(8,128)S(1)} custom-call(s32[4,6]{1,0:T(4,128)S(1)} %copy-done.4, s32[4]{0:T(128)S(1)} %copy-done.5, bf16[1024,1024]{1,0:T(8,128)(2,1)S(1)} %bitcast.85, bf16[4,1024,128]{2,1,0:T(8,128)(2,1)S(1)} %copy-done.1, bf16[4,6,128,128]{3,2,1,0:T(8,128)(2,1)S(1)} %copy-done.3), custom_call_target="tpu_custom_call" | custom-call | flops 2147483648 | bytes 7864320 | tf_op jit(solution)/shard_map/back_to_hidden/pallas_call | solution.py:125
  158.6 1.3 copy-done.7
  159.9 14.0 %first_layer.1 = (bf16[4,1024,128]{2,1,0:T(8,128)(2,1)}, f32[1024,1024]{1,0:T(8,128)}, f32[8,1024]{1,0:T(8,128)S(1)}) custom-call(s32[4,6]{1,0:T(4,128)S(1)} %copy-done.4, s32[4]{0:T(128)S(1)} %copy-done.5, bf16[4,1024,128]{2,1,0:T(8,128)(2,1)S(1)} %copy-done, bf16[4,8,4,128,128]{4,3,2,1,0:T(8,128)(2,1)} %bitcast.4.arr_ref, ...), custom_call_target="tpu_custom_call" | custom-call | flops 4294967296 | bytes 20455424 | tf_op jit(solution)/shard_map/first_layer/pallas_call | solution.py:125
  173.9 1.7 fusion
  175.9 0.5 collective-permute-start.1
  176.5 1.9 collective-permute-done.1
  178.4 1.9 bitcast_add_fusion.1
  180.4 0.4 select_maximum_fusion
  180.8 1.5 copy-done.8
  182.4 30.4 %collective-permute-start.2 = (bf16[4,2,40,1024]{3,2,0,1:T(8,128)(2,1)S(1)}, bf16[4,2,40,1024]{3,2,0,1:T(8,128)(2,1)}, u32[]{:S(2)}, u32[]{:S(2)}) collective-permute-start(bf16[4,2,40,1024]{3,2,0,1:T(8,128)(2,1)S(1)} %fusion.2), channel_id=1, source_target_pairs={{0,1},{1,0},{2,3},{3,2},{4,5},{5,4},{6,7},{7,6},{8,9},{9,8},{10,11... | collective-permute-start | bytes 1966088 | tf_op jit(solution)/shard_map/ppermute | solution.py:149
  212.9 24.5 %collective-permute-done.2 = bf16[4,2,40,1024]{3,2,0,1:T(8,128)(2,1)} collective-permute-done((bf16[4,2,40,1024]{3,2,0,1:T(8,128)(2,1)S(1)}, bf16[4,2,40,1024]{3,2,0,1:T(8,128)(2,1)}, u32[]{:S(2)}, u32[]{:S(2)}) %collective-permute-start.2) | collective-permute-done | bytes 655392 | tf_op jit(solution)/shard_map/ppermute | solution.py:149
  237.4 1.7 bitcast_add_fusion.2
  239.1 1.1 copy-done.9
  240.2 1.5 collective-permute-start.3
  241.7 8.3 %collective-permute-done.3 = bf16[4,40,1024]{2,1,0:T(8,128)(2,1)} collective-permute-done((bf16[4,40,1024]{2,1,0:T(8,128)(2,1)S(1)}, bf16[4,40,1024]{2,1,0:T(8,128)(2,1)}, u32[]{:S(2)}, u32[]{:S(2)}) %collective-permute-start.3) | collective-permute-done | bytes 327712 | tf_op jit(solution)/shard_map/ppermute | solution.py:149
  250.0 1.3 bitcast_add_fusion.3
  251.3 10.8 %second_layer.1 = f32[1024,1024]{1,0:T(8,128)} custom-call(s32[4,6]{1,0:T(4,128)S(1)} %copy-done.4, s32[4]{0:T(128)S(1)} %copy-done.5, bf16[4,1024,128]{2,1,0:T(8,128)(2,1)S(1)} %copy-done.6, bf16[4,8,4,128,128]{4,3,2,1,0:T(8,128)(2,1)} %bitcast.14.arr_ref, bf16[4,6,128,128]{3,2,1,0:T(8,128)(2,1)S(1)} %copy-done.3, bf16[4,1024,128]{2,1,0:T(8,128)(2,1)S(1)} %copy-done.2), custom_call_target="tpu_custom_call" | custom-call | flops 3221225472 | bytes 14155776 | tf_op jit(solution)/shard_map/second_layer/pallas_call | solution.py:125
  262.1 1.7 fusion.1
  263.9 2.6 collective-permute-done.4
  266.6 1.9 bitcast_add_fusion
  268.5 0.2 fusion.19
  268.7 1.0 collective-permute-start.7
  269.7 2.4 collective-permute-start.5
  272.1 5.0 %collective-permute-done.7 = bf16[4,2,32,512]{3,2,0,1:T(8,128)(2,1)S(1)} collective-permute-done((bf16[4,2,32,512]{3,2,0,1:T(8,128)(2,1)S(1)}, bf16[4,2,32,512]{3,2,0,1:T(8,128)(2,1)S(1)}, u32[]{:S(2)}, u32[]{:S(2)}) %collective-permute-start.7) | collective-permute-done | bytes 262176 | tf_op jit(solution)/shard_map/ppermute | solution.py:149
  277.3 2.0 collective-permute-start.8
  279.4 1.4 collective-permute-start.6
  280.8 1.5 collective-permute-done.8
  282.3 2.1 collective-permute-done.6
  284.7 1.9 collective-permute-start.9
  286.7 4.7 %collective-permute-done.11 = bf16[72,1024]{1,0:T(8,128)(2,1)S(1)} collective-permute-done((bf16[72,1024]{1,0:T(8,128)(2,1)S(1)}, bf16[72,1024]{1,0:T(8,128)(2,1)S(1)}, u32[]{:S(2)}, u32[]{:S(2)}) %collective-permute-start.11) | collective-permute-done | bytes 147488 | tf_op jit(solution)/shard_map/ppermute | solution.py:149
  291.4 4.4 %collective-permute-done.10 = bf16[72,1024]{1,0:T(8,128)(2,1)S(1)} collective-permute-done((bf16[72,1024]{1,0:T(8,128)(2,1)S(1)}, bf16[72,1024]{1,0:T(8,128)(2,1)S(1)}, u32[]{:S(2)}, u32[]{:S(2)}) %collective-permute-start.10) | collective-permute-done | bytes 147488 | tf_op jit(solution)/shard_map/ppermute | solution.py:149
  295.9 1.3 collective-permute-start.12
  297.2 3.9 %collective-permute-done.12 = bf16[72,1024]{1,0:T(8,128)(2,1)S(1)} collective-permute-done((bf16[72,1024]{1,0:T(8,128)(2,1)S(1)}, bf16[72,1024]{1,0:T(8,128)(2,1)S(1)}, u32[]{:S(2)}, u32[]{:S(2)}) %collective-permute-start.12) | collective-permute-done | bytes 147488 | tf_op jit(solution)/shard_map/ppermute | solution.py:158
  301.2 0.5 copy.75
  301.7 0.3 broadcast_in_dim.54
  302.0 3.9 %dynamic_update_slice.16 = bf16[2,2,72,1024]{3,0,1,2:T(2,128)(2,1)S(1)} dynamic-update-slice(bf16[2,2,72,1024]{3,0,1,2:T(2,128)(2,1)S(1)} %broadcast_in_dim.54, bf16[1,2,72,1024]{3,0,1,2:T(2,128)(2,1)S(1)} %copy.75, s32[]{:T(128)S(6)} %select_n.136, s32[]{:T(128)} %constant.184.clone.1, s32[]{:T(128)} %constant.184.clone.1, s32[]{:T(128)} %constant.184.clone.1) | dynamic-update-slice | bytes 589828 | tf_op jit(solution)/shard_map/jit(dynamic_update_index_in_dim)/dynamic_update_slice | solution.py:155
  305.9 0.5 copy.76
  306.4 3.9 %dynamic_update_slice.17 = bf16[2,2,72,1024]{3,0,1,2:T(2,128)(2,1)S(1)} dynamic-update-slice(bf16[2,2,72,1024]{3,0,1,2:T(2,128)(2,1)S(1)} %dynamic_update_slice.16, bf16[1,2,72,1024]{3,0,1,2:T(2,128)(2,1)S(1)} %copy.76, s32[]{:T(128)S(6)} %select_n.138, s32[]{:T(128)} %constant.184.clone.1, s32[]{:T(128)} %constant.184.clone.1, s32[]{:T(128)} %constant.184.clone.1) | dynamic-update-slice | bytes 589828 | tf_op jit(solution)/shard_map/jit(dynamic_update_index_in_dim)/dynamic_update_slice | solution.py:157
  310.3 0.7 convert_bitcast_fusion
  311.0 1.1 copy.77
  312.1 1.1 copy.78
  313.2 0.6 reshape_squeeze.12
  (67 shorter events, 1.8 us)
Async XLA Ops:
  19.0 8.4 %copy-start.11 = (bf16[128]{0:T(256)(128)(2,1)S(1)}, bf16[128]{0:T(256)(128)(2,1)}, u32[]{:S(2)}) copy-start(bf16[128]{0:T(256)(128)(2,1)} %param.24) | copy-start | bytes 772
  19.0 118.3 %all-to-all-start = ((bf16[32,4,128,128]{3,2,1,0:T(8,128)(2,1)}), bf16[32,4,128,128]{3,2,1,0:T(8,128)(2,1)}, u32[]{:S(2)}, u32[]{:S(2)}) async-start(bf16[32,4,128,128]{3,2,1,0:T(8,128)(2,1)} %broadcast_select_fusion.3), calls=%async_computation | async-start | bytes 8388608 | tf_op jit(solution)/shard_map/all_to_all | solution.py:220
  26.5 80.4 %copy-start.10 = (s32[1,32,4]{1,2,0:T(4,128)S(1)}, s32[1,32,4]{1,2,0:T(4,128)}, u32[]{:S(2)}) copy-start(s32[1,32,4]{1,2,0:T(4,128)} %param.17) | copy-start | bytes 1540
  26.5 78.1 %all-gather.5.cloned.1.call-start = ((), (), s32[]{:S(2)}) async-start(), calls=%async_computation.2 | async-start | bytes 1474560 | tf_op jit(solution)/shard_map/all_gather | solution.py:234
  28.1 115.8 %all-gather.7.cloned.1.call-start = ((), (), s32[]{:S(2)}) async-start(), calls=%async_computation.3 | async-start | bytes 5242880 | tf_op jit(solution)/shard_map/all_gather | solution.py:240
  137.3 114.0 %all-to-all-start.1 = ((bf16[32,4,128,128]{3,2,1,0:T(8,128)(2,1)}), bf16[32,4,128,128]{3,2,1,0:T(8,128)(2,1)}, u32[]{:S(2)}, u32[]{:S(2)}) async-start(bf16[32,4,128,128]{3,2,1,0:T(8,128)(2,1)} %broadcast_select_fusion.2), calls=%async_computation.1 | async-start | bytes 8388608 | tf_op jit(solution)/shard_map/all_to_all | solution.py:220
  152.5 2.0 copy-start.1
  152.5 2.1 copy-start.3
  152.5 2.1 copy-start.4
  152.5 2.1 copy-start.5
  154.6 5.4 %copy-start = (bf16[4,1024,128]{2,1,0:T(8,128)(2,1)S(1)}, bf16[4,1024,128]{2,1,0:T(8,128)(2,1)}, u32[]{:S(2)}) copy-start(bf16[4,1024,128]{2,1,0:T(8,128)(2,1)} %own_ref.1) | copy-start | bytes 3145732
  158.6 1.4 copy-start.7
  175.7 2.8 collective-permute-start
  175.9 2.5 collective-permute-start.1
  180.8 1.5 copy-start.8
  182.4 54.9 %collective-permute-start.2 = (bf16[4,2,40,1024]{3,2,0,1:T(8,128)(2,1)S(1)}, bf16[4,2,40,1024]{3,2,0,1:T(8,128)(2,1)}, u32[]{:S(2)}, u32[]{:S(2)}) collective-permute-start(bf16[4,2,40,1024]{3,2,0,1:T(8,128)(2,1)S(1)} %fusion.2), channel_id=1, source_target_pairs={{0,1},{1,0},{2,3},{3,2},{4,5},{5,4},{6,7},{7,6},{8,9},{9,8},{10,11... | collective-permute-start | bytes 1966088 | tf_op jit(solution)/shard_map/ppermute | solution.py:149
  212.9 38.4 %copy-start.2 = (bf16[4,1024,128]{2,1,0:T(8,128)(2,1)S(1)}, bf16[4,1024,128]{2,1,0:T(8,128)(2,1)}, u32[]{:S(2)}) copy-start(bf16[4,1024,128]{2,1,0:T(8,128)(2,1)} %cot_ref.1) | copy-start | bytes 3145732
  212.9 38.4 %copy-start.6 = (bf16[4,1024,128]{2,1,0:T(8,128)(2,1)S(1)}, bf16[4,1024,128]{2,1,0:T(8,128)(2,1)}, u32[]{:S(2)}) copy-start(bf16[4,1024,128]{2,1,0:T(8,128)(2,1)} %get-tuple-element.23.own_ref) | copy-start | bytes 3145732
  239.1 1.1 copy-start.9
  240.2 9.8 %collective-permute-start.3 = (bf16[4,40,1024]{2,1,0:T(8,128)(2,1)S(1)}, bf16[4,40,1024]{2,1,0:T(8,128)(2,1)}, u32[]{:S(2)}, u32[]{:S(2)}) collective-permute-start(bf16[4,40,1024]{2,1,0:T(8,128)(2,1)S(1)} %fusion.3), channel_id=1, source_target_pairs={{0,16},{8,24},{16,0},{24,8},{1,17},{9,25},{17,1},{25,9},{2,18},{10... | collective-permute-start | bytes 983048 | tf_op jit(solution)/shard_map/ppermute | solution.py:149
  263.8 2.7 collective-permute-start.4
  268.7 8.4 %collective-permute-start.7 = (bf16[4,2,32,512]{3,2,0,1:T(8,128)(2,1)S(1)}, bf16[4,2,32,512]{3,2,0,1:T(8,128)(2,1)S(1)}, u32[]{:S(2)}, u32[]{:S(2)}) collective-permute-start(bf16[4,2,32,512]{3,2,0,1:T(8,128)(2,1)S(1)} %fusion.9), channel_id=1, source_target_pairs={{0,16},{8,24},{16,0},{24,8},{1,17},{9,25},{17,1},{25,9},{2,18},{10... | collective-permute-start | bytes 786440 | tf_op jit(solution)/shard_map/ppermute | solution.py:149
  269.7 9.5 %collective-permute-start.5 = (bf16[4,2,32,512]{3,2,0,1:T(8,128)(2,1)S(1)}, bf16[4,2,32,512]{3,2,0,1:T(8,128)(2,1)S(1)}, u32[]{:S(2)}, u32[]{:S(2)}) collective-permute-start(bf16[4,2,32,512]{3,2,0,1:T(8,128)(2,1)S(1)} %fusion.8), channel_id=1, source_target_pairs={{0,1},{1,0},{2,3},{3,2},{4,5},{5,4},{6,7},{7,6},{8,9},{9,8},{10,11... | collective-permute-start | bytes 786440 | tf_op jit(solution)/shard_map/ppermute | solution.py:149
  277.3 5.0 %collective-permute-start.8 = (bf16[4,32,512]{2,1,0:T(8,128)(2,1)S(1)}, bf16[4,32,512]{2,1,0:T(8,128)(2,1)S(1)}, u32[]{:S(2)}, u32[]{:S(2)}) collective-permute-start(bf16[4,32,512]{2,1,0:T(8,128)(2,1)S(1)} %fusion.15), channel_id=1, source_target_pairs={{0,1},{1,0},{2,3},{3,2},{4,5},{5,4},{6,7},{7,6},{8,9},{9,8},{10,11... | collective-permute-start | bytes 393224 | tf_op jit(solution)/shard_map/ppermute | solution.py:149
  279.4 5.0 %collective-permute-start.6 = (bf16[4,32,512]{2,1,0:T(8,128)(2,1)S(1)}, bf16[4,32,512]{2,1,0:T(8,128)(2,1)S(1)}, u32[]{:S(2)}, u32[]{:S(2)}) collective-permute-start(bf16[4,32,512]{2,1,0:T(8,128)(2,1)S(1)} %fusion.14), channel_id=1, source_target_pairs={{0,16},{8,24},{16,0},{24,8},{1,17},{9,25},{17,1},{25,9},{2,18},{10... | collective-permute-start | bytes 393224 | tf_op jit(solution)/shard_map/ppermute | solution.py:149
  284.6 6.8 %collective-permute-start.11 = (bf16[72,1024]{1,0:T(8,128)(2,1)S(1)}, bf16[72,1024]{1,0:T(8,128)(2,1)S(1)}, u32[]{:S(2)}, u32[]{:S(2)}) collective-permute-start(bf16[72,1024]{1,0:T(8,128)(2,1)S(1)} %get-tuple-element.34), channel_id=1, source_target_pairs={{0,6},{1,7},{2,0},{3,1},{4,2},{5,3},{6,4},{7,5},{8,14},{9,15},{10,... | collective-permute-start | bytes 442376 | tf_op jit(solution)/shard_map/ppermute | solution.py:149
  284.7 11.1 %collective-permute-start.10 = (bf16[72,1024]{1,0:T(8,128)(2,1)S(1)}, bf16[72,1024]{1,0:T(8,128)(2,1)S(1)}, u32[]{:S(2)}, u32[]{:S(2)}) collective-permute-start(bf16[72,1024]{1,0:T(8,128)(2,1)S(1)} %get-tuple-element.35), channel_id=1, source_target_pairs={{0,4},{1,5},{2,6},{3,7},{4,0},{5,1},{6,2},{7,3},{8,12},{9,13},{10,... | collective-permute-start | bytes 442376 | tf_op jit(solution)/shard_map/ppermute | solution.py:149
  284.7 11.1 %collective-permute-start.9 = (bf16[72,1024]{1,0:T(8,128)(2,1)S(1)}, bf16[72,1024]{1,0:T(8,128)(2,1)S(1)}, u32[]{:S(2)}, u32[]{:S(2)}) collective-permute-start(bf16[72,1024]{1,0:T(8,128)(2,1)S(1)} %get-tuple-element.33), channel_id=1, source_target_pairs={{0,2},{1,3},{2,4},{3,5},{4,6},{5,7},{6,0},{7,1},{8,10},{9,11},{10,... | collective-permute-start | bytes 442376 | tf_op jit(solution)/shard_map/ppermute | solution.py:149
  295.9 5.2 %collective-permute-start.12 = (bf16[72,1024]{1,0:T(8,128)(2,1)S(1)}, bf16[72,1024]{1,0:T(8,128)(2,1)S(1)}, u32[]{:S(2)}, u32[]{:S(2)}) collective-permute-start(bf16[72,1024]{1,0:T(8,128)(2,1)S(1)} %get-tuple-element.26), channel_id=1, source_target_pairs={{0,16},{8,24},{16,0},{24,8},{1,17},{9,25},{17,1},{25,9},{2,18},{10... | collective-permute-start | bytes 442376 | tf_op jit(solution)/shard_map/ppermute | solution.py:158
  301.1 4.8 %collective-permute-start.13 = (bf16[2,72,1024]{2,1,0:T(8,128)(2,1)S(1)}, bf16[2,72,1024]{2,1,0:T(8,128)(2,1)S(1)}, u32[]{:S(2)}, u32[]{:S(2)}) collective-permute-start(bf16[2,72,1024]{2,1,0:T(8,128)(2,1)S(1)} %bitcast_dynamic-update-slice_fusion), channel_id=1, source_target_pairs={{0,8},{8,0},{16,24},{24,16},{1,9},{9,1},{17,25},{25,17},{2,10},{10... | collective-permute-start | bytes 884744 | tf_op jit(solution)/shard_map/ppermute | solution.py:158
Sparse Core Ops, SparseCore 0:
  30.1 74.4 all-gather.4
  107.0 36.8 all-gather.6
